TPU v7x, 32 devices: a whole 2x2x4 slice. The times are simulated.
32 devices in a mesh: pipe: 2 (over x), ctx: 16 (over z, y, core).
Axes of the slice: x: 2, y: 2, z: 4, core: 2. Of those that a mesh axis runs over, the one named last changes fastest.
Arguments:
- saved_in: bfloat16 [2, 2048, 2048], P('pipe', 'ctx'), may hold values from -20 to 20, as said below
- grad_in: bfloat16 [2, 2048, 2048], P('pipe', 'ctx'), may hold values from -6 to 6
- queries: bfloat16 [2, 2048, 2048], P('pipe', 'ctx'), may hold values from -60 to 60
- d_heads: bfloat16 [2, 2048, 2048], P('pipe', 'ctx'), may hold values from -6 to 6
- kv_weights: bfloat16 [2, 2048, 512], P('pipe', 'ctx'), may hold values from -0.125 to 0.125
Outputs:
- grad_out: bfloat16 [2, 2048, 2048], P('pipe', 'ctx')
- d_queries: bfloat16 [2, 2048, 2048], P('pipe', 'ctx')
- weight_grad: float32 [2, 2048, 512], P('pipe', 'ctx')
Inputs may be any that keep to these rules, and one draw needn't show every extreme that they name: `saved_in`: stored layer activations.
All inputs are finite; a program needn't handle non-finite values.
Results may differ from a plain program's by a relative error of at most 0.0039.
The roundings to bfloat16 on the way count: a program that leaves them out, or rounds other values in their place, can miss the bound.
Values may be sent and summed in bfloat16 or wider, within the bound.
No kernel may reach another device: no remote copies, remote signals or barrier semaphores. Data moves between devices by JAX's collectives and lax.ppermute only.
A program may use at most 64 MiB of HBM per device.

v0:
```python
import math

import jax
import jax.numpy as jnp
from jax import lax
from jax.sharding import PartitionSpec as P

HEAD_DIM = 128
KV_HEADS = 2


epsilon = 1e-06


def shifted(block, axis, distance):
    devices = range(lax.axis_size(axis))
    route = [((i - distance) % len(devices), i) for i in devices]
    return lax.ppermute(block, axis, route)


def padded(cells, sides, width):
    for axis, dim in sides:
        count = lax.axis_size(axis)
        head = lax.slice_in_dim(cells, 0, width, axis=dim)
        tail = lax.slice_in_dim(cells, cells.shape[dim] - width, cells.shape[dim], axis=dim)
        cells = jnp.concatenate(
            [
                lax.ppermute(tail, axis, [(i, (i + 1) % count) for i in range(count)]),
                cells,
                lax.ppermute(head, axis, [((i + 1) % count, i) for i in range(count)]),
            ],
            axis=dim,
        )
    return cells


def window_mask(row_count):
    query_pos = lax.broadcasted_iota(jnp.int32, (row_count, 3 * row_count), 0)
    key_pos = lax.broadcasted_iota(jnp.int32, (row_count, 3 * row_count), 1)
    offset = key_pos - query_pos
    return (offset >= 0) & (offset <= 2 * row_count)


def per_device(saved_in, grad_in, queries, d_heads, kv_weights):
    upstream = shifted(grad_in, "pipe", -1)[0]
    kv_matrix = lax.all_gather(kv_weights[0], "ctx", axis=0, tiled=True)
    saved = saved_in[0]
    row_count, model_width = saved.shape
    kv_width = kv_matrix.shape[1] // 2
    groups = KV_HEADS
    head_dim = HEAD_DIM
    per_group = model_width // (groups * head_dim)
    score_scale = 1.0 / math.sqrt(head_dim)
    highest = lax.Precision.HIGHEST
    saved_wide = saved.astype(jnp.float32)
    factor = lax.rsqrt(jnp.mean(saved_wide * saved_wide, axis=-1, keepdims=True) + epsilon)
    normed = saved_wide * factor
    normed_b = normed.astype(jnp.bfloat16)
    kv_rows = jnp.dot(normed_b, kv_matrix, preferred_element_type=jnp.float32).astype(jnp.bfloat16)
    wide_kv = padded(kv_rows, (("ctx", 0),), row_count)
    key_rows = wide_kv[:, :kv_width].reshape(3 * row_count, groups, head_dim)
    value_rows = wide_kv[:, kv_width:].reshape(3 * row_count, groups, head_dim)
    own_query = queries[0].reshape(row_count, groups, per_group, head_dim)
    grad_heads = d_heads[0].reshape(row_count, groups, per_group, head_dim)
    valid = window_mask(row_count)[None, None]
    scores = (
        jnp.einsum("qgne,kge->gnqk", own_query, key_rows, preferred_element_type=jnp.float32)
        * score_scale
    )
    scores = jnp.where(valid, scores, -1e30)
    row_peak = jnp.max(scores, axis=-1, keepdims=True)
    lifted = jnp.exp(scores - row_peak)
    row_total = jnp.sum(lifted, axis=-1, keepdims=True)
    probs = lifted / row_total
    probs_b = probs.astype(jnp.bfloat16)
    d_probs = jnp.einsum(
        "qgne,kge->gnqk", grad_heads, value_rows, preferred_element_type=jnp.float32
    )
    row_dot = jnp.sum(probs * d_probs, axis=-1, keepdims=True)
    d_scores = (probs * (d_probs - row_dot) * score_scale).astype(jnp.bfloat16)
    d_queries = (
        jnp.einsum("gnqk,kge->qgne", d_scores, key_rows, preferred_element_type=jnp.float32)
        .astype(jnp.bfloat16)
        .reshape(row_count, model_width)
    )
    d_key_wide = jnp.einsum(
        "gnqk,qgne->kge", d_scores, own_query, preferred_element_type=jnp.float32
    ).reshape(3 * row_count, kv_width)
    d_value_wide = jnp.einsum(
        "gnqk,qgne->kge", probs_b, grad_heads, preferred_element_type=jnp.float32
    ).reshape(3 * row_count, kv_width)
    d_wide = jnp.concatenate([d_key_wide, d_value_wide], axis=1)
    from_upper = shifted(d_wide[:row_count].astype(jnp.bfloat16), "ctx", -1).astype(jnp.float32)
    from_lower = shifted(d_wide[2 * row_count :].astype(jnp.bfloat16), "ctx", 1).astype(jnp.float32)
    d_kv = d_wide[row_count : 2 * row_count] + from_upper + from_lower
    d_normed = jnp.dot(d_kv, kv_matrix.astype(jnp.float32).T, precision=highest)
    upstream_wide = upstream.astype(jnp.float32)
    grad_out = (
        upstream_wide
        + factor * (d_normed - normed * jnp.mean(d_normed * normed, axis=-1, keepdims=True))
    ).astype(jnp.bfloat16)
    terms = jnp.dot(normed_b.astype(jnp.float32).T, d_kv, precision=highest)
    total_tokens = row_count * lax.axis_size("ctx")
    weight_grad = lax.psum_scatter(terms, "ctx", scatter_dimension=0, tiled=True) * (
        1.0 / math.sqrt(total_tokens)
    )
    return (grad_out[None], d_queries[None], weight_grad[None])


def solution(mesh):
    in_specs = (
        P("pipe", "ctx", None),
        P("pipe", "ctx", None),
        P("pipe", "ctx", None),
        P("pipe", "ctx", None),
        P("pipe", "ctx", None),
    )
    out_specs = (P("pipe", "ctx", None), P("pipe", "ctx", None), P("pipe", "ctx", None))
    return jax.shard_map(
        per_device, mesh=mesh, in_specs=in_specs, out_specs=out_specs, check_vma=False
    )
```

profile of v0, /device:TPU:0, one launch (start us, length us, event | category | flops | bytes accessed | tf_op | source)
XLA Modules:
  0.0 169.5 jit_solution(3735802185375871388)
XLA Ops:
  7.2 0.0 all-gather.3.cloned.1.call-start
  7.2 0.7 all-gather.3.cloned.1.call-update
  7.9 0.0 reduce-scatter.2.cloned.1.call-start
  8.0 1.2 fusion.30
  9.2 45.1 %all-gather.3.cloned.1.call-done = bf16[1,2048,512]{2,1,0:T(8,128)(2,1)} async-done(((bf16[1,128,512]{2,1,0:T(8,128)(2,1)}), bf16[1,2048,512]{2,1,0:T(8,128)(2,1)}) %all-gather.3.cloned.1.call-update) | async-done | bytes 2097168 | tf_op jit(solution)/shard_map/all_gather | solution.py:46
  54.3 2.3 %fusion.22 = bf16[128,512]{1,0:T(8,128)(2,1)S(1)} fusion(bf16[1,2048,512]{2,1,0:T(8,128)(2,1)} %all-gather.3.cloned.1.call-done, bf16[1,128,2048]{2,1,0:T(8,128)(2,1)} %param.5, f32[128]{0:T(128)S(1)} %add_rsqrt_fusion), kind=kOutput, calls=%fused_computation.29 | convolution fusion | flops 269287424 | bytes 2753024 | tf_op jit(solution)/shard_map/dot_general | solution.py:59
  56.6 2.0 %collective-permute-start.2 = (bf16[128,512]{1,0:T(8,128)(2,1)S(1)}, bf16[128,512]{1,0:T(8,128)(2,1)S(1)}, u32[]{:S(2)}, u32[]{:S(2)}) collective-permute-start(bf16[128,512]{1,0:T(8,128)(2,1)S(1)} %fusion.22), channel_id=1, source_target_pairs={{1,0},{2,1},{3,2},{4,3},{5,4},{6,5},{7,6},{8,7},{9,8},{10,9},{11,1... | collective-permute-start | bytes 393224 | tf_op jit(solution)/shard_map/ppermute | solution.py:30
  58.6 0.3 copy.33
  58.9 0.3 copy.34
  59.2 1.9 %collective-permute-done.2 = bf16[128,512]{1,0:T(8,128)(2,1)S(1)} collective-permute-done((bf16[128,512]{1,0:T(8,128)(2,1)S(1)}, bf16[128,512]{1,0:T(8,128)(2,1)S(1)}, u32[]{:S(2)}, u32[]{:S(2)}) %collective-permute-start.2) | collective-permute-done | bytes 131104 | tf_op jit(solution)/shard_map/ppermute | solution.py:30
  61.1 4.6 %collective-permute-done.1 = bf16[128,512]{1,0:T(8,128)(2,1)S(1)} collective-permute-done((bf16[128,512]{1,0:T(8,128)(2,1)S(1)}, bf16[128,512]{1,0:T(8,128)(2,1)S(1)}, u32[]{:S(2)}, u32[]{:S(2)}) %collective-permute-start.1) | collective-permute-done | bytes 131104 | tf_op jit(solution)/shard_map/ppermute | solution.py:28
  65.7 0.1 reshape.47
  65.8 0.2 copy.25
  66.0 0.1 reshape.48
  66.0 2.2 %fusion.41 = f32[2,384,128,8]{2,1,3,0:T(8,128)} fusion(bf16[128,2,8,128]{0,3,2,1:T(8,128)(2,1)S(1)} %bitcast.93, bf16[384,2,128,1]{2,1,0,3:T(2,128)(2,1)S(1)} %bitcast.96), kind=kOutput, calls=%fused_computation.48 | convolution fusion | flops 201326592 | bytes 3866624 | tf_op jit(solution)/shard_map/qgne,kge->gnqk/dot_general | solution.py:76
  68.3 2.9 %fusion.56 = (f32[2,8,128]{2,1,0:T(8,128)S(1)}, f32[2,8,128,384]{2,3,1,0:T(8,128)}) fusion(pred[128,384]{0,1:T(8,128)(4,1)S(1)} %fusion.45, bf16[384,2,128,1]{0,2,3,1:T(8,128)(2,1)S(1)} %copy.25, bf16[128,2,8,128]{0,3,2,1:T(8,128)(2,1)S(1)} %bitcast.97), kind=kOutput, calls=%fused_computation.64 | convolution fusion | flops 204472704 | bytes 3923968 | tf_op jit(solution)/shard_map/sub | solution.py:72
  71.1 2.5 %fusion.10 = f32[2,384,128,1]{1,2,3,0:T(8,128)S(1)} fusion(bf16[128,2,8,128]{0,3,2,1:T(8,128)(2,1)S(1)} %bitcast.94, f32[2,8,128,384]{2,3,1,0:T(8,128)} %get-tuple-element.11, f32[2,8,128]{2,1,0:T(8,128)S(1)} %get-tuple-element.10), kind=kOutput, calls=%fused_computation.14 | convolution fusion | flops 202899456 | bytes 4071424 | tf_op jit(solution)/shard_map/gnqk,qgne->kge/dot_general | solution.py:89
  73.7 5.8 %fusion.17 = f32[2,384,128,1]{1,2,3,0:T(8,128)S(1)} fusion(bf16[128,2,8,128]{0,3,2,1:T(8,128)(2,1)S(1)} %bitcast.98, f32[2,384,128,8]{2,1,3,0:T(8,128)} %fusion.41, f32[2,8,128,384]{2,3,1,0:T(8,128)} %get-tuple-element.11, f32[2,8,128]{2,1,0:T(8,128)S(1)} %get-tuple-element.10), kind=kOutput, calls=%fused_computation.22 | convolution fusion | flops 206834048 | bytes 7217152 | tf_op jit(solution)/shard_map/gnqk,qgne->kge/dot_general | solution.py:86
  79.5 0.1 collective-permute-start.3
  79.6 0.5 collective-permute-start.4
  80.1 2.0 %collective-permute-done.3 = bf16[128,512]{0,1:T(8,128)(2,1)S(1)} collective-permute-done((bf16[128,512]{0,1:T(8,128)(2,1)S(1)}, bf16[128,512]{0,1:T(8,128)(2,1)S(1)}, u32[]{:S(2)}, u32[]{:S(2)}) %collective-permute-start.3) | collective-permute-done | bytes 131104 | tf_op jit(solution)/shard_map/ppermute | solution.py:18
  82.1 4.6 %collective-permute-done.4 = bf16[128,512]{0,1:T(8,128)(2,1)S(1)} collective-permute-done((bf16[128,512]{0,1:T(8,128)(2,1)S(1)}, bf16[128,512]{0,1:T(8,128)(2,1)S(1)}, u32[]{:S(2)}, u32[]{:S(2)}) %collective-permute-start.4) | collective-permute-done | bytes 131104 | tf_op jit(solution)/shard_map/ppermute | solution.py:18
  86.7 0.7 copy-done.2
  87.4 3.8 %fusion.38 = f32[2048,512]{1,0:T(8,128)} fusion(bf16[1,128,2048]{2,1,0:T(8,128)(2,1)S(1)} %copy-done, f32[128]{0:T(128)S(1)} %add_rsqrt_fusion, f32[384,256]{0,1:T(8,128)S(1)} %bitcast.91, f32[384,256]{0,1:T(8,128)S(1)} %bitcast.88, bf16[128,512]{0,1:T(8,128)(2,1)S(1)} %collective-permute-done.4, bf16[128,512]{0,1:T(8,128)(2,1)S(1)} %collective-permute-done.3), kind=kOutput, calls=%fused_computation.47 | convolution fusion | flops 1611726848 | bytes 5767680 | tf_op jit(solution)/shard_map/dot_general | solution.py:102
  91.2 0.0 reduce-scatter.2.cloned.1.call-update
  91.2 1.5 collective-permute-start
  92.8 7.2 %fusion.21 = bf16[2,128,8,128]{3,1,2,0:T(8,128)(2,1)} fusion(bf16[384,2,128,1]{0,2,3,1:T(8,128)(2,1)} %copy-done.5, f32[2,384,128,8]{2,1,3,0:T(8,128)} %fusion.41, f32[2,8,128,384]{2,3,1,0:T(8,128)} %get-tuple-element.11, f32[2,8,128]{2,1,0:T(8,128)S(1)} %get-tuple-element.10), kind=kOutput, calls=%fused_computation.28 | convolution fusion | flops 207096192 | bytes 7020544 | tf_op jit(solution)/shard_map/gnqk,kge->qgne/dot_general | solution.py:82
  99.9 2.1 %copy.18 = bf16[1,128,2048]{2,1,0:T(8,128)(2,1)} copy(bf16[1,128,2048]{1,2,0:T(8,128)(2,1)} %bitcast.99) | data formatting | bytes 1048576
  102.0 2.9 %fusion.25 = (f32[128]{0:T(128)S(1)}, f32[128,2048]{1,0:T(8,128)S(1)}) fusion(bf16[1,128,2048]{2,1,0:T(8,128)(2,1)S(1)} %copy-done, f32[128]{0:T(128)S(1)} %add_rsqrt_fusion, bf16[1,2048,512]{2,1,0:T(8,128)(2,1)S(1)} %copy-done.1, f32[384,256]{0,1:T(8,128)S(1)} %bitcast.92, f32[384,256]{0,1:T(8,128)S(1)} %bitcast.89, bf16[128,512]{0,1:T(8,128)(2,1)} %copy-done.2, ...), kind=kOutput, calls=%fused_computation.30 | convolution fusion | flops 1611988864 | bytes 4719616 | tf_op jit(solution)/shard_map/dot_general | solution.py:96
  104.9 2.3 %fusion.32 = bf16[1,128,2048]{2,1,0:T(8,128)(2,1)} fusion(f32[128,2048]{1,0:T(8,128)S(1)} %get-tuple-element.13, bf16[1,128,2048]{2,1,0:T(8,128)(2,1)} %collective-permute-done, bf16[1,128,2048]{2,1,0:T(8,128)(2,1)S(1)} %copy-done, f32[128]{0:T(128)S(1)} %broadcast_multiply_fusion, f32[128]{0:T(128)S(1)} %add_rsqrt_fusion), kind=kLoop, calls=%fused_computation.40 | loop fusion | flops 2097152 | bytes 2622464 | tf_op jit(solution)/shard_map/broadcast_in_dim | solution.py:107
  107.2 53.8 %reduce-scatter.2.cloned.1.call-done = f32[128,512]{1,0:T(8,128)} async-done(((f32[2048,512]{1,0:T(8,128)}), f32[128,512]{1,0:T(8,128)}) %reduce-scatter.2.cloned.1.call-update) | async-done | bytes 262160 | tf_op jit(solution)/shard_map/reduce_scatter | solution.py:104
  161.0 1.7 multiply_bitcast_fusion
  (20 shorter events, 0.2 us)
Async XLA Ops:
  7.2 51.4 %copy-start.3 = (bf16[1,128,2048]{2,1,0:T(8,128)(2,1)S(1)}, bf16[1,128,2048]{2,1,0:T(8,128)(2,1)}, u32[]{:S(2)}) copy-start(bf16[1,128,2048]{2,1,0:T(8,128)(2,1)} %param.7) | copy-start | bytes 1572868
  7.2 51.7 %copy-start.4 = (bf16[1,128,2048]{2,1,0:T(8,128)(2,1)S(1)}, bf16[1,128,2048]{2,1,0:T(8,128)(2,1)}, u32[]{:S(2)}) copy-start(bf16[1,128,2048]{2,1,0:T(8,128)(2,1)} %param.8) | copy-start | bytes 1572868
  7.2 47.1 %all-gather.3.cloned.1.call-start = ((), (), s32[]{:S(2)}) async-start(), calls=%async_computation.2 | async-start | bytes 2228224 | tf_op jit(solution)/shard_map/all_gather | solution.py:46
  7.9 153.0 %reduce-scatter.2.cloned.1.call-start = ((), (), s32[]{:S(2)}) async-start(), calls=%async_computation.1 | async-start | bytes 4456448 | tf_op jit(solution)/shard_map/reduce_scatter | solution.py:104
  56.6 4.5 %collective-permute-start.2 = (bf16[128,512]{1,0:T(8,128)(2,1)S(1)}, bf16[128,512]{1,0:T(8,128)(2,1)S(1)}, u32[]{:S(2)}, u32[]{:S(2)}) collective-permute-start(bf16[128,512]{1,0:T(8,128)(2,1)S(1)} %fusion.22), channel_id=1, source_target_pairs={{1,0},{2,1},{3,2},{4,3},{5,4},{6,5},{7,6},{8,7},{9,8},{10,9},{11,1... | collective-permute-start | bytes 393224 | tf_op jit(solution)/shard_map/ppermute | solution.py:30
  58.6 7.1 %collective-permute-start.1 = (bf16[128,512]{1,0:T(8,128)(2,1)S(1)}, bf16[128,512]{1,0:T(8,128)(2,1)S(1)}, u32[]{:S(2)}, u32[]{:S(2)}) collective-permute-start(bf16[128,512]{1,0:T(8,128)(2,1)S(1)} %fusion.22), channel_id=1, source_target_pairs={{0,1},{1,2},{2,3},{3,4},{4,5},{5,6},{6,7},{7,8},{8,9},{9,10},{10,1... | collective-permute-start | bytes 393224 | tf_op jit(solution)/shard_map/ppermute | solution.py:28
  66.0 5.2 %copy-start.5 = (bf16[384,2,128,1]{0,2,3,1:T(8,128)(2,1)}, bf16[384,2,128,1]{0,2,3,1:T(8,128)(2,1)S(1)}, u32[]{:S(2)}) copy-start(bf16[384,2,128,1]{0,2,3,1:T(8,128)(2,1)S(1)} %copy.25) | copy-start | bytes 589828
  73.6 13.7 %copy-start = (bf16[1,128,2048]{2,1,0:T(8,128)(2,1)S(1)}, bf16[1,128,2048]{2,1,0:T(8,128)(2,1)}, u32[]{:S(2)}) copy-start(bf16[1,128,2048]{2,1,0:T(8,128)(2,1)} %param.5) | copy-start | bytes 1572868
  79.5 2.6 %collective-permute-start.3 = (bf16[128,512]{0,1:T(8,128)(2,1)S(1)}, bf16[128,512]{0,1:T(8,128)(2,1)S(1)}, u32[]{:S(2)}, u32[]{:S(2)}) collective-permute-start(bf16[128,512]{0,1:T(8,128)(2,1)S(1)} %get-tuple-element.6), channel_id=1, source_target_pairs={{1,0},{2,1},{3,2},{4,3},{5,4},{6,5},{7,6},{8,7},{9,8},{10,9},{11,1... | collective-permute-start | bytes 393224 | tf_op jit(solution)/shard_map/ppermute | solution.py:18
  79.6 7.1 %collective-permute-start.4 = (bf16[128,512]{0,1:T(8,128)(2,1)S(1)}, bf16[128,512]{0,1:T(8,128)(2,1)S(1)}, u32[]{:S(2)}, u32[]{:S(2)}) collective-permute-start(bf16[128,512]{0,1:T(8,128)(2,1)S(1)} %get-tuple-element.7), channel_id=1, source_target_pairs={{15,0},{0,1},{1,2},{2,3},{3,4},{4,5},{5,6},{6,7},{7,8},{8,9},{9,10... | collective-permute-start | bytes 393224 | tf_op jit(solution)/shard_map/ppermute | solution.py:18
  86.7 0.7 copy-start.2
  91.2 10.8 %copy-start.1 = (bf16[1,2048,512]{2,1,0:T(8,128)(2,1)S(1)}, bf16[1,2048,512]{2,1,0:T(8,128)(2,1)}, u32[]{:S(2)}) copy-start(bf16[1,2048,512]{2,1,0:T(8,128)(2,1)} %all-gather.3.cloned.1.call-done) | copy-start | bytes 6291460
  91.2 13.7 %collective-permute-start = (bf16[1,128,2048]{2,1,0:T(8,128)(2,1)}, bf16[1,128,2048]{2,1,0:T(8,128)(2,1)}, u32[]{:S(2)}, u32[]{:S(2)}) collective-permute-start(bf16[1,128,2048]{2,1,0:T(8,128)(2,1)} %param.6), channel_id=1, source_target_pairs={{16,0},{0,16},{17,1},{1,17},{18,2},{2,18},{19,3},{3,19},{20,4},{4,... | collective-permute-start | bytes 1572872 | tf_op jit(solution)/shard_map/ppermute | solution.py:18
Sparse Core Ops, SparseCore 0:
  10.2 44.0 all-gather.2
  91.4 69.5 reduce-scatter.1
where the time goes:
time: 170 us; the launch traced here: 169 us
  waiting for transfers between devices  113 us (66%)
  matrix products  29.5 us (17%)
  between operations  14.2 us (8%)
  other arithmetic  5.29 us (3%)
  starting transfers between devices  4.16 us (2%)
  local copies, waits for them, and re-layouts  3.64 us (2%)
    reduce_scatter x1, waiting for transfers between devices, per_device(): lax.psum_scatter(terms, 'ctx', scatter_dimension=0, tiled=True)  53.8 us
    all_gather x1, waiting for transfers between devices, per_device(): kv_matrix = lax.all_gather(kv_weights[0], 'ctx', axis=0, tiled=True)  45.1 us
    dot_general x1, matrix products, per_device(): jnp.einsum('gnqk,kge->qgne', d_scores, key_rows, preferred_element_type=j...  7.16 us
    ppermute x3, waiting for transfers between devices, shifted(): return lax.ppermute(block, axis, route)  6.65 us
    dot_general x1, matrix products, per_device(): jnp.einsum('gnqk,qgne->kge', d_scores, own_query, preferred_element_type=...  5.75 us
    ppermute x1, waiting for transfers between devices, padded(): lax.ppermute(tail, axis, [(i, (i + 1) % count) for i in range(count)])  4.57 us
    broadcast_in_dim x2, other arithmetic, per_device(): return (grad_out[None], d_queries[None], weight_grad[None])  3.94 us
    dot_general x1, matrix products, per_device(): terms = jnp.dot(normed_b.astype(jnp.float32).T, d_kv, precision=highest)  3.84 us
  transfers between devices with their start and end apart: 7, of which 6 were waited for; matrix products, arithmetic and copies ran while one was open for 10% of the time, Pallas kernels for 0%

commit v1 on v0

v1 whole, which is shorter than its diff:
```python
import functools
import math

import jax
import jax.numpy as jnp
from jax import lax
from jax.experimental import pallas as pl
from jax.experimental.pallas import tpu as pltpu
from jax.sharding import PartitionSpec as P

HEAD_DIM = 128
KV_HEADS = 2
EPSILON = 1e-06
NT = (((1,), (1,)), ((), ()))
VMEM = pl.BlockSpec(memory_space=pltpu.VMEM)
SMEM = pl.BlockSpec(memory_space=pltpu.SMEM)
PARAMS = pltpu.CompilerParams(vmem_limit_bytes=48 * 1024 * 1024)


def f32dot(a, b, dims=(((1,), (0,)), ((), ()))):
    return lax.dot_general(a, b, dims, preferred_element_type=jnp.float32)


def call(kernel, outs, args, scratch=()):
    in_specs = [SMEM if a.dtype == jnp.int32 else VMEM for a in args]
    return pl.pallas_call(
        kernel,
        out_shape=[jax.ShapeDtypeStruct(s, d) for s, d in outs],
        in_specs=in_specs,
        out_specs=[VMEM] * len(outs),
        scratch_shapes=list(scratch),
        compiler_params=PARAMS,
    )(*args)


def norm_kernel(me_ref, saved_ref, *refs):
    plain, turned = refs[:4], refs[4:8]
    factor_ref, held, held_t = refs[8:]
    blocks, _, width = held.shape
    rest = me_ref[0] % 4
    wide = saved_ref[...].astype(jnp.float32)
    factor = lax.rsqrt(jnp.mean(wide * wide, axis=-1, keepdims=True) + EPSILON)
    factor_ref[...] = factor
    normed = (wide * factor).astype(jnp.bfloat16)
    for b in range(blocks):
        part = normed[:, b * width : (b + 1) * width]
        held[b] = part
        held_t[b] = part.T
    for d in range(4):
        for zz in range(blocks // 4):
            source = zz * 4 + (rest ^ d)
            plain[d][zz] = held[source]
            turned[d][zz] = held_t[source]


def kv_kernel(me_ref, *refs):
    plain, weights, out_ref = refs[:4], refs[4:-1], refs[-1]
    own = me_ref[0] // 4
    total = None
    for delta, weight in enumerate(weights):
        part = f32dot(plain[delta % 4][own ^ (delta // 4)], weight[...])
        total = part if total is None else total + part
    out_ref[...] = total.astype(jnp.bfloat16)


def attention_kernel(q_ref, g_ref, lower_ref, own_ref, upper_ref, dq_ref, dl_ref, do_ref, du_ref):
    rows, model = q_ref.shape
    dim = HEAD_DIM
    kv_width = KV_HEADS * dim
    per_group = model // kv_width
    scale = 1.0 / math.sqrt(dim)
    key_pos = lax.broadcasted_iota(jnp.int32, (rows, rows), 0)
    query_pos = lax.broadcasted_iota(jnp.int32, (rows, rows), 1)
    first = jnp.concatenate([key_pos >= query_pos] * 2, axis=1)
    last = jnp.concatenate([key_pos <= query_pos] * 2, axis=1)
    for group in range(KV_HEADS):
        at = group * dim
        keys = jnp.concatenate([r[:, at : at + dim] for r in (lower_ref, own_ref, upper_ref)], axis=0)
        at += kv_width
        values = jnp.concatenate([r[:, at : at + dim] for r in (lower_ref, own_ref, upper_ref)], axis=0)
        keys_t = keys.T
        d_keys = d_values = None
        for pair in range(per_group // 2):
            h = (group * per_group + 2 * pair) * dim
            q = jnp.concatenate([q_ref[:, h : h + dim], q_ref[:, h + dim : h + 2 * dim]], axis=0)
            g = jnp.concatenate([g_ref[:, h : h + dim], g_ref[:, h + dim : h + 2 * dim]], axis=0)
            scores = f32dot(keys, q, NT) * scale
            scores = jnp.concatenate(
                [
                    jnp.where(first, scores[:rows], -1e30),
                    scores[rows : 2 * rows],
                    jnp.where(last, scores[2 * rows :], -1e30),
                ],
                axis=0,
            )
            lifted = jnp.exp(scores - jnp.max(scores, axis=0, keepdims=True))
            probs = lifted * (1.0 / jnp.sum(lifted, axis=0, keepdims=True))
            d_probs = f32dot(values, g, NT)
            weighted = probs * d_probs
            row_dot = jnp.sum(weighted, axis=0, keepdims=True)
            d_scores = ((weighted - probs * row_dot) * scale).astype(jnp.bfloat16)
            probs_b = probs.astype(jnp.bfloat16)
            dk = f32dot(d_scores, q)
            dv = f32dot(probs_b, g)
            d_keys = dk if d_keys is None else d_keys + dk
            d_values = dv if d_values is None else d_values + dv
            dq = f32dot(keys_t, d_scores).astype(jnp.bfloat16)
            dq_ref[:, h : h + dim] = dq[:, :rows].T
            dq_ref[:, h + dim : h + 2 * dim] = dq[:, rows:].T
        for at, grad in ((group * dim, d_keys), (kv_width + group * dim, d_values)):
            dl_ref[:, at : at + dim] = grad[:rows].astype(jnp.bfloat16)
            do_ref[:, at : at + dim] = grad[rows : 2 * rows]
            du_ref[:, at : at + dim] = grad[2 * rows :].astype(jnp.bfloat16)


def terms_kernel(me_ref, *refs):
    turned, grads, outs = refs[:4], refs[4:8], refs[8:]
    own = me_ref[0] // 4
    d_kv = jnp.concatenate([r[...] for r in grads], axis=0)
    for delta, out_ref in enumerate(outs):
        lhs = jnp.concatenate([t[own ^ delta] for t in turned], axis=1)
        out_ref[...] = f32dot(lhs, d_kv).astype(out_ref.dtype)


def input_kernel(me_ref, saved_ref, factor_ref, up_ref, do_ref, a_ref, b_ref, *refs):
    weights, out_ref, held = refs[:-2], refs[-2], refs[-1]
    blocks, rows, width = held.shape
    d_kv = do_ref[...] + a_ref[...].astype(jnp.float32) + b_ref[...].astype(jnp.float32)
    high = d_kv.astype(jnp.bfloat16)
    low = (d_kv - high.astype(jnp.float32)).astype(jnp.bfloat16)
    both = jnp.concatenate([high, low], axis=0)
    for delta, weight in enumerate(weights):
        part = f32dot(both, weight[...], NT)
        held[me_ref[0] ^ delta] = part[:rows] + part[rows:]
    factor = factor_ref[...]
    acc = jnp.zeros((rows, width), jnp.float32)
    for b in range(blocks):
        normed = saved_ref[:, b * width : (b + 1) * width].astype(jnp.float32) * factor
        acc = acc + held[b] * normed
    mean = jnp.sum(acc, axis=-1, keepdims=True) * (1.0 / (blocks * width))
    for b in range(blocks):
        at = slice(b * width, (b + 1) * width)
        normed = saved_ref[:, at].astype(jnp.float32) * factor
        grad = up_ref[:, at].astype(jnp.float32) + factor * (held[b] - normed * mean)
        out_ref[:, at] = grad.astype(jnp.bfloat16)


def swap(block, distance):
    count = lax.axis_size("ctx")
    return lax.ppermute(block, "ctx", [(i, i ^ distance) for i in range(count)])


def shifted(block, axis, distance):
    count = lax.axis_size(axis)
    return lax.ppermute(block, axis, [((i - distance) % count, i) for i in range(count)])


def gathered(block):
    count = lax.axis_size("ctx")
    parts = {0: block}
    step = count // 2
    while step >= 4:
        parts.update({d ^ step: swap(p, step) for d, p in list(parts.items())})
        step //= 2
    parts.update({d ^ 2: swap(p, 2) for d, p in list(parts.items())})
    parts.update({d ^ 1: swap(p, 1) for d, p in list(parts.items())})
    return [parts[d] for d in range(count)]


def per_device(saved_in, grad_in, queries, d_heads, kv_weights):
    count = lax.axis_size("ctx")
    me = lax.axis_index("ctx").astype(jnp.int32).reshape(1)
    bf16, f32 = jnp.bfloat16, jnp.float32
    saved = saved_in[0]
    rows, model = saved.shape
    width, kv2 = kv_weights.shape[1:]
    tall = count // 4
    weights = gathered(kv_weights[0])
    upstream = shifted(grad_in, "pipe", -1)[0]
    pieces = call(
        norm_kernel,
        [((tall, rows, width), bf16)] * 4 + [((tall, width, rows), bf16)] * 4 + [((rows, 1), f32)],
        [me, saved],
        [pltpu.VMEM((count, rows, width), bf16), pltpu.VMEM((count, width, rows), bf16)],
    )
    plain, turned, factor = pieces[:4], pieces[4:8], pieces[8]
    turned = [turned[0]] + [swap(turned[d], d) for d in (1, 2, 3)]
    (kv,) = call(kv_kernel, [((rows, kv2), bf16)], [me, *plain, *weights])
    kv_lower = shifted(kv, "ctx", 1)
    kv_upper = shifted(kv, "ctx", -1)
    half = ((rows, kv2), bf16)
    d_queries, d_lower, d_own, d_upper = call(
        attention_kernel,
        [((rows, model), bf16), half, ((rows, kv2), f32), half],
        [queries[0], d_heads[0], kv_lower, kv, kv_upper],
    )
    from_upper = shifted(d_lower, "ctx", -1)
    from_lower = shifted(d_upper, "ctx", 1)
    d_kv = (d_own + from_upper.astype(f32) + from_lower.astype(f32)).astype(bf16)
    beside = swap(d_kv, 1)
    across = swap(d_kv, 2)
    grads = [d_kv, beside, across, swap(across, 1)]
    terms = call(
        terms_kernel,
        [((width, kv2), f32)] + [((width, kv2), bf16)] * (tall - 1),
        [me, *turned, *grads],
    )
    total = terms[0]
    for delta in range(1, tall):
        total = total + swap(terms[delta], 4 * delta).astype(f32)
    weight_grad = total * (1.0 / math.sqrt(rows * count))
    (grad_out,) = call(
        input_kernel,
        [((rows, model), bf16)],
        [me, saved, factor, upstream, d_own, from_upper, from_lower, *weights],
        [pltpu.VMEM((count, rows, width), f32)],
    )
    return (grad_out[None], d_queries[None], weight_grad[None])


def solution(mesh):
    spec = P("pipe", "ctx", None)
    return jax.shard_map(
        per_device, mesh=mesh, in_specs=(spec,) * 5, out_specs=(spec,) * 3, check_vma=False
    )
```

time: 170 us -> 71.7 us (0.42)
  waiting for transfers between devices: 113 us -> 33.4 us
  matrix products: 29.5 us -> 0 us
  starting transfers between devices: 4.16 us -> 25.6 us
  between operations: 14.2 us -> 0.75 us
  Pallas kernels: 0 us -> 8.89 us
  other arithmetic: 5.29 us -> 0.81 us
  local copies, waits for them, and re-layouts: 3.64 us -> 1.47 us
    reduce_scatter x1 -> x0, waiting for transfers between devices: 53.8 us -> none  [per_device(): lax.psum_scatter(terms, 'ctx', scatter_dimension=0, tiled=True)]
    all_gather x1 -> x0, waiting for transfers between devices: 45.1 us -> none  [per_device(): kv_matrix = lax.all_gather(kv_weights[0], 'ctx', axis=0, tiled=True)]
    dot_general x7 -> x0, matrix products: 26.6 us -> none  [the longest x1 7.16 us: per_device(): jnp.einsum('gnqk,kge->qgne', d_scores, key_rows, preferred_element_type=j...]
    ppermute x5 -> x29, starting transfers between devices: 4.09 us -> 25.6 us  [the longest x24 19.5 us: swap(): return lax.ppermute(block, 'ctx', [(i, i ^ distance) for i in range(count)])]
    ppermute x5 -> x29, waiting for transfers between devices: 13.1 us -> 33.4 us  [the longest x24 21.1 us: swap(): return lax.ppermute(block, 'ctx', [(i, i ^ distance) for i in range(count)])]
    pallas_call x0 -> x5, Pallas kernels: none -> 8.89 us  [call(): pl.pallas_call(kernel, out_shape=[jax.ShapeDtypeStruct(s, d) for s, d in...]
    broadcast_in_dim x2 -> x1, other arithmetic: 3.94 us -> 0.77 us  [per_device(): return (grad_out[None], d_queries[None], weight_grad[None])]
    sub x1 -> x0, matrix products: 2.87 us -> none  [per_device(): lifted = jnp.exp(scores - row_peak)]
  transfers between devices with their start and end apart: 7 -> 29, of which waited for: 6 -> 13; matrix products, arithmetic and copies ran while one was open for 10% -> 0% of each run, Pallas kernels for 0% -> 5%
where the time goes in v1:
time: 71.7 us; the launch traced here: 70.9 us
  waiting for transfers between devices  33.4 us (47%)
  starting transfers between devices  25.6 us (36%)
  Pallas kernels  8.89 us (12%)
  local copies, waits for them, and re-layouts  1.47 us (2%)
  other arithmetic  0.81 us (1%)
  between operations  0.75 us (1%)
    ppermute x24, waiting for transfers between devices, swap(): return lax.ppermute(block, 'ctx', [(i, i ^ distance) for i in range(count)])  21.1 us
    ppermute x24, starting transfers between devices, swap(): return lax.ppermute(block, 'ctx', [(i, i ^ distance) for i in range(count)])  19.5 us
    ppermute x5, waiting for transfers between devices, shifted(): lax.ppermute(block, axis, [((i - distance) % count, i) for i in range(cou...  12.3 us
    pallas_call x5, Pallas kernels, call(): pl.pallas_call(kernel, out_shape=[jax.ShapeDtypeStruct(s, d) for s, d in...  8.89 us
    ppermute x5, starting transfers between devices, shifted(): lax.ppermute(block, axis, [((i - distance) % count, i) for i in range(cou...  6.11 us
    unnamed x12, local copies, waits for them, and re-layouts  1.47 us
  transfers between devices with their start and end apart: 29, of which 13 were waited for; matrix products, arithmetic and copies ran while one was open for 0% of the time, Pallas kernels for 5%

profile of v1, /device:TPU:0, one launch (start us, length us, event | category | flops | bytes accessed | tf_op | source)
XLA Modules:
  0.0 70.9 jit_solution(15415744496070148755)
XLA Ops:
  0.6 4.1 %collective-permute-start.8 = (bf16[128,512]{1,0:T(8,128)(2,1)}, bf16[128,512]{1,0:T(8,128)(2,1)S(1)}, u32[]{:S(2)}, u32[]{:S(2)}) collective-permute-start(bf16[128,512]{1,0:T(8,128)(2,1)} %bitcast.13), channel_id=1, source_target_pairs={{0,8},{1,9},{2,10},{3,11},{4,12},{5,13},{6,14},{7,15},{8,0},{9,1},... | collective-permute-start | bytes 393224 | tf_op jit(solution)/shard_map/ppermute | solution.py:150
  4.7 1.6 %collective-permute-start.4 = (bf16[128,512]{1,0:T(8,128)(2,1)}, bf16[128,512]{1,0:T(8,128)(2,1)S(1)}, u32[]{:S(2)}, u32[]{:S(2)}) collective-permute-start(bf16[128,512]{1,0:T(8,128)(2,1)} %bitcast.14), channel_id=1, source_target_pairs={{0,4},{1,5},{2,6},{3,7},{4,0},{5,1},{6,2},{7,3},{8,12},{9,13},{10,... | collective-permute-start | bytes 393224 | tf_op jit(solution)/shard_map/ppermute | solution.py:150
  6.3 1.5 %collective-permute-start.2 = (bf16[128,512]{1,0:T(8,128)(2,1)}, bf16[128,512]{1,0:T(8,128)(2,1)S(1)}, u32[]{:S(2)}, u32[]{:S(2)}) collective-permute-start(bf16[128,512]{1,0:T(8,128)(2,1)} %bitcast.15), channel_id=1, source_target_pairs={{0,2},{1,3},{2,0},{3,1},{4,6},{5,7},{6,4},{7,5},{8,10},{9,11},{10,... | collective-permute-start | bytes 393224 | tf_op jit(solution)/shard_map/ppermute | solution.py:150
  7.8 3.5 %collective-permute-done.8.refs_12_.refs_8_ = bf16[128,512]{1,0:T(8,128)(2,1)S(1)} collective-permute-done((bf16[128,512]{1,0:T(8,128)(2,1)}, bf16[128,512]{1,0:T(8,128)(2,1)S(1)}, u32[]{:S(2)}, u32[]{:S(2)}) %collective-permute-start.8) | collective-permute-done | bytes 131104 | tf_op jit(solution)/shard_map/ppermute | solution.py:150
  11.4 0.7 %collective-permute-start.12 = (bf16[128,512]{1,0:T(8,128)(2,1)S(1)}, bf16[128,512]{1,0:T(8,128)(2,1)S(1)}, u32[]{:S(2)}, u32[]{:S(2)}) collective-permute-start(bf16[128,512]{1,0:T(8,128)(2,1)S(1)} %collective-permute-done.8.refs_12_.refs_8_), channel_id=1, source_target_pairs={{0,4},{1,5},{2,6},{3,7},{4,0},{5,1},{6,2},{7,3},{8,12},{9,13},{10,... | collective-permute-start | bytes 393224 | tf_op jit(solution)/shard_map/ppermute | solution.py:150
  12.1 1.5 %collective-permute-start.10 = (bf16[128,512]{1,0:T(8,128)(2,1)S(1)}, bf16[128,512]{1,0:T(8,128)(2,1)S(1)}, u32[]{:S(2)}, u32[]{:S(2)}) collective-permute-start(bf16[128,512]{1,0:T(8,128)(2,1)S(1)} %collective-permute-done.8.refs_12_.refs_8_), channel_id=1, source_target_pairs={{0,2},{1,3},{2,0},{3,1},{4,6},{5,7},{6,4},{7,5},{8,10},{9,11},{10,... | collective-permute-start | bytes 393224 | tf_op jit(solution)/shard_map/ppermute | solution.py:150
  13.6 0.6 collective-permute-start.6
  14.3 2.0 %collective-permute-done.12.refs_16_.refs_12_ = bf16[128,512]{1,0:T(8,128)(2,1)S(1)} collective-permute-done((bf16[128,512]{1,0:T(8,128)(2,1)S(1)}, bf16[128,512]{1,0:T(8,128)(2,1)S(1)}, u32[]{:S(2)}, u32[]{:S(2)}) %collective-permute-start.12) | collective-permute-done | bytes 131104 | tf_op jit(solution)/shard_map/ppermute | solution.py:150
  16.3 1.6 %collective-permute-start.14 = (bf16[128,512]{1,0:T(8,128)(2,1)S(1)}, bf16[128,512]{1,0:T(8,128)(2,1)S(1)}, u32[]{:S(2)}, u32[]{:S(2)}) collective-permute-start(bf16[128,512]{1,0:T(8,128)(2,1)S(1)} %collective-permute-done.12.refs_16_.refs_12_), channel_id=1, source_target_pairs={{0,2},{1,3},{2,0},{3,1},{4,6},{5,7},{6,4},{7,5},{8,10},{9,11},{10,... | collective-permute-start | bytes 393224 | tf_op jit(solution)/shard_map/ppermute | solution.py:150
  17.9 0.5 collective-permute-start.13
  18.4 2.1 %collective-permute-done.6.refs_10_.refs_6_ = bf16[128,512]{1,0:T(8,128)(2,1)S(1)} collective-permute-done((bf16[128,512]{1,0:T(8,128)(2,1)S(1)}, bf16[128,512]{1,0:T(8,128)(2,1)S(1)}, u32[]{:S(2)}, u32[]{:S(2)}) %collective-permute-start.6) | collective-permute-done | bytes 131104 | tf_op jit(solution)/shard_map/ppermute | solution.py:150
  20.5 0.5 collective-permute-start.7
  21.0 1.8 %collective-permute-done.14.refs_18_.refs_14_ = bf16[128,512]{1,0:T(8,128)(2,1)S(1)} collective-permute-done((bf16[128,512]{1,0:T(8,128)(2,1)S(1)}, bf16[128,512]{1,0:T(8,128)(2,1)S(1)}, u32[]{:S(2)}, u32[]{:S(2)}) %collective-permute-start.14) | collective-permute-done | bytes 131104 | tf_op jit(solution)/shard_map/ppermute | solution.py:150
  22.8 1.0 %copy-done = bf16[1,128,2048]{2,1,0:T(8,128)(2,1)S(1)} copy-done((bf16[1,128,2048]{2,1,0:T(8,128)(2,1)S(1)}, bf16[1,128,2048]{2,1,0:T(8,128)(2,1)}, u32[]{:S(2)}) %copy-start) | copy-done | bytes 524312
  24.8 0.7 shard_map.77.own_ref
  25.5 4.1 %collective-permute-start.17 = (bf16[128,512]{1,0:T(8,128)(2,1)S(1)}, bf16[128,512]{1,0:T(8,128)(2,1)S(1)}, u32[]{:S(2)}, u32[]{:S(2)}) collective-permute-start(bf16[128,512]{1,0:T(8,128)(2,1)S(1)} %shard_map.77.own_ref), channel_id=1, source_target_pairs={{1,0},{2,1},{3,2},{4,3},{5,4},{6,5},{7,6},{8,7},{9,8},{10,9},{11,1... | collective-permute-start | bytes 393224 | tf_op jit(solution)/shard_map/ppermute | solution.py:155
  29.6 2.5 %collective-permute-done.17.upper_ref = bf16[128,512]{1,0:T(8,128)(2,1)S(1)} collective-permute-done((bf16[128,512]{1,0:T(8,128)(2,1)S(1)}, bf16[128,512]{1,0:T(8,128)(2,1)S(1)}, u32[]{:S(2)}, u32[]{:S(2)}) %collective-permute-start.17) | collective-permute-done | bytes 131104 | tf_op jit(solution)/shard_map/ppermute | solution.py:155
  32.1 4.6 %collective-permute-done.16.lower_ref = bf16[128,512]{1,0:T(8,128)(2,1)S(1)} collective-permute-done((bf16[128,512]{1,0:T(8,128)(2,1)S(1)}, bf16[128,512]{1,0:T(8,128)(2,1)S(1)}, u32[]{:S(2)}, u32[]{:S(2)}) %collective-permute-start.16) | collective-permute-done | bytes 131104 | tf_op jit(solution)/shard_map/ppermute | solution.py:155
  36.7 4.9 %shard_map.78 = (bf16[128,2048]{1,0:T(8,128)(2,1)}, bf16[128,512]{1,0:T(8,128)(2,1)S(1)}, f32[128,512]{1,0:T(8,128)S(1)}, bf16[128,512]{1,0:T(8,128)(2,1)S(1)}) custom-call(bf16[128,2048]{1,0:T(8,128)(2,1)S(1)} %bitcast.19, bf16[128,2048]{1,0:T(8,128)(2,1)S(1)} %bitcast.20, bf16[128,512]{1,0:T(8,128)(2,1)S(1)} %collective-permute-done.16.lower_ref, ...), custom_call_target="tpu_custom_call" | custom-call | tf_op jit(solution)/shard_map/pallas_call | solution.py:26
  41.6 0.5 collective-permute-start.19
  42.1 1.5 %collective-permute-start = (bf16[1,128,2048]{2,1,0:T(8,128)(2,1)S(1)}, bf16[1,128,2048]{2,1,0:T(8,128)(2,1)S(1)}, u32[]{:S(2)}, u32[]{:S(2)}) collective-permute-start(bf16[1,128,2048]{2,1,0:T(8,128)(2,1)S(1)} %copy-done.5), channel_id=1, source_target_pairs={{16,0},{0,16},{17,1},{1,17},{18,2},{2,18},{19,3},{3,19},{20,4},{4,... | collective-permute-start | bytes 1572872 | tf_op jit(solution)/shard_map/ppermute | solution.py:155
  43.5 0.5 collective-permute-done.18.a_ref
  44.1 4.7 %collective-permute-done.19.b_ref = bf16[128,512]{1,0:T(8,128)(2,1)S(1)} collective-permute-done((bf16[128,512]{1,0:T(8,128)(2,1)S(1)}, bf16[128,512]{1,0:T(8,128)(2,1)S(1)}, u32[]{:S(2)}, u32[]{:S(2)}) %collective-permute-start.19) | collective-permute-done | bytes 131104 | tf_op jit(solution)/shard_map/ppermute | solution.py:155
  48.9 2.0 %collective-permute-start.21 = (bf16[4,128,128]{2,1,0:T(8,128)(2,1)S(1)}, bf16[4,128,128]{2,1,0:T(8,128)(2,1)S(1)}, u32[]{:S(2)}, u32[]{:S(2)}) collective-permute-start(bf16[4,128,128]{2,1,0:T(8,128)(2,1)S(1)} %get-tuple-element.31), channel_id=1, source_target_pairs={{0,2},{1,3},{2,0},{3,1},{4,6},{5,7},{6,4},{7,5},{8,10},{9,11},{10,... | collective-permute-start | bytes 393224 | tf_op jit(solution)/shard_map/ppermute | solution.py:150
  51.1 2.7 %collective-permute-done.24.refs_6_ = bf16[128,512]{1,0:T(8,128)(2,1)S(1)} collective-permute-done((bf16[128,512]{1,0:T(8,128)(2,1)S(1)}, bf16[128,512]{1,0:T(8,128)(2,1)S(1)}, u32[]{:S(2)}, u32[]{:S(2)}) %collective-permute-start.24) | collective-permute-done | bytes 131104 | tf_op jit(solution)/shard_map/ppermute | solution.py:150
  53.8 2.7 %collective-permute-done.21.refs_2_ = bf16[4,128,128]{2,1,0:T(8,128)(2,1)S(1)} collective-permute-done((bf16[4,128,128]{2,1,0:T(8,128)(2,1)S(1)}, bf16[4,128,128]{2,1,0:T(8,128)(2,1)S(1)}, u32[]{:S(2)}, u32[]{:S(2)}) %collective-permute-start.21) | collective-permute-done | bytes 131104 | tf_op jit(solution)/shard_map/ppermute | solution.py:150
  57.3 2.8 %collective-permute-start.27 = (bf16[128,512]{1,0:T(8,128)(2,1)S(1)}, bf16[128,512]{1,0:T(8,128)(2,1)S(1)}, u32[]{:S(2)}, u32[]{:S(2)}) collective-permute-start(bf16[128,512]{1,0:T(8,128)(2,1)S(1)} %get-tuple-element.35), channel_id=1, source_target_pairs={{0,8},{1,9},{2,10},{3,11},{4,12},{5,13},{6,14},{7,15},{8,0},{9,1},... | collective-permute-start | bytes 393224 | tf_op jit(solution)/shard_map/ppermute | solution.py:150
  60.1 1.6 %collective-permute-start.28 = (bf16[128,512]{1,0:T(8,128)(2,1)S(1)}, bf16[128,512]{1,0:T(8,128)(2,1)S(1)}, u32[]{:S(2)}, u32[]{:S(2)}) collective-permute-start(bf16[128,512]{1,0:T(8,128)(2,1)S(1)} %get-tuple-element.36), channel_id=1, source_target_pairs={{0,12},{1,13},{2,14},{3,15},{4,8},{5,9},{6,10},{7,11},{8,4},{9,5},... | collective-permute-start | bytes 393224 | tf_op jit(solution)/shard_map/ppermute | solution.py:150
  61.7 2.5 %shard_map.79 = bf16[128,2048]{1,0:T(8,128)(2,1)} custom-call(s32[1]{0:T(128)} %bitcast.me_ref, bf16[128,2048]{1,0:T(8,128)(2,1)S(1)} %bitcast.11, f32[128,1]{1,0:T(8,128)S(1)} %get-tuple-element.20.factor_ref, bf16[128,2048]{1,0:T(8,128)(2,1)S(1)} %bitcast.12, f32[128,512]{1,0:T(8,128)S(1)} %get-tuple-element.25.do_ref, ...), custom_call_target="tpu_custom_call" | custom-call | tf_op jit(solution)/shard_map/pallas_call | solution.py:26
  64.2 0.9 %collective-permute-done.26 = bf16[128,512]{1,0:T(8,128)(2,1)S(1)} collective-permute-done((bf16[128,512]{1,0:T(8,128)(2,1)S(1)}, bf16[128,512]{1,0:T(8,128)(2,1)S(1)}, u32[]{:S(2)}, u32[]{:S(2)}) %collective-permute-start.26) | collective-permute-done | bytes 131104 | tf_op jit(solution)/shard_map/ppermute | solution.py:150
  65.0 5.1 %collective-permute-done.27 = bf16[128,512]{1,0:T(8,128)(2,1)S(1)} collective-permute-done((bf16[128,512]{1,0:T(8,128)(2,1)S(1)}, bf16[128,512]{1,0:T(8,128)(2,1)S(1)}, u32[]{:S(2)}, u32[]{:S(2)}) %collective-permute-start.27) | collective-permute-done | bytes 131104 | tf_op jit(solution)/shard_map/ppermute | solution.py:150
  70.2 0.8 %multiply_bitcast_fusion = f32[1,128,512]{2,1,0:T(8,128)} fusion(bf16[128,512]{1,0:T(8,128)(2,1)S(1)} %collective-permute-done.28, bf16[128,512]{1,0:T(8,128)(2,1)S(1)} %collective-permute-done.27, f32[128,512]{1,0:T(8,128)S(1)} %get-tuple-element.33, bf16[128,512]{1,0:T(8,128)(2,1)S(1)} %collective-permute-done.26), kind=kLoop, calls=%fused_computation | loop fusion | flops 458752 | bytes 917504 | tf_op jit(solution)/shard_map/broadcast_in_dim | solution.py:218
  (45 shorter events, 2.1 us)
Async XLA Ops:
  0.6 10.7 %collective-permute-start.8 = (bf16[128,512]{1,0:T(8,128)(2,1)}, bf16[128,512]{1,0:T(8,128)(2,1)S(1)}, u32[]{:S(2)}, u32[]{:S(2)}) collective-permute-start(bf16[128,512]{1,0:T(8,128)(2,1)} %bitcast.13), channel_id=1, source_target_pairs={{0,8},{1,9},{2,10},{3,11},{4,12},{5,13},{6,14},{7,15},{8,0},{9,1},... | collective-permute-start | bytes 393224 | tf_op jit(solution)/shard_map/ppermute | solution.py:150
  4.7 8.9 %collective-permute-start.4 = (bf16[128,512]{1,0:T(8,128)(2,1)}, bf16[128,512]{1,0:T(8,128)(2,1)S(1)}, u32[]{:S(2)}, u32[]{:S(2)}) collective-permute-start(bf16[128,512]{1,0:T(8,128)(2,1)} %bitcast.14), channel_id=1, source_target_pairs={{0,4},{1,5},{2,6},{3,7},{4,0},{5,1},{6,2},{7,3},{8,12},{9,13},{10,... | collective-permute-start | bytes 393224 | tf_op jit(solution)/shard_map/ppermute | solution.py:150
  6.3 7.3 %collective-permute-start.2 = (bf16[128,512]{1,0:T(8,128)(2,1)}, bf16[128,512]{1,0:T(8,128)(2,1)S(1)}, u32[]{:S(2)}, u32[]{:S(2)}) collective-permute-start(bf16[128,512]{1,0:T(8,128)(2,1)} %bitcast.15), channel_id=1, source_target_pairs={{0,2},{1,3},{2,0},{3,1},{4,6},{5,7},{6,4},{7,5},{8,10},{9,11},{10,... | collective-permute-start | bytes 393224 | tf_op jit(solution)/shard_map/ppermute | solution.py:150
  7.8 6.4 %collective-permute-start.1 = (bf16[128,512]{1,0:T(8,128)(2,1)}, bf16[128,512]{1,0:T(8,128)(2,1)S(1)}, u32[]{:S(2)}, u32[]{:S(2)}) collective-permute-start(bf16[128,512]{1,0:T(8,128)(2,1)} %bitcast.16), channel_id=1, source_target_pairs={{0,1},{1,0},{2,3},{3,2},{4,5},{5,4},{6,7},{7,6},{8,9},{9,8},{10,11... | collective-permute-start | bytes 393224 | tf_op jit(solution)/shard_map/ppermute | solution.py:150
  11.4 5.0 %collective-permute-start.12 = (bf16[128,512]{1,0:T(8,128)(2,1)S(1)}, bf16[128,512]{1,0:T(8,128)(2,1)S(1)}, u32[]{:S(2)}, u32[]{:S(2)}) collective-permute-start(bf16[128,512]{1,0:T(8,128)(2,1)S(1)} %collective-permute-done.8.refs_12_.refs_8_), channel_id=1, source_target_pairs={{0,4},{1,5},{2,6},{3,7},{4,0},{5,1},{6,2},{7,3},{8,12},{9,13},{10,... | collective-permute-start | bytes 393224 | tf_op jit(solution)/shard_map/ppermute | solution.py:150
  12.1 5.8 %collective-permute-start.10 = (bf16[128,512]{1,0:T(8,128)(2,1)S(1)}, bf16[128,512]{1,0:T(8,128)(2,1)S(1)}, u32[]{:S(2)}, u32[]{:S(2)}) collective-permute-start(bf16[128,512]{1,0:T(8,128)(2,1)S(1)} %collective-permute-done.8.refs_12_.refs_8_), channel_id=1, source_target_pairs={{0,2},{1,3},{2,0},{3,1},{4,6},{5,7},{6,4},{7,5},{8,10},{9,11},{10,... | collective-permute-start | bytes 393224 | tf_op jit(solution)/shard_map/ppermute | solution.py:150
  13.6 4.3 %collective-permute-start.9 = (bf16[128,512]{1,0:T(8,128)(2,1)S(1)}, bf16[128,512]{1,0:T(8,128)(2,1)S(1)}, u32[]{:S(2)}, u32[]{:S(2)}) collective-permute-start(bf16[128,512]{1,0:T(8,128)(2,1)S(1)} %collective-permute-done.8.refs_12_.refs_8_), channel_id=1, source_target_pairs={{0,1},{1,0},{2,3},{3,2},{4,5},{5,4},{6,7},{7,6},{8,9},{9,8},{10,11... | collective-permute-start | bytes 393224 | tf_op jit(solution)/shard_map/ppermute | solution.py:150
  13.6 6.9 %collective-permute-start.6 = (bf16[128,512]{1,0:T(8,128)(2,1)S(1)}, bf16[128,512]{1,0:T(8,128)(2,1)S(1)}, u32[]{:S(2)}, u32[]{:S(2)}) collective-permute-start(bf16[128,512]{1,0:T(8,128)(2,1)S(1)} %collective-permute-done.4.refs_8_.refs_4_), channel_id=1, source_target_pairs={{0,2},{1,3},{2,0},{3,1},{4,6},{5,7},{6,4},{7,5},{8,10},{9,11},{10,... | collective-permute-start | bytes 393224 | tf_op jit(solution)/shard_map/ppermute | solution.py:150
  14.2 6.3 %collective-permute-start.5 = (bf16[128,512]{1,0:T(8,128)(2,1)S(1)}, bf16[128,512]{1,0:T(8,128)(2,1)S(1)}, u32[]{:S(2)}, u32[]{:S(2)}) collective-permute-start(bf16[128,512]{1,0:T(8,128)(2,1)S(1)} %collective-permute-done.4.refs_8_.refs_4_), channel_id=1, source_target_pairs={{0,1},{1,0},{2,3},{3,2},{4,5},{5,4},{6,7},{7,6},{8,9},{9,8},{10,11... | collective-permute-start | bytes 393224 | tf_op jit(solution)/shard_map/ppermute | solution.py:150
  16.3 6.5 %collective-permute-start.14 = (bf16[128,512]{1,0:T(8,128)(2,1)S(1)}, bf16[128,512]{1,0:T(8,128)(2,1)S(1)}, u32[]{:S(2)}, u32[]{:S(2)}) collective-permute-start(bf16[128,512]{1,0:T(8,128)(2,1)S(1)} %collective-permute-done.12.refs_16_.refs_12_), channel_id=1, source_target_pairs={{0,2},{1,3},{2,0},{3,1},{4,6},{5,7},{6,4},{7,5},{8,10},{9,11},{10,... | collective-permute-start | bytes 393224 | tf_op jit(solution)/shard_map/ppermute | solution.py:150
  17.9 6.4 %collective-permute-start.3 = (bf16[128,512]{1,0:T(8,128)(2,1)S(1)}, bf16[128,512]{1,0:T(8,128)(2,1)S(1)}, u32[]{:S(2)}, u32[]{:S(2)}) collective-permute-start(bf16[128,512]{1,0:T(8,128)(2,1)S(1)} %collective-permute-done.2.refs_6_.refs_2_), channel_id=1, source_target_pairs={{0,1},{1,0},{2,3},{3,2},{4,5},{5,4},{6,7},{7,6},{8,9},{9,8},{10,11... | collective-permute-start | bytes 393224 | tf_op jit(solution)/shard_map/ppermute | solution.py:150
  17.9 6.4 %collective-permute-start.13 = (bf16[128,512]{1,0:T(8,128)(2,1)S(1)}, bf16[128,512]{1,0:T(8,128)(2,1)S(1)}, u32[]{:S(2)}, u32[]{:S(2)}) collective-permute-start(bf16[128,512]{1,0:T(8,128)(2,1)S(1)} %collective-permute-done.12.refs_16_.refs_12_), channel_id=1, source_target_pairs={{0,1},{1,0},{2,3},{3,2},{4,5},{5,4},{6,7},{7,6},{8,9},{9,8},{10,11... | collective-permute-start | bytes 393224 | tf_op jit(solution)/shard_map/ppermute | solution.py:150
  20.5 3.8 %collective-permute-start.11 = (bf16[128,512]{1,0:T(8,128)(2,1)S(1)}, bf16[128,512]{1,0:T(8,128)(2,1)S(1)}, u32[]{:S(2)}, u32[]{:S(2)}) collective-permute-start(bf16[128,512]{1,0:T(8,128)(2,1)S(1)} %collective-permute-done.10.refs_14_.refs_10_), channel_id=1, source_target_pairs={{0,1},{1,0},{2,3},{3,2},{4,5},{5,4},{6,7},{7,6},{8,9},{9,8},{10,11... | collective-permute-start | bytes 393224 | tf_op jit(solution)/shard_map/ppermute | solution.py:150
  20.5 3.8 %collective-permute-start.7 = (bf16[128,512]{1,0:T(8,128)(2,1)S(1)}, bf16[128,512]{1,0:T(8,128)(2,1)S(1)}, u32[]{:S(2)}, u32[]{:S(2)}) collective-permute-start(bf16[128,512]{1,0:T(8,128)(2,1)S(1)} %collective-permute-done.6.refs_10_.refs_6_), channel_id=1, source_target_pairs={{0,1},{1,0},{2,3},{3,2},{4,5},{5,4},{6,7},{7,6},{8,9},{9,8},{10,11... | collective-permute-start | bytes 393224 | tf_op jit(solution)/shard_map/ppermute | solution.py:150
  22.8 1.5 %collective-permute-start.15 = (bf16[128,512]{1,0:T(8,128)(2,1)S(1)}, bf16[128,512]{1,0:T(8,128)(2,1)S(1)}, u32[]{:S(2)}, u32[]{:S(2)}) collective-permute-start(bf16[128,512]{1,0:T(8,128)(2,1)S(1)} %collective-permute-done.14.refs_18_.refs_14_), channel_id=1, source_target_pairs={{0,1},{1,0},{2,3},{3,2},{4,5},{5,4},{6,7},{7,6},{8,9},{9,8},{10,11... | collective-permute-start | bytes 393224 | tf_op jit(solution)/shard_map/ppermute | solution.py:150
  24.8 11.9 %copy-start.3 = (bf16[1,128,2048]{2,1,0:T(8,128)(2,1)S(1)}, bf16[1,128,2048]{2,1,0:T(8,128)(2,1)}, u32[]{:S(2)}) copy-start(bf16[1,128,2048]{2,1,0:T(8,128)(2,1)} %param.7) | copy-start | bytes 1572868
  24.8 11.9 %copy-start.4 = (bf16[1,128,2048]{2,1,0:T(8,128)(2,1)S(1)}, bf16[1,128,2048]{2,1,0:T(8,128)(2,1)}, u32[]{:S(2)}) copy-start(bf16[1,128,2048]{2,1,0:T(8,128)(2,1)} %param.8) | copy-start | bytes 1572868
  25.5 6.6 %collective-permute-start.17 = (bf16[128,512]{1,0:T(8,128)(2,1)S(1)}, bf16[128,512]{1,0:T(8,128)(2,1)S(1)}, u32[]{:S(2)}, u32[]{:S(2)}) collective-permute-start(bf16[128,512]{1,0:T(8,128)(2,1)S(1)} %shard_map.77.own_ref), channel_id=1, source_target_pairs={{1,0},{2,1},{3,2},{4,3},{5,4},{6,5},{7,6},{8,7},{9,8},{10,9},{11,1... | collective-permute-start | bytes 393224 | tf_op jit(solution)/shard_map/ppermute | solution.py:155
  29.6 7.1 %collective-permute-start.16 = (bf16[128,512]{1,0:T(8,128)(2,1)S(1)}, bf16[128,512]{1,0:T(8,128)(2,1)S(1)}, u32[]{:S(2)}, u32[]{:S(2)}) collective-permute-start(bf16[128,512]{1,0:T(8,128)(2,1)S(1)} %shard_map.77.own_ref), channel_id=1, source_target_pairs={{15,0},{0,1},{1,2},{2,3},{3,4},{4,5},{5,6},{6,7},{7,8},{8,9},{9,10... | collective-permute-start | bytes 393224 | tf_op jit(solution)/shard_map/ppermute | solution.py:155
  36.7 5.4 %copy-start.5 = (bf16[1,128,2048]{2,1,0:T(8,128)(2,1)S(1)}, bf16[1,128,2048]{2,1,0:T(8,128)(2,1)}, u32[]{:S(2)}) copy-start(bf16[1,128,2048]{2,1,0:T(8,128)(2,1)} %param.6) | copy-start | bytes 1572868
  41.5 2.5 %collective-permute-start.18 = (bf16[128,512]{1,0:T(8,128)(2,1)S(1)}, bf16[128,512]{1,0:T(8,128)(2,1)S(1)}, u32[]{:S(2)}, u32[]{:S(2)}) collective-permute-start(bf16[128,512]{1,0:T(8,128)(2,1)S(1)} %get-tuple-element.26), channel_id=1, source_target_pairs={{1,0},{2,1},{3,2},{4,3},{5,4},{6,5},{7,6},{8,7},{9,8},{10,9},{11,1... | collective-permute-start | bytes 393224 | tf_op jit(solution)/shard_map/ppermute | solution.py:155
  41.6 7.2 %collective-permute-start.19 = (bf16[128,512]{1,0:T(8,128)(2,1)S(1)}, bf16[128,512]{1,0:T(8,128)(2,1)S(1)}, u32[]{:S(2)}, u32[]{:S(2)}) collective-permute-start(bf16[128,512]{1,0:T(8,128)(2,1)S(1)} %get-tuple-element.27), channel_id=1, source_target_pairs={{15,0},{0,1},{1,2},{2,3},{3,4},{4,5},{5,6},{6,7},{7,8},{8,9},{9,10... | collective-permute-start | bytes 393224 | tf_op jit(solution)/shard_map/ppermute | solution.py:155
  42.1 19.6 %collective-permute-start = (bf16[1,128,2048]{2,1,0:T(8,128)(2,1)S(1)}, bf16[1,128,2048]{2,1,0:T(8,128)(2,1)S(1)}, u32[]{:S(2)}, u32[]{:S(2)}) collective-permute-start(bf16[1,128,2048]{2,1,0:T(8,128)(2,1)S(1)} %copy-done.5), channel_id=1, source_target_pairs={{16,0},{0,16},{17,1},{1,17},{18,2},{2,18},{19,3},{3,19},{20,4},{4,... | collective-permute-start | bytes 1572872 | tf_op jit(solution)/shard_map/ppermute | solution.py:155
  43.5 7.4 %collective-permute-start.20 = (bf16[4,128,128]{2,1,0:T(8,128)(2,1)S(1)}, bf16[4,128,128]{2,1,0:T(8,128)(2,1)S(1)}, u32[]{:S(2)}, u32[]{:S(2)}) collective-permute-start(bf16[4,128,128]{2,1,0:T(8,128)(2,1)S(1)} %get-tuple-element.30), channel_id=1, source_target_pairs={{0,1},{1,0},{2,3},{3,2},{4,5},{5,4},{6,7},{7,6},{8,9},{9,8},{10,11... | collective-permute-start | bytes 393224 | tf_op jit(solution)/shard_map/ppermute | solution.py:150
  48.8 5.0 %collective-permute-start.24 = (bf16[128,512]{1,0:T(8,128)(2,1)S(1)}, bf16[128,512]{1,0:T(8,128)(2,1)S(1)}, u32[]{:S(2)}, u32[]{:S(2)}) collective-permute-start(bf16[128,512]{1,0:T(8,128)(2,1)S(1)} %add_convert_fusion.refs_4_), channel_id=1, source_target_pairs={{0,2},{1,3},{2,0},{3,1},{4,6},{5,7},{6,4},{7,5},{8,10},{9,11},{10,... | collective-permute-start | bytes 393224 | tf_op jit(solution)/shard_map/ppermute | solution.py:150
  48.9 7.7 %collective-permute-start.21 = (bf16[4,128,128]{2,1,0:T(8,128)(2,1)S(1)}, bf16[4,128,128]{2,1,0:T(8,128)(2,1)S(1)}, u32[]{:S(2)}, u32[]{:S(2)}) collective-permute-start(bf16[4,128,128]{2,1,0:T(8,128)(2,1)S(1)} %get-tuple-element.31), channel_id=1, source_target_pairs={{0,2},{1,3},{2,0},{3,1},{4,6},{5,7},{6,4},{7,5},{8,10},{9,11},{10,... | collective-permute-start | bytes 393224 | tf_op jit(solution)/shard_map/ppermute | solution.py:150
  50.9 5.9 %collective-permute-start.22 = (bf16[4,128,128]{2,1,0:T(8,128)(2,1)S(1)}, bf16[4,128,128]{2,1,0:T(8,128)(2,1)S(1)}, u32[]{:S(2)}, u32[]{:S(2)}) collective-permute-start(bf16[4,128,128]{2,1,0:T(8,128)(2,1)S(1)} %get-tuple-element.32), channel_id=1, source_target_pairs={{0,3},{1,2},{2,1},{3,0},{4,7},{5,6},{6,5},{7,4},{8,11},{9,10},{10,... | collective-permute-start | bytes 393224 | tf_op jit(solution)/shard_map/ppermute | solution.py:150
  50.9 5.9 %collective-permute-start.23 = (bf16[128,512]{1,0:T(8,128)(2,1)S(1)}, bf16[128,512]{1,0:T(8,128)(2,1)S(1)}, u32[]{:S(2)}, u32[]{:S(2)}) collective-permute-start(bf16[128,512]{1,0:T(8,128)(2,1)S(1)} %add_convert_fusion.refs_4_), channel_id=1, source_target_pairs={{0,1},{1,0},{2,3},{3,2},{4,5},{5,4},{6,7},{7,6},{8,9},{9,8},{10,11... | collective-permute-start | bytes 393224 | tf_op jit(solution)/shard_map/ppermute | solution.py:150
  53.8 2.9 %collective-permute-start.25 = (bf16[128,512]{1,0:T(8,128)(2,1)S(1)}, bf16[128,512]{1,0:T(8,128)(2,1)S(1)}, u32[]{:S(2)}, u32[]{:S(2)}) collective-permute-start(bf16[128,512]{1,0:T(8,128)(2,1)S(1)} %collective-permute-done.24.refs_6_), channel_id=1, source_target_pairs={{0,1},{1,0},{2,3},{3,2},{4,5},{5,4},{6,7},{7,6},{8,9},{9,8},{10,11... | collective-permute-start | bytes 393224 | tf_op jit(solution)/shard_map/ppermute | solution.py:150
  57.2 7.8 %collective-permute-start.26 = (bf16[128,512]{1,0:T(8,128)(2,1)S(1)}, bf16[128,512]{1,0:T(8,128)(2,1)S(1)}, u32[]{:S(2)}, u32[]{:S(2)}) collective-permute-start(bf16[128,512]{1,0:T(8,128)(2,1)S(1)} %get-tuple-element.34), channel_id=1, source_target_pairs={{0,4},{1,5},{2,6},{3,7},{4,0},{5,1},{6,2},{7,3},{8,12},{9,13},{10,... | collective-permute-start | bytes 393224 | tf_op jit(solution)/shard_map/ppermute | solution.py:150
  57.3 12.8 %collective-permute-start.27 = (bf16[128,512]{1,0:T(8,128)(2,1)S(1)}, bf16[128,512]{1,0:T(8,128)(2,1)S(1)}, u32[]{:S(2)}, u32[]{:S(2)}) collective-permute-start(bf16[128,512]{1,0:T(8,128)(2,1)S(1)} %get-tuple-element.35), channel_id=1, source_target_pairs={{0,8},{1,9},{2,10},{3,11},{4,12},{5,13},{6,14},{7,15},{8,0},{9,1},... | collective-permute-start | bytes 393224 | tf_op jit(solution)/shard_map/ppermute | solution.py:150
  60.1 10.0 %collective-permute-start.28 = (bf16[128,512]{1,0:T(8,128)(2,1)S(1)}, bf16[128,512]{1,0:T(8,128)(2,1)S(1)}, u32[]{:S(2)}, u32[]{:S(2)}) collective-permute-start(bf16[128,512]{1,0:T(8,128)(2,1)S(1)} %get-tuple-element.36), channel_id=1, source_target_pairs={{0,12},{1,13},{2,14},{3,15},{4,8},{5,9},{6,10},{7,11},{8,4},{9,5},... | collective-permute-start | bytes 393224 | tf_op jit(solution)/shard_map/ppermute | solution.py:150
  (3 other events, 6.9 us)

commit v2 on v1

--- a/solution.py
+++ b/solution.py
@@ -63,7 +63,7 @@
     out_ref[...] = total.astype(jnp.bfloat16)
 
 
-def attention_kernel(q_ref, g_ref, lower_ref, own_ref, upper_ref, dq_ref, dl_ref, do_ref, du_ref):
+def attention_kernel(me_ref, q_ref, g_ref, own_ref, beside_ref, across_ref, dq_ref, db_ref, do_ref, da_ref):
     rows, model = q_ref.shape
     dim = HEAD_DIM
     kv_width = KV_HEADS * dim
@@ -71,13 +71,15 @@
     scale = 1.0 / math.sqrt(dim)
     key_pos = lax.broadcasted_iota(jnp.int32, (rows, rows), 0)
     query_pos = lax.broadcasted_iota(jnp.int32, (rows, rows), 1)
-    first = jnp.concatenate([key_pos >= query_pos] * 2, axis=1)
-    last = jnp.concatenate([key_pos <= query_pos] * 2, axis=1)
+    offset = (key_pos - query_pos) * (1 - 2 * (me_ref[0] % 2))
+    beside_mask = jnp.concatenate([offset <= 0] * 2, axis=1)
+    across_mask = jnp.concatenate([offset >= 0] * 2, axis=1)
+    parts = (beside_ref, own_ref, across_ref)
     for group in range(KV_HEADS):
         at = group * dim
-        keys = jnp.concatenate([r[:, at : at + dim] for r in (lower_ref, own_ref, upper_ref)], axis=0)
+        keys = jnp.concatenate([r[:, at : at + dim] for r in parts], axis=0)
         at += kv_width
-        values = jnp.concatenate([r[:, at : at + dim] for r in (lower_ref, own_ref, upper_ref)], axis=0)
+        values = jnp.concatenate([r[:, at : at + dim] for r in parts], axis=0)
         keys_t = keys.T
         d_keys = d_values = None
         for pair in range(per_group // 2):
@@ -87,9 +89,9 @@
             scores = f32dot(keys, q, NT) * scale
             scores = jnp.concatenate(
                 [
-                    jnp.where(first, scores[:rows], -1e30),
+                    jnp.where(beside_mask, scores[:rows], -1e30),
                     scores[rows : 2 * rows],
-                    jnp.where(last, scores[2 * rows :], -1e30),
+                    jnp.where(across_mask, scores[2 * rows :], -1e30),
                 ],
                 axis=0,
             )
@@ -108,9 +110,9 @@
             dq_ref[:, h : h + dim] = dq[:, :rows].T
             dq_ref[:, h + dim : h + 2 * dim] = dq[:, rows:].T
         for at, grad in ((group * dim, d_keys), (kv_width + group * dim, d_values)):
-            dl_ref[:, at : at + dim] = grad[:rows].astype(jnp.bfloat16)
+            db_ref[:, at : at + dim] = grad[:rows].astype(jnp.bfloat16)
             do_ref[:, at : at + dim] = grad[rows : 2 * rows]
-            du_ref[:, at : at + dim] = grad[2 * rows :].astype(jnp.bfloat16)
+            da_ref[:, at : at + dim] = grad[2 * rows :].astype(jnp.bfloat16)
 
 
 def terms_kernel(me_ref, *refs):
@@ -155,16 +157,30 @@
     return lax.ppermute(block, axis, [((i - distance) % count, i) for i in range(count)])
 
 
-def gathered(block):
-    count = lax.axis_size("ctx")
-    parts = {0: block}
-    step = count // 2
+def crossed(block):
+    count = lax.axis_size("ctx")
+    route = [(i, (i + 1) % count if i % 2 else (i - 1) % count) for i in range(count)]
+    return lax.ppermute(block, "ctx", route)
+
+
+def gathered(block, meanwhile):
+    count = lax.axis_size("ctx")
+    first = count // 2
+    parts = {0: block, first: swap(block, first)}
+    parts[2] = swap(block, 2)
+    far = [0, first]
+    step = first // 2
     while step >= 4:
-        parts.update({d ^ step: swap(p, step) for d, p in list(parts.items())})
+        for d in list(far):
+            parts[d ^ step] = swap(parts[d], step)
+            far.append(d ^ step)
         step //= 2
-    parts.update({d ^ 2: swap(p, 2) for d, p in list(parts.items())})
+    parts[first], meanwhile = lax.optimization_barrier((parts[first], meanwhile))
+    for d in far[1:]:
+        direct = d & (first | 4) == first | 4 and first > 4
+        parts[d ^ 2] = swap(parts[d ^ 4], 6) if direct else swap(parts[d], 2)
     parts.update({d ^ 1: swap(p, 1) for d, p in list(parts.items())})
-    return [parts[d] for d in range(count)]
+    return [parts[d] for d in range(count)], meanwhile
 
 
 def per_device(saved_in, grad_in, queries, d_heads, kv_weights):
@@ -175,44 +191,45 @@
     rows, model = saved.shape
     width, kv2 = kv_weights.shape[1:]
     tall = count // 4
-    weights = gathered(kv_weights[0])
-    upstream = shifted(grad_in, "pipe", -1)[0]
     pieces = call(
         norm_kernel,
         [((tall, rows, width), bf16)] * 4 + [((tall, width, rows), bf16)] * 4 + [((rows, 1), f32)],
         [me, saved],
         [pltpu.VMEM((count, rows, width), bf16), pltpu.VMEM((count, width, rows), bf16)],
     )
+    weights, pieces = gathered(kv_weights[0], pieces)
+    weights[8], grad_in = lax.optimization_barrier((weights[8], grad_in))
+    upstream = shifted(grad_in, "pipe", -1)[0]
     plain, turned, factor = pieces[:4], pieces[4:8], pieces[8]
     turned = [turned[0]] + [swap(turned[d], d) for d in (1, 2, 3)]
-    (kv,) = call(kv_kernel, [((rows, kv2), bf16)], [me, *plain, *weights])
-    kv_lower = shifted(kv, "ctx", 1)
-    kv_upper = shifted(kv, "ctx", -1)
     half = ((rows, kv2), bf16)
-    d_queries, d_lower, d_own, d_upper = call(
+    (kv,) = call(kv_kernel, [half], [me, *plain, *weights])
+    across = crossed(kv)
+    beside = swap(kv, 1)
+    d_queries, d_beside, d_own, d_across = call(
         attention_kernel,
         [((rows, model), bf16), half, ((rows, kv2), f32), half],
-        [queries[0], d_heads[0], kv_lower, kv, kv_upper],
-    )
-    from_upper = shifted(d_lower, "ctx", -1)
-    from_lower = shifted(d_upper, "ctx", 1)
-    d_kv = (d_own + from_upper.astype(f32) + from_lower.astype(f32)).astype(bf16)
-    beside = swap(d_kv, 1)
-    across = swap(d_kv, 2)
-    grads = [d_kv, beside, across, swap(across, 1)]
+        [me, queries[0], d_heads[0], kv, beside, across],
+    )
+    d_across, turned, upstream = lax.optimization_barrier((d_across, turned, upstream))
+    from_across = crossed(d_across)
+    from_beside = swap(d_beside, 1)
+    d_kv = (d_own + from_beside.astype(f32) + from_across.astype(f32)).astype(bf16)
+    above = swap(d_kv, 2)
+    grads = [d_kv, swap(d_kv, 1), above, swap(above, 1)]
     terms = call(
         terms_kernel,
         [((width, kv2), f32)] + [((width, kv2), bf16)] * (tall - 1),
         [me, *turned, *grads],
     )
     total = terms[0]
-    for delta in range(1, tall):
+    for delta in reversed(range(1, tall)):
         total = total + swap(terms[delta], 4 * delta).astype(f32)
     weight_grad = total * (1.0 / math.sqrt(rows * count))
     (grad_out,) = call(
         input_kernel,
         [((rows, model), bf16)],
-        [me, saved, factor, upstream, d_own, from_upper, from_lower, *weights],
+        [me, saved, factor, upstream, d_own, from_beside, from_across, *weights],
         [pltpu.VMEM((count, rows, width), f32)],
     )
     return (grad_out[None], d_queries[None], weight_grad[None])

time: 71.7 us -> 65.8 us (0.918)
  waiting for transfers between devices: 33.4 us -> 24.5 us
  starting transfers between devices: 25.6 us -> 29.6 us
    ppermute x5 -> x1, waiting for transfers between devices: 12.3 us -> 0.01 us  [shifted(): lax.ppermute(block, axis, [((i - distance) % count, i) for i in range(cou...]
    ppermute x0 -> x2, starting transfers between devices: none -> 8.28 us  [crossed(): return lax.ppermute(block, 'ctx', route)]
    ppermute x0 -> x2, waiting for transfers between devices: none -> 5.54 us  [crossed(): return lax.ppermute(block, 'ctx', route)]
    ppermute x5 -> x1, starting transfers between devices: 6.11 us -> 1.56 us  [shifted(): lax.ppermute(block, axis, [((i - distance) % count, i) for i in range(cou...]
    ppermute x24 -> x26, waiting for transfers between devices: 21.1 us -> 19 us  [swap(): return lax.ppermute(block, 'ctx', [(i, i ^ distance) for i in range(count)])]
    unnamed x12 -> x10, local copies, waits for them, and re-layouts: 1.47 us -> 1.06 us
    ppermute x24 -> x26, starting transfers between devices: 19.5 us -> 19.7 us  [swap(): return lax.ppermute(block, 'ctx', [(i, i ^ distance) for i in range(count)])]
  transfers between devices with their start and end apart: 29 -> 29, of which waited for: 13 -> 13; matrix products, arithmetic and copies ran while one was open for 0% -> 0% of each run, Pallas kernels for 5% -> 13%
where the time goes in v2:
time: 65.8 us; the launch traced here: 65.6 us
  starting transfers between devices  29.6 us (45%)
  waiting for transfers between devices  24.5 us (37%)
  Pallas kernels  8.93 us (14%)
  local copies, waits for them, and re-layouts  1.06 us (2%)
  other arithmetic  0.81 us (1%)
  between operations  0.73 us (1%)
    ppermute x26, starting transfers between devices, swap(): return lax.ppermute(block, 'ctx', [(i, i ^ distance) for i in range(count)])  19.7 us
    ppermute x26, waiting for transfers between devices, swap(): return lax.ppermute(block, 'ctx', [(i, i ^ distance) for i in range(count)])  19 us
    pallas_call x5, Pallas kernels, call(): pl.pallas_call(kernel, out_shape=[jax.ShapeDtypeStruct(s, d) for s, d in...  8.93 us
    ppermute x2, starting transfers between devices, crossed(): return lax.ppermute(block, 'ctx', route)  8.28 us
    ppermute x2, waiting for transfers between devices, crossed(): return lax.ppermute(block, 'ctx', route)  5.54 us
    ppermute x1, starting transfers between devices, shifted(): lax.ppermute(block, axis, [((i - distance) % count, i) for i in range(cou...  1.56 us
  transfers between devices with their start and end apart: 29, of which 13 were waited for; matrix products, arithmetic and copies ran while one was open for 0% of the time, Pallas kernels for 13%

profile of v2, /device:TPU:0, one launch (start us, length us, event | category | flops | bytes accessed | tf_op | source)
XLA Modules:
  0.0 65.6 jit_solution(5597557544588397808)
XLA Ops:
  0.6 3.1 %collective-permute-start.4 = (bf16[128,512]{1,0:T(8,128)(2,1)}, bf16[128,512]{1,0:T(8,128)(2,1)S(1)}, u32[]{:S(2)}, u32[]{:S(2)}) collective-permute-start(bf16[128,512]{1,0:T(8,128)(2,1)} %bitcast.13), channel_id=1, source_target_pairs={{0,4},{1,5},{2,6},{3,7},{4,0},{5,1},{6,2},{7,3},{8,12},{9,13},{10,... | collective-permute-start | bytes 393224 | tf_op jit(solution)/shard_map/ppermute | solution.py:152
  3.7 1.5 %collective-permute-start.2 = (bf16[128,512]{1,0:T(8,128)(2,1)}, bf16[128,512]{1,0:T(8,128)(2,1)S(1)}, u32[]{:S(2)}, u32[]{:S(2)}) collective-permute-start(bf16[128,512]{1,0:T(8,128)(2,1)} %bitcast.14), channel_id=1, source_target_pairs={{0,2},{1,3},{2,0},{3,1},{4,6},{5,7},{6,4},{7,5},{8,10},{9,11},{10,... | collective-permute-start | bytes 393224 | tf_op jit(solution)/shard_map/ppermute | solution.py:152
  5.2 2.6 %collective-permute-start = (bf16[128,512]{1,0:T(8,128)(2,1)}, bf16[128,512]{1,0:T(8,128)(2,1)S(1)}, u32[]{:S(2)}, u32[]{:S(2)}) collective-permute-start(bf16[128,512]{1,0:T(8,128)(2,1)} %bitcast.15), channel_id=1, source_target_pairs={{0,8},{1,9},{2,10},{3,11},{4,12},{5,13},{6,14},{7,15},{8,0},{9,1},... | collective-permute-start | bytes 393224 | tf_op jit(solution)/shard_map/ppermute | solution.py:152
  7.8 2.8 %collective-permute-start.6 = (bf16[128,512]{1,0:T(8,128)(2,1)S(1)}, bf16[128,512]{1,0:T(8,128)(2,1)S(1)}, u32[]{:S(2)}, u32[]{:S(2)}) collective-permute-start(bf16[128,512]{1,0:T(8,128)(2,1)S(1)} %collective-permute-done.4.refs_8_.refs_4_), channel_id=1, source_target_pairs={{0,2},{1,3},{2,0},{3,1},{4,6},{5,7},{6,4},{7,5},{8,10},{9,11},{10,... | collective-permute-start | bytes 393224 | tf_op jit(solution)/shard_map/ppermute | solution.py:152
  10.6 0.5 collective-permute-start.3
  11.1 1.0 %copy-done = bf16[1,128,2048]{2,1,0:T(8,128)(2,1)S(1)} copy-done((bf16[1,128,2048]{2,1,0:T(8,128)(2,1)S(1)}, bf16[1,128,2048]{2,1,0:T(8,128)(2,1)}, u32[]{:S(2)}) %copy-start) | copy-done | bytes 524312
  12.6 1.3 %collective-permute-done.refs_12_.refs_8_ = bf16[128,512]{1,0:T(8,128)(2,1)S(1)} collective-permute-done((bf16[128,512]{1,0:T(8,128)(2,1)}, bf16[128,512]{1,0:T(8,128)(2,1)S(1)}, u32[]{:S(2)}, u32[]{:S(2)}) %collective-permute-start) | collective-permute-done | bytes 131104 | tf_op jit(solution)/shard_map/ppermute | solution.py:152
  13.9 2.0 %collective-permute-start.13 = (bf16[128,512]{1,0:T(8,128)(2,1)S(1)}, bf16[128,512]{1,0:T(8,128)(2,1)S(1)}, u32[]{:S(2)}, u32[]{:S(2)}) collective-permute-start(bf16[128,512]{1,0:T(8,128)(2,1)S(1)} %collective-permute-done.refs_12_.refs_8_), channel_id=1, source_target_pairs={{0,6},{1,7},{2,4},{3,5},{4,2},{5,3},{6,0},{7,1},{8,14},{9,15},{10,... | collective-permute-start | bytes 393224 | tf_op jit(solution)/shard_map/ppermute | solution.py:152
  15.9 1.5 %collective-permute-start.9 = (bf16[128,512]{1,0:T(8,128)(2,1)S(1)}, bf16[128,512]{1,0:T(8,128)(2,1)S(1)}, u32[]{:S(2)}, u32[]{:S(2)}) collective-permute-start(bf16[128,512]{1,0:T(8,128)(2,1)S(1)} %collective-permute-done.refs_12_.refs_8_), channel_id=1, source_target_pairs={{0,2},{1,3},{2,0},{3,1},{4,6},{5,7},{6,4},{7,5},{8,10},{9,11},{10,... | collective-permute-start | bytes 393224 | tf_op jit(solution)/shard_map/ppermute | solution.py:152
  17.4 1.6 %collective-permute-start.20 = (bf16[1,128,2048]{2,1,0:T(8,128)(2,1)}, bf16[1,128,2048]{2,1,0:T(8,128)(2,1)S(1)}, u32[]{:S(2)}, u32[]{:S(2)}) collective-permute-start(bf16[1,128,2048]{2,1,0:T(8,128)(2,1)} %param.6), channel_id=1, source_target_pairs={{16,0},{0,16},{17,1},{1,17},{18,2},{2,18},{19,3},{3,19},{20,4},{4,... | collective-permute-start | bytes 1572872 | tf_op jit(solution)/shard_map/ppermute | solution.py:157
  18.9 0.8 %collective-permute-done.11.refs_16_.refs_12_ = bf16[128,512]{1,0:T(8,128)(2,1)S(1)} collective-permute-done((bf16[128,512]{1,0:T(8,128)(2,1)S(1)}, bf16[128,512]{1,0:T(8,128)(2,1)S(1)}, u32[]{:S(2)}, u32[]{:S(2)}) %collective-permute-start.11) | collective-permute-done | bytes 131104 | tf_op jit(solution)/shard_map/ppermute | solution.py:152
  19.8 1.1 %collective-permute-done.13.refs_18_.refs_14_ = bf16[128,512]{1,0:T(8,128)(2,1)S(1)} collective-permute-done((bf16[128,512]{1,0:T(8,128)(2,1)S(1)}, bf16[128,512]{1,0:T(8,128)(2,1)S(1)}, u32[]{:S(2)}, u32[]{:S(2)}) %collective-permute-start.13) | collective-permute-done | bytes 131104 | tf_op jit(solution)/shard_map/ppermute | solution.py:152
  20.8 1.3 %collective-permute-done.9.refs_14_.refs_10_ = bf16[128,512]{1,0:T(8,128)(2,1)S(1)} collective-permute-done((bf16[128,512]{1,0:T(8,128)(2,1)S(1)}, bf16[128,512]{1,0:T(8,128)(2,1)S(1)}, u32[]{:S(2)}, u32[]{:S(2)}) %collective-permute-start.9) | collective-permute-done | bytes 131104 | tf_op jit(solution)/shard_map/ppermute | solution.py:152
  22.1 0.5 collective-permute-start.10
  22.7 0.8 %collective-permute-done.14.refs_19_.refs_15_ = bf16[128,512]{1,0:T(8,128)(2,1)S(1)} collective-permute-done((bf16[128,512]{1,0:T(8,128)(2,1)S(1)}, bf16[128,512]{1,0:T(8,128)(2,1)S(1)}, u32[]{:S(2)}, u32[]{:S(2)}) %collective-permute-start.14) | collective-permute-done | bytes 131104 | tf_op jit(solution)/shard_map/ppermute | solution.py:152
  23.7 0.7 %shard_map.77.own_ref = bf16[128,512]{1,0:T(8,128)(2,1)S(1)} custom-call(s32[1]{0:T(128)} %bitcast.me_ref, bf16[4,128,128]{2,1,0:T(8,128)(2,1)S(1)} %get-tuple-element.48.refs_0_, bf16[4,128,128]{2,1,0:T(8,128)(2,1)S(1)} %get-tuple-element.49.refs_1_, bf16[4,128,128]{2,1,0:T(8,128)(2,1)S(1)} %get-tuple-element.50.refs_2_, ...), custom_call_target="tpu_custom_call" | custom-call | tf_op jit(solution)/shard_map/pallas_call | solution.py:26
  24.4 4.6 %collective-permute-start.16 = (bf16[128,512]{1,0:T(8,128)(2,1)S(1)}, bf16[128,512]{1,0:T(8,128)(2,1)S(1)}, u32[]{:S(2)}, u32[]{:S(2)}) collective-permute-start(bf16[128,512]{1,0:T(8,128)(2,1)S(1)} %shard_map.77.own_ref), channel_id=1, source_target_pairs={{0,15},{1,2},{2,1},{3,4},{4,3},{5,6},{6,5},{7,8},{8,7},{9,10},{10,... | collective-permute-start | bytes 393224 | tf_op jit(solution)/shard_map/ppermute | solution.py:163
  29.0 0.5 collective-permute-start.17
  29.5 2.1 %collective-permute-done.16.across_ref = bf16[128,512]{1,0:T(8,128)(2,1)S(1)} collective-permute-done((bf16[128,512]{1,0:T(8,128)(2,1)S(1)}, bf16[128,512]{1,0:T(8,128)(2,1)S(1)}, u32[]{:S(2)}, u32[]{:S(2)}) %collective-permute-start.16) | collective-permute-done | bytes 131104 | tf_op jit(solution)/shard_map/ppermute | solution.py:163
  31.6 4.9 %shard_map.78 = (bf16[128,2048]{1,0:T(8,128)(2,1)}, bf16[128,512]{1,0:T(8,128)(2,1)S(1)}, f32[128,512]{1,0:T(8,128)S(1)}, bf16[128,512]{1,0:T(8,128)(2,1)S(1)}) custom-call(s32[1]{0:T(128)} %bitcast.me_ref, bf16[128,2048]{1,0:T(8,128)(2,1)S(1)} %bitcast.19, bf16[128,2048]{1,0:T(8,128)(2,1)S(1)} %bitcast.20, bf16[128,512]{1,0:T(8,128)(2,1)S(1)} %shard_map.77.own_ref, ...), custom_call_target="tpu_custom_call" | custom-call | tf_op jit(solution)/shard_map/pallas_call | solution.py:26
  36.5 0.9 %collective-permute-done.19.refs_3_ = bf16[4,128,128]{2,1,0:T(8,128)(2,1)S(1)} collective-permute-done((bf16[4,128,128]{2,1,0:T(8,128)(2,1)S(1)}, bf16[4,128,128]{2,1,0:T(8,128)(2,1)S(1)}, u32[]{:S(2)}, u32[]{:S(2)}) %collective-permute-start.19) | collective-permute-done | bytes 131104 | tf_op jit(solution)/shard_map/ppermute | solution.py:152
  37.5 3.7 %collective-permute-start.22 = (bf16[128,512]{1,0:T(8,128)(2,1)S(1)}, bf16[128,512]{1,0:T(8,128)(2,1)S(1)}, u32[]{:S(2)}, u32[]{:S(2)}) collective-permute-start(bf16[128,512]{1,0:T(8,128)(2,1)S(1)} %get-tuple-element.63), channel_id=1, source_target_pairs={{0,15},{1,2},{2,1},{3,4},{4,3},{5,6},{6,5},{7,8},{8,7},{9,10},{10,... | collective-permute-start | bytes 393224 | tf_op jit(solution)/shard_map/ppermute | solution.py:163
  41.2 3.4 %collective-permute-done.22.b_ref = bf16[128,512]{1,0:T(8,128)(2,1)S(1)} collective-permute-done((bf16[128,512]{1,0:T(8,128)(2,1)S(1)}, bf16[128,512]{1,0:T(8,128)(2,1)S(1)}, u32[]{:S(2)}, u32[]{:S(2)}) %collective-permute-start.22) | collective-permute-done | bytes 131104 | tf_op jit(solution)/shard_map/ppermute | solution.py:163
  44.8 4.9 %collective-permute-done.24.refs_6_ = bf16[128,512]{1,0:T(8,128)(2,1)S(1)} collective-permute-done((bf16[128,512]{1,0:T(8,128)(2,1)S(1)}, bf16[128,512]{1,0:T(8,128)(2,1)S(1)}, u32[]{:S(2)}, u32[]{:S(2)}) %collective-permute-start.24) | collective-permute-done | bytes 131104 | tf_op jit(solution)/shard_map/ppermute | solution.py:152
  49.7 1.3 %collective-permute-done.25.refs_7_ = bf16[128,512]{1,0:T(8,128)(2,1)S(1)} collective-permute-done((bf16[128,512]{1,0:T(8,128)(2,1)S(1)}, bf16[128,512]{1,0:T(8,128)(2,1)S(1)}, u32[]{:S(2)}, u32[]{:S(2)}) %collective-permute-start.25) | collective-permute-done | bytes 131104 | tf_op jit(solution)/shard_map/ppermute | solution.py:152
  51.0 0.5 shard_map.80
  51.5 3.9 %collective-permute-start.26 = (bf16[128,512]{1,0:T(8,128)(2,1)S(1)}, bf16[128,512]{1,0:T(8,128)(2,1)S(1)}, u32[]{:S(2)}, u32[]{:S(2)}) collective-permute-start(bf16[128,512]{1,0:T(8,128)(2,1)S(1)} %get-tuple-element.70), channel_id=1, source_target_pairs={{0,12},{1,13},{2,14},{3,15},{4,8},{5,9},{6,10},{7,11},{8,4},{9,5},... | collective-permute-start | bytes 393224 | tf_op jit(solution)/shard_map/ppermute | solution.py:152
  55.4 0.6 collective-permute-start.28
  56.1 2.5 %shard_map.79 = bf16[128,2048]{1,0:T(8,128)(2,1)} custom-call(s32[1]{0:T(128)} %bitcast.me_ref, bf16[128,2048]{1,0:T(8,128)(2,1)S(1)} %bitcast.11, f32[128,1]{1,0:T(8,128)S(1)} %get-tuple-element.47.factor_ref, bf16[128,2048]{1,0:T(8,128)(2,1)S(1)} %bitcast.12, f32[128,512]{1,0:T(8,128)S(1)} %get-tuple-element.61.do_ref, ...), custom_call_target="tpu_custom_call" | custom-call | tf_op jit(solution)/shard_map/pallas_call | solution.py:26
  58.5 1.3 %collective-permute-done.26 = bf16[128,512]{1,0:T(8,128)(2,1)S(1)} collective-permute-done((bf16[128,512]{1,0:T(8,128)(2,1)S(1)}, bf16[128,512]{1,0:T(8,128)(2,1)S(1)}, u32[]{:S(2)}, u32[]{:S(2)}) %collective-permute-start.26) | collective-permute-done | bytes 131104 | tf_op jit(solution)/shard_map/ppermute | solution.py:152
  59.8 5.0 %collective-permute-done.27 = bf16[128,512]{1,0:T(8,128)(2,1)S(1)} collective-permute-done((bf16[128,512]{1,0:T(8,128)(2,1)S(1)}, bf16[128,512]{1,0:T(8,128)(2,1)S(1)}, u32[]{:S(2)}, u32[]{:S(2)}) %collective-permute-start.27) | collective-permute-done | bytes 131104 | tf_op jit(solution)/shard_map/ppermute | solution.py:152
  64.9 0.8 %multiply_bitcast_fusion = f32[1,128,512]{2,1,0:T(8,128)} fusion(bf16[128,512]{1,0:T(8,128)(2,1)S(1)} %collective-permute-done.28, bf16[128,512]{1,0:T(8,128)(2,1)S(1)} %collective-permute-done.27, f32[128,512]{1,0:T(8,128)S(1)} %get-tuple-element.69, bf16[128,512]{1,0:T(8,128)(2,1)S(1)} %collective-permute-done.26), kind=kLoop, calls=%fused_computation | loop fusion | flops 458752 | bytes 917504 | tf_op jit(solution)/shard_map/broadcast_in_dim | solution.py:235
  (43 shorter events, 0.9 us)
Async XLA Ops:
  0.6 7.2 %collective-permute-start.4 = (bf16[128,512]{1,0:T(8,128)(2,1)}, bf16[128,512]{1,0:T(8,128)(2,1)S(1)}, u32[]{:S(2)}, u32[]{:S(2)}) collective-permute-start(bf16[128,512]{1,0:T(8,128)(2,1)} %bitcast.13), channel_id=1, source_target_pairs={{0,4},{1,5},{2,6},{3,7},{4,0},{5,1},{6,2},{7,3},{8,12},{9,13},{10,... | collective-permute-start | bytes 393224 | tf_op jit(solution)/shard_map/ppermute | solution.py:152
  3.7 6.9 %collective-permute-start.2 = (bf16[128,512]{1,0:T(8,128)(2,1)}, bf16[128,512]{1,0:T(8,128)(2,1)S(1)}, u32[]{:S(2)}, u32[]{:S(2)}) collective-permute-start(bf16[128,512]{1,0:T(8,128)(2,1)} %bitcast.14), channel_id=1, source_target_pairs={{0,2},{1,3},{2,0},{3,1},{4,6},{5,7},{6,4},{7,5},{8,10},{9,11},{10,... | collective-permute-start | bytes 393224 | tf_op jit(solution)/shard_map/ppermute | solution.py:152
  5.2 8.6 %collective-permute-start = (bf16[128,512]{1,0:T(8,128)(2,1)}, bf16[128,512]{1,0:T(8,128)(2,1)S(1)}, u32[]{:S(2)}, u32[]{:S(2)}) collective-permute-start(bf16[128,512]{1,0:T(8,128)(2,1)} %bitcast.15), channel_id=1, source_target_pairs={{0,8},{1,9},{2,10},{3,11},{4,12},{5,13},{6,14},{7,15},{8,0},{9,1},... | collective-permute-start | bytes 393224 | tf_op jit(solution)/shard_map/ppermute | solution.py:152
  7.8 6.0 %collective-permute-start.1 = (bf16[128,512]{1,0:T(8,128)(2,1)}, bf16[128,512]{1,0:T(8,128)(2,1)S(1)}, u32[]{:S(2)}, u32[]{:S(2)}) collective-permute-start(bf16[128,512]{1,0:T(8,128)(2,1)} %bitcast.16), channel_id=1, source_target_pairs={{0,1},{1,0},{2,3},{3,2},{4,5},{5,4},{6,7},{7,6},{8,9},{9,8},{10,11... | collective-permute-start | bytes 393224 | tf_op jit(solution)/shard_map/ppermute | solution.py:152
  7.8 8.1 %collective-permute-start.6 = (bf16[128,512]{1,0:T(8,128)(2,1)S(1)}, bf16[128,512]{1,0:T(8,128)(2,1)S(1)}, u32[]{:S(2)}, u32[]{:S(2)}) collective-permute-start(bf16[128,512]{1,0:T(8,128)(2,1)S(1)} %collective-permute-done.4.refs_8_.refs_4_), channel_id=1, source_target_pairs={{0,2},{1,3},{2,0},{3,1},{4,6},{5,7},{6,4},{7,5},{8,10},{9,11},{10,... | collective-permute-start | bytes 393224 | tf_op jit(solution)/shard_map/ppermute | solution.py:152
  10.6 6.8 %collective-permute-start.5 = (bf16[128,512]{1,0:T(8,128)(2,1)S(1)}, bf16[128,512]{1,0:T(8,128)(2,1)S(1)}, u32[]{:S(2)}, u32[]{:S(2)}) collective-permute-start(bf16[128,512]{1,0:T(8,128)(2,1)S(1)} %collective-permute-done.4.refs_8_.refs_4_), channel_id=1, source_target_pairs={{0,1},{1,0},{2,3},{3,2},{4,5},{5,4},{6,7},{7,6},{8,9},{9,8},{10,11... | collective-permute-start | bytes 393224 | tf_op jit(solution)/shard_map/ppermute | solution.py:152
  10.6 6.8 %collective-permute-start.3 = (bf16[128,512]{1,0:T(8,128)(2,1)S(1)}, bf16[128,512]{1,0:T(8,128)(2,1)S(1)}, u32[]{:S(2)}, u32[]{:S(2)}) collective-permute-start(bf16[128,512]{1,0:T(8,128)(2,1)S(1)} %collective-permute-done.2.refs_6_.refs_2_), channel_id=1, source_target_pairs={{0,1},{1,0},{2,3},{3,2},{4,5},{5,4},{6,7},{7,6},{8,9},{9,8},{10,11... | collective-permute-start | bytes 393224 | tf_op jit(solution)/shard_map/ppermute | solution.py:152
  12.2 11.5 %copy-start.2 = (bf16[1,128,512]{2,1,0:T(8,128)(2,1)S(1)}, bf16[1,128,512]{2,1,0:T(8,128)(2,1)}, u32[]{:S(2)}) copy-start(bf16[1,128,512]{2,1,0:T(8,128)(2,1)} %param.9) | copy-start | bytes 393220
  13.9 17.8 %copy-start.3 = (bf16[1,128,2048]{2,1,0:T(8,128)(2,1)S(1)}, bf16[1,128,2048]{2,1,0:T(8,128)(2,1)}, u32[]{:S(2)}) copy-start(bf16[1,128,2048]{2,1,0:T(8,128)(2,1)} %param.7) | copy-start | bytes 1572868
  13.9 17.8 %copy-start.4 = (bf16[1,128,2048]{2,1,0:T(8,128)(2,1)S(1)}, bf16[1,128,2048]{2,1,0:T(8,128)(2,1)}, u32[]{:S(2)}) copy-start(bf16[1,128,2048]{2,1,0:T(8,128)(2,1)} %param.8) | copy-start | bytes 1572868
  13.9 5.9 %collective-permute-start.11 = (bf16[128,512]{1,0:T(8,128)(2,1)S(1)}, bf16[128,512]{1,0:T(8,128)(2,1)S(1)}, u32[]{:S(2)}, u32[]{:S(2)}) collective-permute-start(bf16[128,512]{1,0:T(8,128)(2,1)S(1)} %collective-permute-done.refs_12_.refs_8_), channel_id=1, source_target_pairs={{0,4},{1,5},{2,6},{3,7},{4,0},{5,1},{6,2},{7,3},{8,12},{9,13},{10,... | collective-permute-start | bytes 393224 | tf_op jit(solution)/shard_map/ppermute | solution.py:152
  13.9 7.0 %collective-permute-start.13 = (bf16[128,512]{1,0:T(8,128)(2,1)S(1)}, bf16[128,512]{1,0:T(8,128)(2,1)S(1)}, u32[]{:S(2)}, u32[]{:S(2)}) collective-permute-start(bf16[128,512]{1,0:T(8,128)(2,1)S(1)} %collective-permute-done.refs_12_.refs_8_), channel_id=1, source_target_pairs={{0,6},{1,7},{2,4},{3,5},{4,2},{5,3},{6,0},{7,1},{8,14},{9,15},{10,... | collective-permute-start | bytes 393224 | tf_op jit(solution)/shard_map/ppermute | solution.py:152
  15.9 6.2 %collective-permute-start.9 = (bf16[128,512]{1,0:T(8,128)(2,1)S(1)}, bf16[128,512]{1,0:T(8,128)(2,1)S(1)}, u32[]{:S(2)}, u32[]{:S(2)}) collective-permute-start(bf16[128,512]{1,0:T(8,128)(2,1)S(1)} %collective-permute-done.refs_12_.refs_8_), channel_id=1, source_target_pairs={{0,2},{1,3},{2,0},{3,1},{4,6},{5,7},{6,4},{7,5},{8,10},{9,11},{10,... | collective-permute-start | bytes 393224 | tf_op jit(solution)/shard_map/ppermute | solution.py:152
  17.4 4.8 %collective-permute-start.8 = (bf16[128,512]{1,0:T(8,128)(2,1)S(1)}, bf16[128,512]{1,0:T(8,128)(2,1)S(1)}, u32[]{:S(2)}, u32[]{:S(2)}) collective-permute-start(bf16[128,512]{1,0:T(8,128)(2,1)S(1)} %collective-permute-done.refs_12_.refs_8_), channel_id=1, source_target_pairs={{0,1},{1,0},{2,3},{3,2},{4,5},{5,4},{6,7},{7,6},{8,9},{9,8},{10,11... | collective-permute-start | bytes 393224 | tf_op jit(solution)/shard_map/ppermute | solution.py:152
  17.4 20.1 %collective-permute-start.20 = (bf16[1,128,2048]{2,1,0:T(8,128)(2,1)}, bf16[1,128,2048]{2,1,0:T(8,128)(2,1)S(1)}, u32[]{:S(2)}, u32[]{:S(2)}) collective-permute-start(bf16[1,128,2048]{2,1,0:T(8,128)(2,1)} %param.6), channel_id=1, source_target_pairs={{16,0},{0,16},{17,1},{1,17},{18,2},{2,18},{19,3},{3,19},{20,4},{4,... | collective-permute-start | bytes 1572872 | tf_op jit(solution)/shard_map/ppermute | solution.py:157
  19.8 2.9 %collective-permute-start.7 = (bf16[128,512]{1,0:T(8,128)(2,1)S(1)}, bf16[128,512]{1,0:T(8,128)(2,1)S(1)}, u32[]{:S(2)}, u32[]{:S(2)}) collective-permute-start(bf16[128,512]{1,0:T(8,128)(2,1)S(1)} %collective-permute-done.6.refs_10_.refs_6_), channel_id=1, source_target_pairs={{0,1},{1,0},{2,3},{3,2},{4,5},{5,4},{6,7},{7,6},{8,9},{9,8},{10,11... | collective-permute-start | bytes 393224 | tf_op jit(solution)/shard_map/ppermute | solution.py:152
  20.8 1.8 %collective-permute-start.12 = (bf16[128,512]{1,0:T(8,128)(2,1)S(1)}, bf16[128,512]{1,0:T(8,128)(2,1)S(1)}, u32[]{:S(2)}, u32[]{:S(2)}) collective-permute-start(bf16[128,512]{1,0:T(8,128)(2,1)S(1)} %collective-permute-done.11.refs_16_.refs_12_), channel_id=1, source_target_pairs={{0,1},{1,0},{2,3},{3,2},{4,5},{5,4},{6,7},{7,6},{8,9},{9,8},{10,11... | collective-permute-start | bytes 393224 | tf_op jit(solution)/shard_map/ppermute | solution.py:152
  22.1 1.3 %collective-permute-start.14 = (bf16[128,512]{1,0:T(8,128)(2,1)S(1)}, bf16[128,512]{1,0:T(8,128)(2,1)S(1)}, u32[]{:S(2)}, u32[]{:S(2)}) collective-permute-start(bf16[128,512]{1,0:T(8,128)(2,1)S(1)} %collective-permute-done.13.refs_18_.refs_14_), channel_id=1, source_target_pairs={{0,1},{1,0},{2,3},{3,2},{4,5},{5,4},{6,7},{7,6},{8,9},{9,8},{10,11... | collective-permute-start | bytes 393224 | tf_op jit(solution)/shard_map/ppermute | solution.py:152
  22.1 1.5 %collective-permute-start.10 = (bf16[128,512]{1,0:T(8,128)(2,1)S(1)}, bf16[128,512]{1,0:T(8,128)(2,1)S(1)}, u32[]{:S(2)}, u32[]{:S(2)}) collective-permute-start(bf16[128,512]{1,0:T(8,128)(2,1)S(1)} %collective-permute-done.9.refs_14_.refs_10_), channel_id=1, source_target_pairs={{0,1},{1,0},{2,3},{3,2},{4,5},{5,4},{6,7},{7,6},{8,9},{9,8},{10,11... | collective-permute-start | bytes 393224 | tf_op jit(solution)/shard_map/ppermute | solution.py:152
  24.4 7.2 %collective-permute-start.16 = (bf16[128,512]{1,0:T(8,128)(2,1)S(1)}, bf16[128,512]{1,0:T(8,128)(2,1)S(1)}, u32[]{:S(2)}, u32[]{:S(2)}) collective-permute-start(bf16[128,512]{1,0:T(8,128)(2,1)S(1)} %shard_map.77.own_ref), channel_id=1, source_target_pairs={{0,15},{1,2},{2,1},{3,4},{4,3},{5,6},{6,5},{7,8},{8,7},{9,10},{10,... | collective-permute-start | bytes 393224 | tf_op jit(solution)/shard_map/ppermute | solution.py:163
  29.0 2.7 %collective-permute-start.15 = (bf16[128,512]{1,0:T(8,128)(2,1)S(1)}, bf16[128,512]{1,0:T(8,128)(2,1)S(1)}, u32[]{:S(2)}, u32[]{:S(2)}) collective-permute-start(bf16[128,512]{1,0:T(8,128)(2,1)S(1)} %shard_map.77.own_ref), channel_id=1, source_target_pairs={{0,1},{1,0},{2,3},{3,2},{4,5},{5,4},{6,7},{7,6},{8,9},{9,8},{10,11... | collective-permute-start | bytes 393224 | tf_op jit(solution)/shard_map/ppermute | solution.py:152
  29.0 7.6 %collective-permute-start.17 = (bf16[4,128,128]{2,1,0:T(8,128)(2,1)S(1)}, bf16[4,128,128]{2,1,0:T(8,128)(2,1)S(1)}, u32[]{:S(2)}, u32[]{:S(2)}) collective-permute-start(bf16[4,128,128]{2,1,0:T(8,128)(2,1)S(1)} %get-tuple-element.56), channel_id=1, source_target_pairs={{0,1},{1,0},{2,3},{3,2},{4,5},{5,4},{6,7},{7,6},{8,9},{9,8},{10,11... | collective-permute-start | bytes 393224 | tf_op jit(solution)/shard_map/ppermute | solution.py:152
  29.5 7.1 %collective-permute-start.18 = (bf16[4,128,128]{2,1,0:T(8,128)(2,1)S(1)}, bf16[4,128,128]{2,1,0:T(8,128)(2,1)S(1)}, u32[]{:S(2)}, u32[]{:S(2)}) collective-permute-start(bf16[4,128,128]{2,1,0:T(8,128)(2,1)S(1)} %get-tuple-element.57), channel_id=1, source_target_pairs={{0,2},{1,3},{2,0},{3,1},{4,6},{5,7},{6,4},{7,5},{8,10},{9,11},{10,... | collective-permute-start | bytes 393224 | tf_op jit(solution)/shard_map/ppermute | solution.py:152
  31.6 5.9 %collective-permute-start.19 = (bf16[4,128,128]{2,1,0:T(8,128)(2,1)S(1)}, bf16[4,128,128]{2,1,0:T(8,128)(2,1)S(1)}, u32[]{:S(2)}, u32[]{:S(2)}) collective-permute-start(bf16[4,128,128]{2,1,0:T(8,128)(2,1)S(1)} %get-tuple-element.58), channel_id=1, source_target_pairs={{0,3},{1,2},{2,1},{3,0},{4,7},{5,6},{6,5},{7,4},{8,11},{9,10},{10,... | collective-permute-start | bytes 393224 | tf_op jit(solution)/shard_map/ppermute | solution.py:152
  36.5 4.6 %collective-permute-start.21 = (bf16[128,512]{1,0:T(8,128)(2,1)S(1)}, bf16[128,512]{1,0:T(8,128)(2,1)S(1)}, u32[]{:S(2)}, u32[]{:S(2)}) collective-permute-start(bf16[128,512]{1,0:T(8,128)(2,1)S(1)} %get-tuple-element.62), channel_id=1, source_target_pairs={{0,1},{1,0},{2,3},{3,2},{4,5},{5,4},{6,7},{7,6},{8,9},{9,8},{10,11... | collective-permute-start | bytes 393224 | tf_op jit(solution)/shard_map/ppermute | solution.py:152
  37.5 7.1 %collective-permute-start.22 = (bf16[128,512]{1,0:T(8,128)(2,1)S(1)}, bf16[128,512]{1,0:T(8,128)(2,1)S(1)}, u32[]{:S(2)}, u32[]{:S(2)}) collective-permute-start(bf16[128,512]{1,0:T(8,128)(2,1)S(1)} %get-tuple-element.63), channel_id=1, source_target_pairs={{0,15},{1,2},{2,1},{3,4},{4,3},{5,6},{6,5},{7,8},{8,7},{9,10},{10,... | collective-permute-start | bytes 393224 | tf_op jit(solution)/shard_map/ppermute | solution.py:163
  44.6 5.0 %collective-permute-start.24 = (bf16[128,512]{1,0:T(8,128)(2,1)S(1)}, bf16[128,512]{1,0:T(8,128)(2,1)S(1)}, u32[]{:S(2)}, u32[]{:S(2)}) collective-permute-start(bf16[128,512]{1,0:T(8,128)(2,1)S(1)} %add_convert_fusion.refs_4_), channel_id=1, source_target_pairs={{0,2},{1,3},{2,0},{3,1},{4,6},{5,7},{6,4},{7,5},{8,10},{9,11},{10,... | collective-permute-start | bytes 393224 | tf_op jit(solution)/shard_map/ppermute | solution.py:152
  44.7 5.0 %collective-permute-start.23 = (bf16[128,512]{1,0:T(8,128)(2,1)S(1)}, bf16[128,512]{1,0:T(8,128)(2,1)S(1)}, u32[]{:S(2)}, u32[]{:S(2)}) collective-permute-start(bf16[128,512]{1,0:T(8,128)(2,1)S(1)} %add_convert_fusion.refs_4_), channel_id=1, source_target_pairs={{0,1},{1,0},{2,3},{3,2},{4,5},{5,4},{6,7},{7,6},{8,9},{9,8},{10,11... | collective-permute-start | bytes 393224 | tf_op jit(solution)/shard_map/ppermute | solution.py:152
  49.7 1.3 %collective-permute-start.25 = (bf16[128,512]{1,0:T(8,128)(2,1)S(1)}, bf16[128,512]{1,0:T(8,128)(2,1)S(1)}, u32[]{:S(2)}, u32[]{:S(2)}) collective-permute-start(bf16[128,512]{1,0:T(8,128)(2,1)S(1)} %collective-permute-done.24.refs_6_), channel_id=1, source_target_pairs={{0,1},{1,0},{2,3},{3,2},{4,5},{5,4},{6,7},{7,6},{8,9},{9,8},{10,11... | collective-permute-start | bytes 393224 | tf_op jit(solution)/shard_map/ppermute | solution.py:152
  51.5 8.3 %collective-permute-start.26 = (bf16[128,512]{1,0:T(8,128)(2,1)S(1)}, bf16[128,512]{1,0:T(8,128)(2,1)S(1)}, u32[]{:S(2)}, u32[]{:S(2)}) collective-permute-start(bf16[128,512]{1,0:T(8,128)(2,1)S(1)} %get-tuple-element.70), channel_id=1, source_target_pairs={{0,12},{1,13},{2,14},{3,15},{4,8},{5,9},{6,10},{7,11},{8,4},{9,5},... | collective-permute-start | bytes 393224 | tf_op jit(solution)/shard_map/ppermute | solution.py:152
  55.4 9.4 %collective-permute-start.27 = (bf16[128,512]{1,0:T(8,128)(2,1)S(1)}, bf16[128,512]{1,0:T(8,128)(2,1)S(1)}, u32[]{:S(2)}, u32[]{:S(2)}) collective-permute-start(bf16[128,512]{1,0:T(8,128)(2,1)S(1)} %get-tuple-element.71), channel_id=1, source_target_pairs={{0,8},{1,9},{2,10},{3,11},{4,12},{5,13},{6,14},{7,15},{8,0},{9,1},... | collective-permute-start | bytes 393224 | tf_op jit(solution)/shard_map/ppermute | solution.py:152
  55.4 9.4 %collective-permute-start.28 = (bf16[128,512]{1,0:T(8,128)(2,1)S(1)}, bf16[128,512]{1,0:T(8,128)(2,1)S(1)}, u32[]{:S(2)}, u32[]{:S(2)}) collective-permute-start(bf16[128,512]{1,0:T(8,128)(2,1)S(1)} %get-tuple-element.72), channel_id=1, source_target_pairs={{0,4},{1,5},{2,6},{3,7},{4,0},{5,1},{6,2},{7,3},{8,12},{9,13},{10,... | collective-permute-start | bytes 393224 | tf_op jit(solution)/shard_map/ppermute | solution.py:152
  (2 other events, 12.5 us)

commit v3 on v2

v3 whole, which is shorter than its diff:
```python
import functools
import math

import jax
import jax.numpy as jnp
from jax import lax
from jax.experimental import pallas as pl
from jax.experimental.pallas import tpu as pltpu
from jax.sharding import PartitionSpec as P

HEAD_DIM = 128
KV_HEADS = 2
EPSILON = 1e-06
NT = (((1,), (1,)), ((), ()))
VMEM = pl.BlockSpec(memory_space=pltpu.VMEM)
SMEM = pl.BlockSpec(memory_space=pltpu.SMEM)
PARAMS = pltpu.CompilerParams(vmem_limit_bytes=16 * 1024 * 1024)


def f32dot(a, b, dims=(((1,), (0,)), ((), ()))):
    return lax.dot_general(a, b, dims, preferred_element_type=jnp.float32)


def call(kernel, outs, args, scratch=()):
    in_specs = [SMEM if a.dtype == jnp.int32 else VMEM for a in args]
    return pl.pallas_call(
        kernel,
        out_shape=[jax.ShapeDtypeStruct(s, d) for s, d in outs],
        in_specs=in_specs,
        out_specs=[VMEM] * len(outs),
        scratch_shapes=list(scratch),
        compiler_params=PARAMS,
    )(*args)


def norm_kernel(me_ref, saved_ref, shard_ref, near_ref, lent_ref, t0_ref, t2_ref, t3_ref, factor_ref, copy_ref, held, held_t):
    copy_ref[...] = shard_ref[...]
    blocks, _, width = held.shape
    rest = me_ref[0] % 4
    wide = saved_ref[...].astype(jnp.float32)
    factor = lax.rsqrt(jnp.mean(wide * wide, axis=-1, keepdims=True) + EPSILON)
    factor_ref[...] = factor
    normed = (wide * factor).astype(jnp.bfloat16)
    for b in range(blocks):
        part = normed[:, b * width : (b + 1) * width]
        held[b] = part
        held_t[b] = part.T
    for zz in range(blocks // 4):
        for k in range(2):
            near_ref[k, zz] = held[zz * 4 + (rest ^ (2 * k))]
            lent_ref[k, zz] = held[zz * 4 + (rest ^ (2 * k + 1))]
        for d, ref in ((0, t0_ref), (2, t2_ref), (3, t3_ref)):
            ref[zz] = held_t[zz * 4 + (rest ^ d)]


def kv_kernel(me_ref, near_ref, lent_ref, *refs):
    weights, own_ref, beside_ref = refs[:-2], refs[-2], refs[-1]
    own = me_ref[0] // 4
    rows = own_ref.shape[0]
    total = None
    for half, weight in enumerate(weights):
        at = own ^ (half // 2)
        lhs = jnp.concatenate([near_ref[half % 2, at], lent_ref[half % 2, at]], axis=0)
        part = f32dot(lhs, weight[...])
        total = part if total is None else total + part
    own_ref[...] = total[:rows]
    beside_ref[...] = total[rows:]


def head_pair(ref, pair):
    at = 2 * pair * HEAD_DIM
    first, second = ref[:, at : at + HEAD_DIM], ref[:, at + HEAD_DIM : at + 2 * HEAD_DIM]
    return jnp.concatenate([first, second], axis=0)


def reach(me_ref, rows, near):
    key_pos = lax.broadcasted_iota(jnp.int32, (rows, rows), 0)
    query_pos = lax.broadcasted_iota(jnp.int32, (rows, rows), 1)
    offset = (key_pos - query_pos) * (1 - 2 * (me_ref[0] % 2))
    return jnp.concatenate([offset <= 0 if near else offset >= 0] * 2, axis=1)


def columns(group):
    keys = slice(group * HEAD_DIM, (group + 1) * HEAD_DIM)
    return keys, slice(keys.start + KV_HEADS * HEAD_DIM, keys.stop + KV_HEADS * HEAD_DIM)


def near_kernel(me_ref, q_ref, g_ref, beside_ref, own_ref, lifted_ref, weighted_ref, stats_ref):
    rows = own_ref.shape[0]
    pairs = lifted_ref.shape[0]
    scale = math.log2(math.e) / math.sqrt(HEAD_DIM)
    mask = reach(me_ref, rows, True)
    for group in range(KV_HEADS):
        key_at, value_at = columns(group)
        keys = jnp.concatenate([beside_ref[:, key_at], own_ref[:, key_at]], axis=0)
        values = jnp.concatenate([beside_ref[:, value_at], own_ref[:, value_at]], axis=0)
        for pair in range(group * pairs // KV_HEADS, (group + 1) * pairs // KV_HEADS):
            scores = f32dot(keys, head_pair(q_ref, pair), NT) * scale
            scores = jnp.concatenate([jnp.where(mask, scores[:rows], -1e30), scores[rows:]], axis=0)
            peak = jnp.max(scores, axis=0, keepdims=True)
            lifted = jnp.exp2(scores - peak)
            weighted = lifted * f32dot(values, head_pair(g_ref, pair), NT)
            lifted_ref[pair] = lifted
            weighted_ref[pair] = weighted
            stats_ref[pair, 0:1] = peak
            stats_ref[pair, 1:2] = jnp.sum(lifted, axis=0, keepdims=True)
            stats_ref[pair, 2:3] = jnp.sum(weighted, axis=0, keepdims=True)


def far_kernel(me_ref, q_ref, g_ref, across_ref, stats_ref, owed_ref, d_scores_ref, rest_ref):
    rows = across_ref.shape[0]
    pairs = stats_ref.shape[0]
    scale = 1.0 / math.sqrt(HEAD_DIM)
    mask = reach(me_ref, rows, False)
    for group in range(KV_HEADS):
        key_at, value_at = columns(group)
        keys, values = across_ref[:, key_at], across_ref[:, value_at]
        d_keys = d_values = None
        for pair in range(group * pairs // KV_HEADS, (group + 1) * pairs // KV_HEADS):
            q, g = head_pair(q_ref, pair), head_pair(g_ref, pair)
            scores = f32dot(keys, q, NT) * (scale * math.log2(math.e))
            scores = jnp.where(mask, scores, -1e30)
            near_peak = stats_ref[pair, 0:1]
            peak = jnp.maximum(near_peak, jnp.max(scores, axis=0, keepdims=True))
            lifted = jnp.exp2(scores - peak)
            shrink = jnp.exp2(near_peak - peak)
            weighted = lifted * f32dot(values, g, NT)
            total = stats_ref[pair, 1:2] * shrink + jnp.sum(lifted, axis=0, keepdims=True)
            inverse = 1.0 / total
            row_dot = stats_ref[pair, 2:3] * shrink + jnp.sum(weighted, axis=0, keepdims=True)
            row_dot = row_dot * inverse
            d_scores = ((weighted - lifted * row_dot) * (inverse * scale)).astype(jnp.bfloat16)
            probs = (lifted * inverse).astype(jnp.bfloat16)
            dk, dv = f32dot(d_scores, q), f32dot(probs, g)
            d_keys = dk if d_keys is None else d_keys + dk
            d_values = dv if d_values is None else d_values + dv
            d_scores_ref[pair] = d_scores
            rest_ref[pair, 0:1] = shrink * inverse
            rest_ref[pair, 1:2] = row_dot
        owed_ref[:, key_at] = d_keys.astype(jnp.bfloat16)
        owed_ref[:, value_at] = d_values.astype(jnp.bfloat16)


def close_kernel(q_ref, g_ref, beside_ref, own_ref, across_ref, lifted_ref, weighted_ref, rest_ref, far_ref, dq_ref, db_ref, do_ref):
    rows = own_ref.shape[0]
    pairs = lifted_ref.shape[0]
    scale = 1.0 / math.sqrt(HEAD_DIM)
    for group in range(KV_HEADS):
        key_at, value_at = columns(group)
        keys = jnp.concatenate([r[:, key_at] for r in (beside_ref, own_ref, across_ref)], axis=0).T
        d_keys = d_values = None
        for pair in range(group * pairs // KV_HEADS, (group + 1) * pairs // KV_HEADS):
            lifted = lifted_ref[pair]
            part = rest_ref[pair, 0:1]
            d_scores = (weighted_ref[pair] - lifted * rest_ref[pair, 1:2]) * (part * scale)
            d_scores = d_scores.astype(jnp.bfloat16)
            probs = (lifted * part).astype(jnp.bfloat16)
            dk = f32dot(d_scores, head_pair(q_ref, pair))
            dv = f32dot(probs, head_pair(g_ref, pair))
            d_keys = dk if d_keys is None else d_keys + dk
            d_values = dv if d_values is None else d_values + dv
            dq = f32dot(keys, jnp.concatenate([d_scores, far_ref[pair]], axis=0)).astype(jnp.bfloat16)
            at = 2 * pair * HEAD_DIM
            dq_ref[:, at : at + HEAD_DIM] = dq[:, :rows].T
            dq_ref[:, at + HEAD_DIM : at + 2 * HEAD_DIM] = dq[:, rows:].T
        for at, grad in ((key_at, d_keys), (value_at, d_values)):
            db_ref[:, at] = grad[:rows].astype(jnp.bfloat16)
            do_ref[:, at] = grad[rows:]


def terms_kernel(me_ref, lent_ref, *refs):
    turned, grads, outs = refs[:3], refs[3:7], refs[7:]
    own = me_ref[0] // 4
    d_kv = jnp.concatenate([r[...] for r in grads], axis=0)
    for delta, out_ref in enumerate(outs):
        at = own ^ delta
        lhs = jnp.concatenate([turned[0][at], lent_ref[0, at].T, turned[1][at], turned[2][at]], axis=1)
        out_ref[...] = f32dot(lhs, d_kv).astype(out_ref.dtype)


def input_kernel(own_ref, beside_ref, *refs):
    weights, near_ref, lent_ref = refs[:-2], refs[-2], refs[-1]
    rows, width = own_ref.shape[0], weights[0].shape[0]
    both = jnp.concatenate([own_ref[...], beside_ref[...]], axis=0)
    for half, weight in enumerate(weights):
        part = f32dot(both, weight[...], NT)
        near_ref[half] = part[:rows]
        lent_ref[half] = part[rows:].astype(jnp.bfloat16)


def close_input_kernel(me_ref, saved_ref, factor_ref, up_ref, near_ref, lent_ref, out_ref, held):
    blocks, rows, width = held.shape
    for half in range(blocks // 2):
        delta = half // 2 * 4 + half % 2 * 2
        held[me_ref[0] ^ delta] = near_ref[half]
        held[me_ref[0] ^ delta ^ 1] = lent_ref[half].astype(jnp.float32)
    factor = factor_ref[...]
    acc = jnp.zeros((rows, width), jnp.float32)
    for b in range(blocks):
        normed = saved_ref[:, b * width : (b + 1) * width].astype(jnp.float32) * factor
        acc = acc + held[b] * normed
    mean = jnp.sum(acc, axis=-1, keepdims=True) * (1.0 / (blocks * width))
    for b in range(blocks):
        at = slice(b * width, (b + 1) * width)
        normed = saved_ref[:, at].astype(jnp.float32) * factor
        grad = up_ref[:, at].astype(jnp.float32) + factor * (held[b] - normed * mean)
        out_ref[:, at] = grad.astype(jnp.bfloat16)


def swap(block, distance):
    count = lax.axis_size("ctx")
    return lax.ppermute(block, "ctx", [(i, i ^ distance) for i in range(count)])


def shifted(block, axis, distance):
    count = lax.axis_size(axis)
    return lax.ppermute(block, axis, [((i - distance) % count, i) for i in range(count)])


def crossed(block):
    count = lax.axis_size("ctx")
    route = [(i, (i + 1) % count if i % 2 else (i - 1) % count) for i in range(count)]
    return lax.ppermute(block, "ctx", route)


def gathered(block, pieces):
    count = lax.axis_size("ctx")
    first = count // 2
    parts = {0: block, first: swap(block, first)}
    parts[2] = swap(block, 2)
    far = [0, first]
    step = first // 2
    while step >= 4:
        for d in list(far):
            parts[d ^ step] = swap(parts[d], step)
            far.append(d ^ step)
        step //= 2
    parts[4], pieces = lax.optimization_barrier((parts[4], pieces))
    parts[first], parts[2] = lax.optimization_barrier((parts[first], parts[2]))
    for d in far[1:]:
        direct = d & (first | 4) == first | 4 and first > 4
        parts[d ^ 2] = swap(parts[d ^ 4], 6) if direct else swap(parts[d], 2)
    return [parts[d] for d in range(0, count, 2)], pieces


def per_device(saved_in, grad_in, queries, d_heads, kv_weights):
    count = lax.axis_size("ctx")
    me = lax.axis_index("ctx").astype(jnp.int32).reshape(1)
    bf16, f32 = jnp.bfloat16, jnp.float32
    saved = saved_in[0]
    rows, model = saved.shape
    width, kv2 = kv_weights.shape[1:]
    tall = count // 4
    pieces = call(
        norm_kernel,
        [((2, tall, rows, width), bf16)] * 2 + [((tall, width, rows), bf16)] * 3 + [((rows, 1), f32), ((width, kv2), bf16)],
        [me, saved, kv_weights[0]],
        [pltpu.VMEM((count, rows, width), bf16), pltpu.VMEM((count, width, rows), bf16)],
    )
    weights, pieces = gathered(kv_weights[0], pieces)
    near, lent, *turned, factor, weights[0] = pieces
    lent = swap(lent, 1)
    weights[3], grad_in = lax.optimization_barrier((weights[3], grad_in))
    upstream = shifted(grad_in, "pipe", -1)[0]
    partial = ((rows, kv2), f32)
    half = ((rows, kv2), bf16)
    kv, kv_lent = call(kv_kernel, [partial, partial], [me, near, lent, *weights])
    kv = (kv + swap(kv_lent, 1)).astype(bf16)
    across = crossed(kv)
    beside = swap(kv, 1)
    pairs = model // (2 * HEAD_DIM)
    block = ((pairs, 2 * rows, 2 * rows), f32)
    lifted, weighted, stats = call(
        near_kernel,
        [block, block, ((pairs, 3, 2 * rows), f32)],
        [me, queries[0], d_heads[0], beside, kv],
    )
    stats, turned = lax.optimization_barrier((stats, turned))
    turned = [turned[0], swap(turned[1], 2), swap(turned[2], 3)]
    d_across, far, kept = call(
        far_kernel,
        [half, ((pairs, rows, 2 * rows), bf16), ((pairs, 2, 2 * rows), f32)],
        [me, queries[0], d_heads[0], across, stats],
    )
    from_across = crossed(d_across)
    d_queries, d_beside, d_own = call(
        close_kernel,
        [((rows, model), bf16), half, partial],
        [queries[0], d_heads[0], beside, kv, across, lifted, weighted, kept, far],
    )
    d_beside, turned, upstream = lax.optimization_barrier((d_beside, turned, upstream))
    from_beside = swap(d_beside, 1)
    d_kv = (d_own + from_beside.astype(f32) + from_across.astype(f32)).astype(bf16)
    above = swap(d_kv, 2)
    d_beside = swap(d_kv, 1)
    grads = [d_kv, d_beside, above, swap(above, 1)]
    terms = call(
        terms_kernel,
        [((width, kv2), f32)] + [((width, kv2), bf16)] * (tall - 1),
        [me, lent, *turned, *grads],
    )
    order = [*range(tall // 2, tall), *range(1, tall // 2)]
    received = [swap(terms[delta], 4 * delta) for delta in order]
    near, lent = call(
        input_kernel,
        [((count // 2, rows, width), f32), ((count // 2, rows, width), bf16)],
        [d_kv, d_beside, *weights],
    )
    (grad_out,) = call(
        close_input_kernel,
        [((rows, model), bf16)],
        [me, saved, factor, upstream, near, swap(lent, 1)],
        [pltpu.VMEM((count, rows, width), f32)],
    )
    received, grad_out = lax.optimization_barrier((received, grad_out))
    total = terms[0]
    for part in received:
        total = total + part.astype(f32)
    weight_grad = total * (1.0 / math.sqrt(rows * count))
    return (grad_out[None], d_queries[None], weight_grad[None])


def solution(mesh):
    spec = P("pipe", "ctx", None)
    return jax.shard_map(
        per_device, mesh=mesh, in_specs=(spec,) * 5, out_specs=(spec,) * 3, check_vma=False
    )
```

time: 65.8 us -> 61.3 us (0.932)
  starting transfers between devices: 29.6 us -> 24.7 us
  local copies, waits for them, and re-layouts: 1.06 us -> 1.96 us
    ppermute x26 -> x20, starting transfers between devices: 19.7 us -> 16.3 us  [swap(): return lax.ppermute(block, 'ctx', [(i, i ^ distance) for i in range(count)])]
    ppermute x2, starting transfers between devices: 8.28 us -> 6.83 us  [crossed(): return lax.ppermute(block, 'ctx', route)]
    ppermute x2, waiting for transfers between devices: 5.54 us -> 4.27 us  [crossed(): return lax.ppermute(block, 'ctx', route)]
    ppermute x26 -> x20, waiting for transfers between devices: 19 us -> 19.9 us  [swap(): return lax.ppermute(block, 'ctx', [(i, i ^ distance) for i in range(count)])]
    unnamed x10 -> x12, local copies, waits for them, and re-layouts: 1.06 us -> 1.96 us
    pallas_call x5 -> x8, Pallas kernels: 8.93 us -> 8.59 us  [call(): pl.pallas_call(kernel, out_shape=[jax.ShapeDtypeStruct(s, d) for s, d in...]
  transfers between devices with their start and end apart: 29 -> 23, of which waited for: 13 -> 9; matrix products, arithmetic and copies ran while one was open for 0% -> 0% of each run, Pallas kernels for 13% -> 13%
where the time goes in v3:
time: 61.3 us; the launch traced here: 61.1 us
  starting transfers between devices  24.7 us (40%)
  waiting for transfers between devices  24.2 us (39%)
  Pallas kernels  8.59 us (14%)
  local copies, waits for them, and re-layouts  1.96 us (3%)
  other arithmetic  0.85 us (1%)
  between operations  0.82 us (1%)
    ppermute x20, waiting for transfers between devices, swap(): return lax.ppermute(block, 'ctx', [(i, i ^ distance) for i in range(count)])  19.9 us
    ppermute x20, starting transfers between devices, swap(): return lax.ppermute(block, 'ctx', [(i, i ^ distance) for i in range(count)])  16.3 us
    pallas_call x8, Pallas kernels, call(): pl.pallas_call(kernel, out_shape=[jax.ShapeDtypeStruct(s, d) for s, d in...  8.59 us
    ppermute x2, starting transfers between devices, crossed(): return lax.ppermute(block, 'ctx', route)  6.83 us
    ppermute x2, waiting for transfers between devices, crossed(): return lax.ppermute(block, 'ctx', route)  4.27 us
    unnamed x12, local copies, waits for them, and re-layouts  1.96 us
    ppermute x1, starting transfers between devices, shifted(): lax.ppermute(block, axis, [((i - distance) % count, i) for i in range(cou...  1.55 us
  transfers between devices with their start and end apart: 23, of which 9 were waited for; matrix products, arithmetic and copies ran while one was open for 0% of the time, Pallas kernels for 13%

profile of v3, /device:TPU:0, one launch (start us, length us, event | category | flops | bytes accessed | tf_op | source)
XLA Modules:
  0.0 61.1 jit_solution(11977930368842294074)
XLA Ops:
  0.7 3.1 %collective-permute-start = (bf16[128,512]{1,0:T(8,128)(2,1)}, bf16[128,512]{1,0:T(8,128)(2,1)S(1)}, u32[]{:S(2)}, u32[]{:S(2)}) collective-permute-start(bf16[128,512]{1,0:T(8,128)(2,1)} %bitcast.19), channel_id=1, source_target_pairs={{0,4},{1,5},{2,6},{3,7},{4,0},{5,1},{6,2},{7,3},{8,12},{9,13},{10,... | collective-permute-start | bytes 393224 | tf_op jit(solution)/shard_map/ppermute | solution.py:212
  3.7 2.6 %collective-permute-start.2 = (bf16[128,512]{1,0:T(8,128)(2,1)}, bf16[128,512]{1,0:T(8,128)(2,1)S(1)}, u32[]{:S(2)}, u32[]{:S(2)}) collective-permute-start(bf16[128,512]{1,0:T(8,128)(2,1)} %bitcast.20), channel_id=1, source_target_pairs={{0,8},{1,9},{2,10},{3,11},{4,12},{5,13},{6,14},{7,15},{8,0},{9,1},... | collective-permute-start | bytes 393224 | tf_op jit(solution)/shard_map/ppermute | solution.py:212
  6.3 1.5 %collective-permute-start.3 = (bf16[128,512]{1,0:T(8,128)(2,1)}, bf16[128,512]{1,0:T(8,128)(2,1)S(1)}, u32[]{:S(2)}, u32[]{:S(2)}) collective-permute-start(bf16[128,512]{1,0:T(8,128)(2,1)} %bitcast.21), channel_id=1, source_target_pairs={{0,2},{1,3},{2,0},{3,1},{4,6},{5,7},{6,4},{7,5},{8,10},{9,11},{10,... | collective-permute-start | bytes 393224 | tf_op jit(solution)/shard_map/ppermute | solution.py:212
  7.9 1.0 %copy-done.2 = bf16[1,128,2048]{2,1,0:T(8,128)(2,1)S(1)} copy-done((bf16[1,128,2048]{2,1,0:T(8,128)(2,1)S(1)}, bf16[1,128,2048]{2,1,0:T(8,128)(2,1)}, u32[]{:S(2)}) %copy-start.2) | copy-done | bytes 524312
  8.9 0.9 %copy-done.4 = bf16[1,128,512]{2,1,0:T(8,128)(2,1)S(1)} copy-done((bf16[1,128,512]{2,1,0:T(8,128)(2,1)S(1)}, bf16[1,128,512]{2,1,0:T(8,128)(2,1)}, u32[]{:S(2)}) %copy-start.4) | copy-done | bytes 131096
  9.8 0.4 shard_map.76
  10.3 0.8 %collective-permute-start.4 = (bf16[128,512]{1,0:T(8,128)(2,1)S(1)}, bf16[128,512]{1,0:T(8,128)(2,1)S(1)}, u32[]{:S(2)}, u32[]{:S(2)}) collective-permute-start(bf16[128,512]{1,0:T(8,128)(2,1)S(1)} %collective-permute-done.refs_2_), channel_id=1, source_target_pairs={{0,2},{1,3},{2,0},{3,1},{4,6},{5,7},{6,4},{7,5},{8,10},{9,11},{10,... | collective-permute-start | bytes 393224 | tf_op jit(solution)/shard_map/ppermute | solution.py:212
  11.1 1.6 %collective-permute-done.2.refs_4_ = bf16[128,512]{1,0:T(8,128)(2,1)S(1)} collective-permute-done((bf16[128,512]{1,0:T(8,128)(2,1)}, bf16[128,512]{1,0:T(8,128)(2,1)S(1)}, u32[]{:S(2)}, u32[]{:S(2)}) %collective-permute-start.2) | collective-permute-done | bytes 131104 | tf_op jit(solution)/shard_map/ppermute | solution.py:212
  12.7 1.5 %collective-permute-start.5 = (bf16[128,512]{1,0:T(8,128)(2,1)S(1)}, bf16[128,512]{1,0:T(8,128)(2,1)S(1)}, u32[]{:S(2)}, u32[]{:S(2)}) collective-permute-start(bf16[128,512]{1,0:T(8,128)(2,1)S(1)} %collective-permute-done.2.refs_4_), channel_id=1, source_target_pairs={{0,2},{1,3},{2,0},{3,1},{4,6},{5,7},{6,4},{7,5},{8,10},{9,11},{10,... | collective-permute-start | bytes 393224 | tf_op jit(solution)/shard_map/ppermute | solution.py:212
  14.2 0.4 collective-permute-start.7
  14.6 1.6 %collective-permute-start.6 = (bf16[128,512]{1,0:T(8,128)(2,1)S(1)}, bf16[128,512]{1,0:T(8,128)(2,1)S(1)}, u32[]{:S(2)}, u32[]{:S(2)}) collective-permute-start(bf16[128,512]{1,0:T(8,128)(2,1)S(1)} %collective-permute-done.2.refs_4_), channel_id=1, source_target_pairs={{0,4},{1,5},{2,6},{3,7},{4,0},{5,1},{6,2},{7,3},{8,12},{9,13},{10,... | collective-permute-start | bytes 393224 | tf_op jit(solution)/shard_map/ppermute | solution.py:212
  16.2 1.9 %collective-permute-done.4.refs_3_ = bf16[128,512]{1,0:T(8,128)(2,1)S(1)} collective-permute-done((bf16[128,512]{1,0:T(8,128)(2,1)S(1)}, bf16[128,512]{1,0:T(8,128)(2,1)S(1)}, u32[]{:S(2)}, u32[]{:S(2)}) %collective-permute-start.4) | collective-permute-done | bytes 131104 | tf_op jit(solution)/shard_map/ppermute | solution.py:212
  18.1 3.8 %collective-permute-done.5.refs_5_ = bf16[128,512]{1,0:T(8,128)(2,1)S(1)} collective-permute-done((bf16[128,512]{1,0:T(8,128)(2,1)S(1)}, bf16[128,512]{1,0:T(8,128)(2,1)S(1)}, u32[]{:S(2)}, u32[]{:S(2)}) %collective-permute-start.5) | collective-permute-done | bytes 131104 | tf_op jit(solution)/shard_map/ppermute | solution.py:212
  21.9 0.7 %shard_map.77 = (f32[128,512]{1,0:T(8,128)S(1)}, f32[128,512]{1,0:T(8,128)S(1)}) custom-call(s32[1]{0:T(128)} %bitcast.me_ref, bf16[2,4,128,128]{3,2,1,0:T(8,128)(2,1)S(1)} %get-tuple-element.60.near_ref, bf16[2,4,128,128]{3,2,1,0:T(8,128)(2,1)S(1)} %collective-permute-done.1.lent_ref, bf16[128,512]{1,0:T(8,128)(2,1)S(1)} %get-tuple-element.61.refs_0_, ...), custom_call_target="tpu_custom_call" | custom-call | tf_op jit(solution)/shard_map/pallas_call | solution.py:26
  22.6 1.6 %collective-permute-start.13 = (bf16[1,128,2048]{2,1,0:T(8,128)(2,1)S(1)}, bf16[1,128,2048]{2,1,0:T(8,128)(2,1)S(1)}, u32[]{:S(2)}, u32[]{:S(2)}) collective-permute-start(bf16[1,128,2048]{2,1,0:T(8,128)(2,1)S(1)} %copy-done.5), channel_id=1, source_target_pairs={{16,0},{0,16},{17,1},{1,17},{18,2},{2,18},{19,3},{3,19},{20,4},{4,... | collective-permute-start | bytes 1572872 | tf_op jit(solution)/shard_map/ppermute | solution.py:217
  24.5 3.4 %collective-permute-start.10 = (bf16[128,512]{1,0:T(8,128)(2,1)S(1)}, bf16[128,512]{1,0:T(8,128)(2,1)S(1)}, u32[]{:S(2)}, u32[]{:S(2)}) collective-permute-start(bf16[128,512]{1,0:T(8,128)(2,1)S(1)} %add_convert_fusion.1.own_ref), channel_id=1, source_target_pairs={{0,15},{1,2},{2,1},{3,4},{4,3},{5,6},{6,5},{7,8},{8,7},{9,10},{10,... | collective-permute-start | bytes 393224 | tf_op jit(solution)/shard_map/ppermute | solution.py:223
  27.9 1.0 %shard_map.78 = (f32[8,256,256]{2,1,0:T(8,128)S(1)}, f32[8,256,256]{2,1,0:T(8,128)S(1)}, f32[8,3,256]{2,1,0:T(4,128)S(1)}) custom-call(s32[1]{0:T(128)} %bitcast.me_ref, bf16[128,2048]{1,0:T(8,128)(2,1)S(1)} %bitcast.10, bf16[128,2048]{1,0:T(8,128)(2,1)S(1)} %bitcast.13, bf16[128,512]{1,0:T(8,128)(2,1)S(1)} %collective-permute-done.9.beside_ref, ...), custom_call_target="tpu_custom_call" | custom-call | tf_op jit(solution)/shard_map/pallas_call | solution.py:26
  29.0 2.6 %collective-permute-done.10.across_ref = bf16[128,512]{1,0:T(8,128)(2,1)S(1)} collective-permute-done((bf16[128,512]{1,0:T(8,128)(2,1)S(1)}, bf16[128,512]{1,0:T(8,128)(2,1)S(1)}, u32[]{:S(2)}, u32[]{:S(2)}) %collective-permute-start.10) | collective-permute-done | bytes 131104 | tf_op jit(solution)/shard_map/ppermute | solution.py:223
  31.7 1.9 %shard_map.79 = (bf16[128,512]{1,0:T(8,128)(2,1)S(1)}, bf16[8,128,256]{2,1,0:T(8,128)(2,1)S(1)}, f32[8,2,256]{2,1,0:T(2,128)S(1)}) custom-call(s32[1]{0:T(128)} %bitcast.me_ref, bf16[128,2048]{1,0:T(8,128)(2,1)S(1)} %bitcast.11, bf16[128,2048]{1,0:T(8,128)(2,1)S(1)} %bitcast.14, bf16[128,512]{1,0:T(8,128)(2,1)S(1)} %collective-permute-done.10.across_ref, ...), custom_call_target="tpu_custom_call" | custom-call | tf_op jit(solution)/shard_map/pallas_call | solution.py:26
  33.6 3.5 %collective-permute-start.15 = (bf16[128,512]{1,0:T(8,128)(2,1)S(1)}, bf16[128,512]{1,0:T(8,128)(2,1)S(1)}, u32[]{:S(2)}, u32[]{:S(2)}) collective-permute-start(bf16[128,512]{1,0:T(8,128)(2,1)S(1)} %get-tuple-element.87), channel_id=1, source_target_pairs={{0,15},{1,2},{2,1},{3,4},{4,3},{5,6},{6,5},{7,8},{8,7},{9,10},{10,... | collective-permute-start | bytes 393224 | tf_op jit(solution)/shard_map/ppermute | solution.py:223
  37.1 2.0 %shard_map.80 = (bf16[128,2048]{1,0:T(8,128)(2,1)}, bf16[128,512]{1,0:T(8,128)(2,1)S(1)}, f32[128,512]{1,0:T(8,128)S(1)}) custom-call(bf16[128,2048]{1,0:T(8,128)(2,1)S(1)} %bitcast.12, bf16[128,2048]{1,0:T(8,128)(2,1)S(1)} %bitcast.15, bf16[128,512]{1,0:T(8,128)(2,1)S(1)} %collective-permute-done.9.beside_ref, ...), custom_call_target="tpu_custom_call" | custom-call | tf_op jit(solution)/shard_map/pallas_call | solution.py:26
  39.1 1.6 %collective-permute-done.15 = bf16[128,512]{1,0:T(8,128)(2,1)S(1)} collective-permute-done((bf16[128,512]{1,0:T(8,128)(2,1)S(1)}, bf16[128,512]{1,0:T(8,128)(2,1)S(1)}, u32[]{:S(2)}, u32[]{:S(2)}) %collective-permute-start.15) | collective-permute-done | bytes 131104 | tf_op jit(solution)/shard_map/ppermute | solution.py:223
  41.0 5.2 %collective-permute-done.17.refs_5_ = bf16[128,512]{1,0:T(8,128)(2,1)S(1)} collective-permute-done((bf16[128,512]{1,0:T(8,128)(2,1)S(1)}, bf16[128,512]{1,0:T(8,128)(2,1)S(1)}, u32[]{:S(2)}, u32[]{:S(2)}) %collective-permute-start.17) | collective-permute-done | bytes 131104 | tf_op jit(solution)/shard_map/ppermute | solution.py:212
  46.1 0.7 %shard_map.82 = (f32[8,128,128]{2,1,0:T(8,128)S(1)}, bf16[8,128,128]{2,1,0:T(8,128)(2,1)S(1)}) custom-call(bf16[128,512]{1,0:T(8,128)(2,1)S(1)} %add_convert_fusion.refs_3_.own_ref, bf16[128,512]{1,0:T(8,128)(2,1)S(1)} %collective-permute-done.16.refs_4_.beside_ref, bf16[128,512]{1,0:T(8,128)(2,1)S(1)} %get-tuple-element.61.refs_0_, ...), custom_call_target="tpu_custom_call" | custom-call | tf_op jit(solution)/shard_map/pallas_call | solution.py:26
  46.9 0.6 collective-permute-start.22
  47.5 0.5 shard_map.81
  48.0 1.2 %collective-permute-start.20 = (bf16[128,512]{1,0:T(8,128)(2,1)S(1)}, bf16[128,512]{1,0:T(8,128)(2,1)S(1)}, u32[]{:S(2)}, u32[]{:S(2)}) collective-permute-start(bf16[128,512]{1,0:T(8,128)(2,1)S(1)} %get-tuple-element.89), channel_id=1, source_target_pairs={{0,12},{1,13},{2,14},{3,15},{4,8},{5,9},{6,10},{7,11},{8,4},{9,5},... | collective-permute-start | bytes 393224 | tf_op jit(solution)/shard_map/ppermute | solution.py:212
  49.3 2.2 %collective-permute-start.21 = (bf16[128,512]{1,0:T(8,128)(2,1)S(1)}, bf16[128,512]{1,0:T(8,128)(2,1)S(1)}, u32[]{:S(2)}, u32[]{:S(2)}) collective-permute-start(bf16[128,512]{1,0:T(8,128)(2,1)S(1)} %get-tuple-element.90), channel_id=1, source_target_pairs={{0,4},{1,5},{2,6},{3,7},{4,0},{5,1},{6,2},{7,3},{8,12},{9,13},{10,... | collective-permute-start | bytes 393224 | tf_op jit(solution)/shard_map/ppermute | solution.py:212
  51.5 1.4 %shard_map.83 = bf16[128,2048]{1,0:T(8,128)(2,1)} custom-call(s32[1]{0:T(128)} %bitcast.me_ref, bf16[128,2048]{1,0:T(8,128)(2,1)S(1)} %bitcast.17, f32[128,1]{1,0:T(8,128)S(1)} %get-tuple-element.91.factor_ref, bf16[128,2048]{1,0:T(8,128)(2,1)S(1)} %bitcast.18, f32[8,128,128]{2,1,0:T(8,128)S(1)} %get-tuple-element.93.near_ref, ...), custom_call_target="tpu_custom_call" | custom-call | tf_op jit(solution)/shard_map/pallas_call | solution.py:26
  52.9 5.8 %collective-permute-done.19 = bf16[128,512]{1,0:T(8,128)(2,1)S(1)} collective-permute-done((bf16[128,512]{1,0:T(8,128)(2,1)S(1)}, bf16[128,512]{1,0:T(8,128)(2,1)S(1)}, u32[]{:S(2)}, u32[]{:S(2)}) %collective-permute-start.19) | collective-permute-done | bytes 131104 | tf_op jit(solution)/shard_map/ppermute | solution.py:212
  58.7 1.7 %collective-permute-done.21 = bf16[128,512]{1,0:T(8,128)(2,1)S(1)} collective-permute-done((bf16[128,512]{1,0:T(8,128)(2,1)S(1)}, bf16[128,512]{1,0:T(8,128)(2,1)S(1)}, u32[]{:S(2)}, u32[]{:S(2)}) %collective-permute-start.21) | collective-permute-done | bytes 131104 | tf_op jit(solution)/shard_map/ppermute | solution.py:212
  60.4 0.8 %multiply_bitcast_fusion = f32[1,128,512]{2,1,0:T(8,128)} fusion(bf16[128,512]{1,0:T(8,128)(2,1)S(1)} %collective-permute-done.21, bf16[128,512]{1,0:T(8,128)(2,1)S(1)} %collective-permute-done.20, f32[128,512]{1,0:T(8,128)S(1)} %get-tuple-element.97, bf16[128,512]{1,0:T(8,128)(2,1)S(1)} %collective-permute-done.19), kind=kLoop, calls=%fused_computation | loop fusion | flops 458752 | bytes 917504 | tf_op jit(solution)/shard_map/broadcast_in_dim | solution.py:320
  (37 shorter events, 1.0 us)
Async XLA Ops:
  0.6 27.2 %copy-start = (bf16[1,128,2048]{2,1,0:T(8,128)(2,1)S(1)}, bf16[1,128,2048]{2,1,0:T(8,128)(2,1)}, u32[]{:S(2)}) copy-start(bf16[1,128,2048]{2,1,0:T(8,128)(2,1)} %param.7) | copy-start | bytes 1572868
  0.6 27.2 %copy-start.1 = (bf16[1,128,2048]{2,1,0:T(8,128)(2,1)S(1)}, bf16[1,128,2048]{2,1,0:T(8,128)(2,1)}, u32[]{:S(2)}) copy-start(bf16[1,128,2048]{2,1,0:T(8,128)(2,1)} %param.8) | copy-start | bytes 1572868
  0.7 9.6 %collective-permute-start = (bf16[128,512]{1,0:T(8,128)(2,1)}, bf16[128,512]{1,0:T(8,128)(2,1)S(1)}, u32[]{:S(2)}, u32[]{:S(2)}) collective-permute-start(bf16[128,512]{1,0:T(8,128)(2,1)} %bitcast.19), channel_id=1, source_target_pairs={{0,4},{1,5},{2,6},{3,7},{4,0},{5,1},{6,2},{7,3},{8,12},{9,13},{10,... | collective-permute-start | bytes 393224 | tf_op jit(solution)/shard_map/ppermute | solution.py:212
  3.7 8.9 %collective-permute-start.2 = (bf16[128,512]{1,0:T(8,128)(2,1)}, bf16[128,512]{1,0:T(8,128)(2,1)S(1)}, u32[]{:S(2)}, u32[]{:S(2)}) collective-permute-start(bf16[128,512]{1,0:T(8,128)(2,1)} %bitcast.20), channel_id=1, source_target_pairs={{0,8},{1,9},{2,10},{3,11},{4,12},{5,13},{6,14},{7,15},{8,0},{9,1},... | collective-permute-start | bytes 393224 | tf_op jit(solution)/shard_map/ppermute | solution.py:212
  6.3 6.4 %collective-permute-start.3 = (bf16[128,512]{1,0:T(8,128)(2,1)}, bf16[128,512]{1,0:T(8,128)(2,1)S(1)}, u32[]{:S(2)}, u32[]{:S(2)}) collective-permute-start(bf16[128,512]{1,0:T(8,128)(2,1)} %bitcast.21), channel_id=1, source_target_pairs={{0,2},{1,3},{2,0},{3,1},{4,6},{5,7},{6,4},{7,5},{8,10},{9,11},{10,... | collective-permute-start | bytes 393224 | tf_op jit(solution)/shard_map/ppermute | solution.py:212
  7.8 1.0 %copy-start.2 = (bf16[1,128,2048]{2,1,0:T(8,128)(2,1)S(1)}, bf16[1,128,2048]{2,1,0:T(8,128)(2,1)}, u32[]{:S(2)}) copy-start(bf16[1,128,2048]{2,1,0:T(8,128)(2,1)} %param.5) | copy-start | bytes 1572868
  8.9 0.9 %copy-start.4 = (bf16[1,128,512]{2,1,0:T(8,128)(2,1)S(1)}, bf16[1,128,512]{2,1,0:T(8,128)(2,1)}, u32[]{:S(2)}) copy-start(bf16[1,128,512]{2,1,0:T(8,128)(2,1)} %param.9) | copy-start | bytes 393220
  9.8 12.8 %copy-start.5 = (bf16[1,128,2048]{2,1,0:T(8,128)(2,1)S(1)}, bf16[1,128,2048]{2,1,0:T(8,128)(2,1)}, u32[]{:S(2)}) copy-start(bf16[1,128,2048]{2,1,0:T(8,128)(2,1)} %param.6) | copy-start | bytes 1572868
  10.2 11.6 %collective-permute-start.1 = (bf16[2,4,128,128]{3,2,1,0:T(8,128)(2,1)S(1)}, bf16[2,4,128,128]{3,2,1,0:T(8,128)(2,1)S(1)}, u32[]{:S(2)}, u32[]{:S(2)}) collective-permute-start(bf16[2,4,128,128]{3,2,1,0:T(8,128)(2,1)S(1)} %get-tuple-element.59), channel_id=1, source_target_pairs={{0,1},{1,0},{2,3},{3,2},{4,5},{5,4},{6,7},{7,6},{8,9},{9,8},{10,11... | collective-permute-start | bytes 786440 | tf_op jit(solution)/shard_map/ppermute | solution.py:212
  10.3 7.8 %collective-permute-start.4 = (bf16[128,512]{1,0:T(8,128)(2,1)S(1)}, bf16[128,512]{1,0:T(8,128)(2,1)S(1)}, u32[]{:S(2)}, u32[]{:S(2)}) collective-permute-start(bf16[128,512]{1,0:T(8,128)(2,1)S(1)} %collective-permute-done.refs_2_), channel_id=1, source_target_pairs={{0,2},{1,3},{2,0},{3,1},{4,6},{5,7},{6,4},{7,5},{8,10},{9,11},{10,... | collective-permute-start | bytes 393224 | tf_op jit(solution)/shard_map/ppermute | solution.py:212
  12.7 9.2 %collective-permute-start.5 = (bf16[128,512]{1,0:T(8,128)(2,1)S(1)}, bf16[128,512]{1,0:T(8,128)(2,1)S(1)}, u32[]{:S(2)}, u32[]{:S(2)}) collective-permute-start(bf16[128,512]{1,0:T(8,128)(2,1)S(1)} %collective-permute-done.2.refs_4_), channel_id=1, source_target_pairs={{0,2},{1,3},{2,0},{3,1},{4,6},{5,7},{6,4},{7,5},{8,10},{9,11},{10,... | collective-permute-start | bytes 393224 | tf_op jit(solution)/shard_map/ppermute | solution.py:212
  14.2 7.6 %collective-permute-start.7 = (bf16[128,512]{1,0:T(8,128)(2,1)S(1)}, bf16[128,512]{1,0:T(8,128)(2,1)S(1)}, u32[]{:S(2)}, u32[]{:S(2)}) collective-permute-start(bf16[128,512]{1,0:T(8,128)(2,1)S(1)} %collective-permute-done.2.refs_4_), channel_id=1, source_target_pairs={{0,6},{1,7},{2,4},{3,5},{4,2},{5,3},{6,0},{7,1},{8,14},{9,15},{10,... | collective-permute-start | bytes 393224 | tf_op jit(solution)/shard_map/ppermute | solution.py:212
  14.6 7.3 %collective-permute-start.6 = (bf16[128,512]{1,0:T(8,128)(2,1)S(1)}, bf16[128,512]{1,0:T(8,128)(2,1)S(1)}, u32[]{:S(2)}, u32[]{:S(2)}) collective-permute-start(bf16[128,512]{1,0:T(8,128)(2,1)S(1)} %collective-permute-done.2.refs_4_), channel_id=1, source_target_pairs={{0,4},{1,5},{2,6},{3,7},{4,0},{5,1},{6,2},{7,3},{8,12},{9,13},{10,... | collective-permute-start | bytes 393224 | tf_op jit(solution)/shard_map/ppermute | solution.py:212
  22.6 1.6 %collective-permute-start.8 = (f32[128,512]{1,0:T(8,128)S(1)}, f32[128,512]{1,0:T(8,128)S(1)}, u32[]{:S(2)}, u32[]{:S(2)}) collective-permute-start(f32[128,512]{1,0:T(8,128)S(1)} %get-tuple-element.67), channel_id=1, source_target_pairs={{0,1},{1,0},{2,3},{3,2},{4,5},{5,4},{6,7},{7,6},{8,9},{9,8},{10,11... | collective-permute-start | bytes 786440 | tf_op jit(solution)/shard_map/ppermute | solution.py:212
  22.6 16.4 %collective-permute-start.13 = (bf16[1,128,2048]{2,1,0:T(8,128)(2,1)S(1)}, bf16[1,128,2048]{2,1,0:T(8,128)(2,1)S(1)}, u32[]{:S(2)}, u32[]{:S(2)}) collective-permute-start(bf16[1,128,2048]{2,1,0:T(8,128)(2,1)S(1)} %copy-done.5), channel_id=1, source_target_pairs={{16,0},{0,16},{17,1},{1,17},{18,2},{2,18},{19,3},{3,19},{20,4},{4,... | collective-permute-start | bytes 1572872 | tf_op jit(solution)/shard_map/ppermute | solution.py:217
  24.2 3.6 %collective-permute-start.9 = (bf16[128,512]{1,0:T(8,128)(2,1)S(1)}, bf16[128,512]{1,0:T(8,128)(2,1)S(1)}, u32[]{:S(2)}, u32[]{:S(2)}) collective-permute-start(bf16[128,512]{1,0:T(8,128)(2,1)S(1)} %add_convert_fusion.1.own_ref), channel_id=1, source_target_pairs={{0,1},{1,0},{2,3},{3,2},{4,5},{5,4},{6,7},{7,6},{8,9},{9,8},{10,11... | collective-permute-start | bytes 393224 | tf_op jit(solution)/shard_map/ppermute | solution.py:212
  24.5 7.2 %collective-permute-start.10 = (bf16[128,512]{1,0:T(8,128)(2,1)S(1)}, bf16[128,512]{1,0:T(8,128)(2,1)S(1)}, u32[]{:S(2)}, u32[]{:S(2)}) collective-permute-start(bf16[128,512]{1,0:T(8,128)(2,1)S(1)} %add_convert_fusion.1.own_ref), channel_id=1, source_target_pairs={{0,15},{1,2},{2,1},{3,4},{4,3},{5,6},{6,5},{7,8},{8,7},{9,10},{10,... | collective-permute-start | bytes 393224 | tf_op jit(solution)/shard_map/ppermute | solution.py:223
  28.9 10.2 %collective-permute-start.11 = (bf16[4,128,128]{2,1,0:T(8,128)(2,1)S(1)}, bf16[4,128,128]{2,1,0:T(8,128)(2,1)S(1)}, u32[]{:S(2)}, u32[]{:S(2)}) collective-permute-start(bf16[4,128,128]{2,1,0:T(8,128)(2,1)S(1)} %get-tuple-element.79), channel_id=1, source_target_pairs={{0,2},{1,3},{2,0},{3,1},{4,6},{5,7},{6,4},{7,5},{8,10},{9,11},{10,... | collective-permute-start | bytes 393224 | tf_op jit(solution)/shard_map/ppermute | solution.py:212
  28.9 10.1 %collective-permute-start.12 = (bf16[4,128,128]{2,1,0:T(8,128)(2,1)S(1)}, bf16[4,128,128]{2,1,0:T(8,128)(2,1)S(1)}, u32[]{:S(2)}, u32[]{:S(2)}) collective-permute-start(bf16[4,128,128]{2,1,0:T(8,128)(2,1)S(1)} %get-tuple-element.80), channel_id=1, source_target_pairs={{0,3},{1,2},{2,1},{3,0},{4,7},{5,6},{6,5},{7,4},{8,11},{9,10},{10,... | collective-permute-start | bytes 393224 | tf_op jit(solution)/shard_map/ppermute | solution.py:212
  33.6 7.2 %collective-permute-start.15 = (bf16[128,512]{1,0:T(8,128)(2,1)S(1)}, bf16[128,512]{1,0:T(8,128)(2,1)S(1)}, u32[]{:S(2)}, u32[]{:S(2)}) collective-permute-start(bf16[128,512]{1,0:T(8,128)(2,1)S(1)} %get-tuple-element.87), channel_id=1, source_target_pairs={{0,15},{1,2},{2,1},{3,4},{4,3},{5,6},{6,5},{7,8},{8,7},{9,10},{10,... | collective-permute-start | bytes 393224 | tf_op jit(solution)/shard_map/ppermute | solution.py:223
  39.0 12.5 %copy-start.3 = (bf16[1,128,2048]{2,1,0:T(8,128)(2,1)S(1)}, bf16[1,128,2048]{2,1,0:T(8,128)(2,1)}, u32[]{:S(2)}) copy-start(bf16[1,128,2048]{2,1,0:T(8,128)(2,1)} %param.5) | copy-start | bytes 1572868
  39.1 1.7 %collective-permute-start.14 = (bf16[128,512]{1,0:T(8,128)(2,1)S(1)}, bf16[128,512]{1,0:T(8,128)(2,1)S(1)}, u32[]{:S(2)}, u32[]{:S(2)}) collective-permute-start(bf16[128,512]{1,0:T(8,128)(2,1)S(1)} %get-tuple-element.86), channel_id=1, source_target_pairs={{0,1},{1,0},{2,3},{3,2},{4,5},{5,4},{6,7},{7,6},{8,9},{9,8},{10,11... | collective-permute-start | bytes 393224 | tf_op jit(solution)/shard_map/ppermute | solution.py:212
  40.8 5.3 %collective-permute-start.17 = (bf16[128,512]{1,0:T(8,128)(2,1)S(1)}, bf16[128,512]{1,0:T(8,128)(2,1)S(1)}, u32[]{:S(2)}, u32[]{:S(2)}) collective-permute-start(bf16[128,512]{1,0:T(8,128)(2,1)S(1)} %add_convert_fusion.refs_3_.own_ref), channel_id=1, source_target_pairs={{0,2},{1,3},{2,0},{3,1},{4,6},{5,7},{6,4},{7,5},{8,10},{9,11},{10,... | collective-permute-start | bytes 393224 | tf_op jit(solution)/shard_map/ppermute | solution.py:212
  40.9 5.2 %collective-permute-start.16 = (bf16[128,512]{1,0:T(8,128)(2,1)S(1)}, bf16[128,512]{1,0:T(8,128)(2,1)S(1)}, u32[]{:S(2)}, u32[]{:S(2)}) collective-permute-start(bf16[128,512]{1,0:T(8,128)(2,1)S(1)} %add_convert_fusion.refs_3_.own_ref), channel_id=1, source_target_pairs={{0,1},{1,0},{2,3},{3,2},{4,5},{5,4},{6,7},{7,6},{8,9},{9,8},{10,11... | collective-permute-start | bytes 393224 | tf_op jit(solution)/shard_map/ppermute | solution.py:212
  46.1 1.3 %collective-permute-start.18 = (bf16[128,512]{1,0:T(8,128)(2,1)S(1)}, bf16[128,512]{1,0:T(8,128)(2,1)S(1)}, u32[]{:S(2)}, u32[]{:S(2)}) collective-permute-start(bf16[128,512]{1,0:T(8,128)(2,1)S(1)} %collective-permute-done.17.refs_5_), channel_id=1, source_target_pairs={{0,1},{1,0},{2,3},{3,2},{4,5},{5,4},{6,7},{7,6},{8,9},{9,8},{10,11... | collective-permute-start | bytes 393224 | tf_op jit(solution)/shard_map/ppermute | solution.py:212
  46.9 4.7 %collective-permute-start.22 = (bf16[8,128,128]{2,1,0:T(8,128)(2,1)S(1)}, bf16[8,128,128]{2,1,0:T(8,128)(2,1)S(1)}, u32[]{:S(2)}, u32[]{:S(2)}) collective-permute-start(bf16[8,128,128]{2,1,0:T(8,128)(2,1)S(1)} %get-tuple-element.94), channel_id=1, source_target_pairs={{0,1},{1,0},{2,3},{3,2},{4,5},{5,4},{6,7},{7,6},{8,9},{9,8},{10,11... | collective-permute-start | bytes 786440 | tf_op jit(solution)/shard_map/ppermute | solution.py:212
  48.0 10.7 %collective-permute-start.19 = (bf16[128,512]{1,0:T(8,128)(2,1)S(1)}, bf16[128,512]{1,0:T(8,128)(2,1)S(1)}, u32[]{:S(2)}, u32[]{:S(2)}) collective-permute-start(bf16[128,512]{1,0:T(8,128)(2,1)S(1)} %get-tuple-element.88), channel_id=1, source_target_pairs={{0,8},{1,9},{2,10},{3,11},{4,12},{5,13},{6,14},{7,15},{8,0},{9,1},... | collective-permute-start | bytes 393224 | tf_op jit(solution)/shard_map/ppermute | solution.py:212
  48.0 10.7 %collective-permute-start.20 = (bf16[128,512]{1,0:T(8,128)(2,1)S(1)}, bf16[128,512]{1,0:T(8,128)(2,1)S(1)}, u32[]{:S(2)}, u32[]{:S(2)}) collective-permute-start(bf16[128,512]{1,0:T(8,128)(2,1)S(1)} %get-tuple-element.89), channel_id=1, source_target_pairs={{0,12},{1,13},{2,14},{3,15},{4,8},{5,9},{6,10},{7,11},{8,4},{9,5},... | collective-permute-start | bytes 393224 | tf_op jit(solution)/shard_map/ppermute | solution.py:212
  49.3 11.1 %collective-permute-start.21 = (bf16[128,512]{1,0:T(8,128)(2,1)S(1)}, bf16[128,512]{1,0:T(8,128)(2,1)S(1)}, u32[]{:S(2)}, u32[]{:S(2)}) collective-permute-start(bf16[128,512]{1,0:T(8,128)(2,1)S(1)} %get-tuple-element.90), channel_id=1, source_target_pairs={{0,4},{1,5},{2,6},{3,7},{4,0},{5,1},{6,2},{7,3},{8,12},{9,13},{10,... | collective-permute-start | bytes 393224 | tf_op jit(solution)/shard_map/ppermute | solution.py:212

commit v4 on v3

--- a/solution.py
+++ b/solution.py
@@ -299,7 +299,7 @@
         [((width, kv2), f32)] + [((width, kv2), bf16)] * (tall - 1),
         [me, lent, *turned, *grads],
     )
-    order = [*range(tall // 2, tall), *range(1, tall // 2)]
+    order = [tall // 2, *range(1, tall // 2), *range(tall // 2 + 1, tall)]
     received = [swap(terms[delta], 4 * delta) for delta in order]
     near, lent = call(
         input_kernel,

time: 61.3 us -> 60.2 us (0.982)
  waiting for transfers between devices: 24.2 us -> 22.2 us
  starting transfers between devices: 24.7 us -> 25.6 us
    ppermute x20, waiting for transfers between devices: 19.9 us -> 18 us  [swap(): return lax.ppermute(block, 'ctx', [(i, i ^ distance) for i in range(count)])]
    ppermute x20, starting transfers between devices: 16.3 us -> 17.2 us  [swap(): return lax.ppermute(block, 'ctx', [(i, i ^ distance) for i in range(count)])]
where the time goes in v4:
time: 60.2 us; the launch traced here: 60 us
  starting transfers between devices  25.6 us (43%)
  waiting for transfers between devices  22.2 us (37%)
  Pallas kernels  8.59 us (14%)
  local copies, waits for them, and re-layouts  1.96 us (3%)
  other arithmetic  0.85 us (1%)
  between operations  0.82 us (1%)
    ppermute x20, waiting for transfers between devices, swap(): return lax.ppermute(block, 'ctx', [(i, i ^ distance) for i in range(count)])  18 us
    ppermute x20, starting transfers between devices, swap(): return lax.ppermute(block, 'ctx', [(i, i ^ distance) for i in range(count)])  17.2 us
    pallas_call x8, Pallas kernels, call(): pl.pallas_call(kernel, out_shape=[jax.ShapeDtypeStruct(s, d) for s, d in...  8.59 us
    ppermute x2, starting transfers between devices, crossed(): return lax.ppermute(block, 'ctx', route)  6.83 us
    ppermute x2, waiting for transfers between devices, crossed(): return lax.ppermute(block, 'ctx', route)  4.27 us
    unnamed x12, local copies, waits for them, and re-layouts  1.96 us
    ppermute x1, starting transfers between devices, shifted(): lax.ppermute(block, axis, [((i - distance) % count, i) for i in range(cou...  1.55 us
  transfers between devices with their start and end apart: 23, of which 9 were waited for; matrix products, arithmetic and copies ran while one was open for 0% of the time, Pallas kernels for 13%

profile of v4, /device:TPU:0, one launch (start us, length us, event | category | flops | bytes accessed | tf_op | source)
XLA Modules:
  0.0 60.0 jit_solution(17511024108182078627)
XLA Ops:
  0.7 3.1 %collective-permute-start = (bf16[128,512]{1,0:T(8,128)(2,1)}, bf16[128,512]{1,0:T(8,128)(2,1)S(1)}, u32[]{:S(2)}, u32[]{:S(2)}) collective-permute-start(bf16[128,512]{1,0:T(8,128)(2,1)} %bitcast.19), channel_id=1, source_target_pairs={{0,4},{1,5},{2,6},{3,7},{4,0},{5,1},{6,2},{7,3},{8,12},{9,13},{10,... | collective-permute-start | bytes 393224 | tf_op jit(solution)/shard_map/ppermute | solution.py:212
  3.7 2.6 %collective-permute-start.2 = (bf16[128,512]{1,0:T(8,128)(2,1)}, bf16[128,512]{1,0:T(8,128)(2,1)S(1)}, u32[]{:S(2)}, u32[]{:S(2)}) collective-permute-start(bf16[128,512]{1,0:T(8,128)(2,1)} %bitcast.20), channel_id=1, source_target_pairs={{0,8},{1,9},{2,10},{3,11},{4,12},{5,13},{6,14},{7,15},{8,0},{9,1},... | collective-permute-start | bytes 393224 | tf_op jit(solution)/shard_map/ppermute | solution.py:212
  6.3 1.5 %collective-permute-start.3 = (bf16[128,512]{1,0:T(8,128)(2,1)}, bf16[128,512]{1,0:T(8,128)(2,1)S(1)}, u32[]{:S(2)}, u32[]{:S(2)}) collective-permute-start(bf16[128,512]{1,0:T(8,128)(2,1)} %bitcast.21), channel_id=1, source_target_pairs={{0,2},{1,3},{2,0},{3,1},{4,6},{5,7},{6,4},{7,5},{8,10},{9,11},{10,... | collective-permute-start | bytes 393224 | tf_op jit(solution)/shard_map/ppermute | solution.py:212
  7.9 1.0 %copy-done.2 = bf16[1,128,2048]{2,1,0:T(8,128)(2,1)S(1)} copy-done((bf16[1,128,2048]{2,1,0:T(8,128)(2,1)S(1)}, bf16[1,128,2048]{2,1,0:T(8,128)(2,1)}, u32[]{:S(2)}) %copy-start.2) | copy-done | bytes 524312
  8.9 0.9 %copy-done.4 = bf16[1,128,512]{2,1,0:T(8,128)(2,1)S(1)} copy-done((bf16[1,128,512]{2,1,0:T(8,128)(2,1)S(1)}, bf16[1,128,512]{2,1,0:T(8,128)(2,1)}, u32[]{:S(2)}) %copy-start.4) | copy-done | bytes 131096
  9.8 0.4 shard_map.76
  10.3 0.8 %collective-permute-start.4 = (bf16[128,512]{1,0:T(8,128)(2,1)S(1)}, bf16[128,512]{1,0:T(8,128)(2,1)S(1)}, u32[]{:S(2)}, u32[]{:S(2)}) collective-permute-start(bf16[128,512]{1,0:T(8,128)(2,1)S(1)} %collective-permute-done.refs_2_), channel_id=1, source_target_pairs={{0,2},{1,3},{2,0},{3,1},{4,6},{5,7},{6,4},{7,5},{8,10},{9,11},{10,... | collective-permute-start | bytes 393224 | tf_op jit(solution)/shard_map/ppermute | solution.py:212
  11.1 1.6 %collective-permute-done.2.refs_4_ = bf16[128,512]{1,0:T(8,128)(2,1)S(1)} collective-permute-done((bf16[128,512]{1,0:T(8,128)(2,1)}, bf16[128,512]{1,0:T(8,128)(2,1)S(1)}, u32[]{:S(2)}, u32[]{:S(2)}) %collective-permute-start.2) | collective-permute-done | bytes 131104 | tf_op jit(solution)/shard_map/ppermute | solution.py:212
  12.7 1.5 %collective-permute-start.5 = (bf16[128,512]{1,0:T(8,128)(2,1)S(1)}, bf16[128,512]{1,0:T(8,128)(2,1)S(1)}, u32[]{:S(2)}, u32[]{:S(2)}) collective-permute-start(bf16[128,512]{1,0:T(8,128)(2,1)S(1)} %collective-permute-done.2.refs_4_), channel_id=1, source_target_pairs={{0,2},{1,3},{2,0},{3,1},{4,6},{5,7},{6,4},{7,5},{8,10},{9,11},{10,... | collective-permute-start | bytes 393224 | tf_op jit(solution)/shard_map/ppermute | solution.py:212
  14.2 0.4 collective-permute-start.7
  14.6 1.6 %collective-permute-start.6 = (bf16[128,512]{1,0:T(8,128)(2,1)S(1)}, bf16[128,512]{1,0:T(8,128)(2,1)S(1)}, u32[]{:S(2)}, u32[]{:S(2)}) collective-permute-start(bf16[128,512]{1,0:T(8,128)(2,1)S(1)} %collective-permute-done.2.refs_4_), channel_id=1, source_target_pairs={{0,4},{1,5},{2,6},{3,7},{4,0},{5,1},{6,2},{7,3},{8,12},{9,13},{10,... | collective-permute-start | bytes 393224 | tf_op jit(solution)/shard_map/ppermute | solution.py:212
  16.2 1.9 %collective-permute-done.4.refs_3_ = bf16[128,512]{1,0:T(8,128)(2,1)S(1)} collective-permute-done((bf16[128,512]{1,0:T(8,128)(2,1)S(1)}, bf16[128,512]{1,0:T(8,128)(2,1)S(1)}, u32[]{:S(2)}, u32[]{:S(2)}) %collective-permute-start.4) | collective-permute-done | bytes 131104 | tf_op jit(solution)/shard_map/ppermute | solution.py:212
  18.1 3.8 %collective-permute-done.5.refs_5_ = bf16[128,512]{1,0:T(8,128)(2,1)S(1)} collective-permute-done((bf16[128,512]{1,0:T(8,128)(2,1)S(1)}, bf16[128,512]{1,0:T(8,128)(2,1)S(1)}, u32[]{:S(2)}, u32[]{:S(2)}) %collective-permute-start.5) | collective-permute-done | bytes 131104 | tf_op jit(solution)/shard_map/ppermute | solution.py:212
  21.9 0.7 %shard_map.77 = (f32[128,512]{1,0:T(8,128)S(1)}, f32[128,512]{1,0:T(8,128)S(1)}) custom-call(s32[1]{0:T(128)} %bitcast.me_ref, bf16[2,4,128,128]{3,2,1,0:T(8,128)(2,1)S(1)} %get-tuple-element.60.near_ref, bf16[2,4,128,128]{3,2,1,0:T(8,128)(2,1)S(1)} %collective-permute-done.1.lent_ref, bf16[128,512]{1,0:T(8,128)(2,1)S(1)} %get-tuple-element.61.refs_0_, ...), custom_call_target="tpu_custom_call" | custom-call | tf_op jit(solution)/shard_map/pallas_call | solution.py:26
  22.6 1.6 %collective-permute-start.13 = (bf16[1,128,2048]{2,1,0:T(8,128)(2,1)S(1)}, bf16[1,128,2048]{2,1,0:T(8,128)(2,1)S(1)}, u32[]{:S(2)}, u32[]{:S(2)}) collective-permute-start(bf16[1,128,2048]{2,1,0:T(8,128)(2,1)S(1)} %copy-done.5), channel_id=1, source_target_pairs={{16,0},{0,16},{17,1},{1,17},{18,2},{2,18},{19,3},{3,19},{20,4},{4,... | collective-permute-start | bytes 1572872 | tf_op jit(solution)/shard_map/ppermute | solution.py:217
  24.5 3.4 %collective-permute-start.10 = (bf16[128,512]{1,0:T(8,128)(2,1)S(1)}, bf16[128,512]{1,0:T(8,128)(2,1)S(1)}, u32[]{:S(2)}, u32[]{:S(2)}) collective-permute-start(bf16[128,512]{1,0:T(8,128)(2,1)S(1)} %add_convert_fusion.1.own_ref), channel_id=1, source_target_pairs={{0,15},{1,2},{2,1},{3,4},{4,3},{5,6},{6,5},{7,8},{8,7},{9,10},{10,... | collective-permute-start | bytes 393224 | tf_op jit(solution)/shard_map/ppermute | solution.py:223
  27.9 1.0 %shard_map.78 = (f32[8,256,256]{2,1,0:T(8,128)S(1)}, f32[8,256,256]{2,1,0:T(8,128)S(1)}, f32[8,3,256]{2,1,0:T(4,128)S(1)}) custom-call(s32[1]{0:T(128)} %bitcast.me_ref, bf16[128,2048]{1,0:T(8,128)(2,1)S(1)} %bitcast.10, bf16[128,2048]{1,0:T(8,128)(2,1)S(1)} %bitcast.13, bf16[128,512]{1,0:T(8,128)(2,1)S(1)} %collective-permute-done.9.beside_ref, ...), custom_call_target="tpu_custom_call" | custom-call | tf_op jit(solution)/shard_map/pallas_call | solution.py:26
  29.0 2.6 %collective-permute-done.10.across_ref = bf16[128,512]{1,0:T(8,128)(2,1)S(1)} collective-permute-done((bf16[128,512]{1,0:T(8,128)(2,1)S(1)}, bf16[128,512]{1,0:T(8,128)(2,1)S(1)}, u32[]{:S(2)}, u32[]{:S(2)}) %collective-permute-start.10) | collective-permute-done | bytes 131104 | tf_op jit(solution)/shard_map/ppermute | solution.py:223
  31.7 1.9 %shard_map.79 = (bf16[128,512]{1,0:T(8,128)(2,1)S(1)}, bf16[8,128,256]{2,1,0:T(8,128)(2,1)S(1)}, f32[8,2,256]{2,1,0:T(2,128)S(1)}) custom-call(s32[1]{0:T(128)} %bitcast.me_ref, bf16[128,2048]{1,0:T(8,128)(2,1)S(1)} %bitcast.11, bf16[128,2048]{1,0:T(8,128)(2,1)S(1)} %bitcast.14, bf16[128,512]{1,0:T(8,128)(2,1)S(1)} %collective-permute-done.10.across_ref, ...), custom_call_target="tpu_custom_call" | custom-call | tf_op jit(solution)/shard_map/pallas_call | solution.py:26
  33.6 3.5 %collective-permute-start.15 = (bf16[128,512]{1,0:T(8,128)(2,1)S(1)}, bf16[128,512]{1,0:T(8,128)(2,1)S(1)}, u32[]{:S(2)}, u32[]{:S(2)}) collective-permute-start(bf16[128,512]{1,0:T(8,128)(2,1)S(1)} %get-tuple-element.87), channel_id=1, source_target_pairs={{0,15},{1,2},{2,1},{3,4},{4,3},{5,6},{6,5},{7,8},{8,7},{9,10},{10,... | collective-permute-start | bytes 393224 | tf_op jit(solution)/shard_map/ppermute | solution.py:223
  37.1 2.0 %shard_map.80 = (bf16[128,2048]{1,0:T(8,128)(2,1)}, bf16[128,512]{1,0:T(8,128)(2,1)S(1)}, f32[128,512]{1,0:T(8,128)S(1)}) custom-call(bf16[128,2048]{1,0:T(8,128)(2,1)S(1)} %bitcast.12, bf16[128,2048]{1,0:T(8,128)(2,1)S(1)} %bitcast.15, bf16[128,512]{1,0:T(8,128)(2,1)S(1)} %collective-permute-done.9.beside_ref, ...), custom_call_target="tpu_custom_call" | custom-call | tf_op jit(solution)/shard_map/pallas_call | solution.py:26
  39.1 1.6 %collective-permute-done.15 = bf16[128,512]{1,0:T(8,128)(2,1)S(1)} collective-permute-done((bf16[128,512]{1,0:T(8,128)(2,1)S(1)}, bf16[128,512]{1,0:T(8,128)(2,1)S(1)}, u32[]{:S(2)}, u32[]{:S(2)}) %collective-permute-start.15) | collective-permute-done | bytes 131104 | tf_op jit(solution)/shard_map/ppermute | solution.py:223
  41.0 5.2 %collective-permute-done.17.refs_5_ = bf16[128,512]{1,0:T(8,128)(2,1)S(1)} collective-permute-done((bf16[128,512]{1,0:T(8,128)(2,1)S(1)}, bf16[128,512]{1,0:T(8,128)(2,1)S(1)}, u32[]{:S(2)}, u32[]{:S(2)}) %collective-permute-start.17) | collective-permute-done | bytes 131104 | tf_op jit(solution)/shard_map/ppermute | solution.py:212
  46.1 0.7 %shard_map.82 = (f32[8,128,128]{2,1,0:T(8,128)S(1)}, bf16[8,128,128]{2,1,0:T(8,128)(2,1)S(1)}) custom-call(bf16[128,512]{1,0:T(8,128)(2,1)S(1)} %add_convert_fusion.refs_3_.own_ref, bf16[128,512]{1,0:T(8,128)(2,1)S(1)} %collective-permute-done.16.refs_4_.beside_ref, bf16[128,512]{1,0:T(8,128)(2,1)S(1)} %get-tuple-element.61.refs_0_, ...), custom_call_target="tpu_custom_call" | custom-call | tf_op jit(solution)/shard_map/pallas_call | solution.py:26
  46.9 0.6 collective-permute-start.22
  47.5 0.5 shard_map.81
  48.0 1.5 %collective-permute-start.20 = (bf16[128,512]{1,0:T(8,128)(2,1)S(1)}, bf16[128,512]{1,0:T(8,128)(2,1)S(1)}, u32[]{:S(2)}, u32[]{:S(2)}) collective-permute-start(bf16[128,512]{1,0:T(8,128)(2,1)S(1)} %get-tuple-element.89), channel_id=1, source_target_pairs={{0,4},{1,5},{2,6},{3,7},{4,0},{5,1},{6,2},{7,3},{8,12},{9,13},{10,... | collective-permute-start | bytes 393224 | tf_op jit(solution)/shard_map/ppermute | solution.py:212
  49.5 2.9 %collective-permute-start.21 = (bf16[128,512]{1,0:T(8,128)(2,1)S(1)}, bf16[128,512]{1,0:T(8,128)(2,1)S(1)}, u32[]{:S(2)}, u32[]{:S(2)}) collective-permute-start(bf16[128,512]{1,0:T(8,128)(2,1)S(1)} %get-tuple-element.90), channel_id=1, source_target_pairs={{0,12},{1,13},{2,14},{3,15},{4,8},{5,9},{6,10},{7,11},{8,4},{9,5},... | collective-permute-start | bytes 393224 | tf_op jit(solution)/shard_map/ppermute | solution.py:212
  52.4 1.4 %shard_map.83 = bf16[128,2048]{1,0:T(8,128)(2,1)} custom-call(s32[1]{0:T(128)} %bitcast.me_ref, bf16[128,2048]{1,0:T(8,128)(2,1)S(1)} %bitcast.17, f32[128,1]{1,0:T(8,128)S(1)} %get-tuple-element.91.factor_ref, bf16[128,2048]{1,0:T(8,128)(2,1)S(1)} %bitcast.18, f32[8,128,128]{2,1,0:T(8,128)S(1)} %get-tuple-element.93.near_ref, ...), custom_call_target="tpu_custom_call" | custom-call | tf_op jit(solution)/shard_map/pallas_call | solution.py:26
  53.8 4.9 %collective-permute-done.19 = bf16[128,512]{1,0:T(8,128)(2,1)S(1)} collective-permute-done((bf16[128,512]{1,0:T(8,128)(2,1)S(1)}, bf16[128,512]{1,0:T(8,128)(2,1)S(1)}, u32[]{:S(2)}, u32[]{:S(2)}) %collective-permute-start.19) | collective-permute-done | bytes 131104 | tf_op jit(solution)/shard_map/ppermute | solution.py:212
  58.7 0.5 collective-permute-done.20
  59.3 0.8 %multiply_bitcast_fusion = f32[1,128,512]{2,1,0:T(8,128)} fusion(bf16[128,512]{1,0:T(8,128)(2,1)S(1)} %collective-permute-done.21, bf16[128,512]{1,0:T(8,128)(2,1)S(1)} %collective-permute-done.20, f32[128,512]{1,0:T(8,128)S(1)} %get-tuple-element.97, bf16[128,512]{1,0:T(8,128)(2,1)S(1)} %collective-permute-done.19), kind=kLoop, calls=%fused_computation | loop fusion | flops 458752 | bytes 917504 | tf_op jit(solution)/shard_map/broadcast_in_dim | solution.py:320
  (37 shorter events, 1.0 us)
Async XLA Ops:
  0.6 27.2 %copy-start = (bf16[1,128,2048]{2,1,0:T(8,128)(2,1)S(1)}, bf16[1,128,2048]{2,1,0:T(8,128)(2,1)}, u32[]{:S(2)}) copy-start(bf16[1,128,2048]{2,1,0:T(8,128)(2,1)} %param.7) | copy-start | bytes 1572868
  0.6 27.2 %copy-start.1 = (bf16[1,128,2048]{2,1,0:T(8,128)(2,1)S(1)}, bf16[1,128,2048]{2,1,0:T(8,128)(2,1)}, u32[]{:S(2)}) copy-start(bf16[1,128,2048]{2,1,0:T(8,128)(2,1)} %param.8) | copy-start | bytes 1572868
  0.7 9.6 %collective-permute-start = (bf16[128,512]{1,0:T(8,128)(2,1)}, bf16[128,512]{1,0:T(8,128)(2,1)S(1)}, u32[]{:S(2)}, u32[]{:S(2)}) collective-permute-start(bf16[128,512]{1,0:T(8,128)(2,1)} %bitcast.19), channel_id=1, source_target_pairs={{0,4},{1,5},{2,6},{3,7},{4,0},{5,1},{6,2},{7,3},{8,12},{9,13},{10,... | collective-permute-start | bytes 393224 | tf_op jit(solution)/shard_map/ppermute | solution.py:212
  3.7 8.9 %collective-permute-start.2 = (bf16[128,512]{1,0:T(8,128)(2,1)}, bf16[128,512]{1,0:T(8,128)(2,1)S(1)}, u32[]{:S(2)}, u32[]{:S(2)}) collective-permute-start(bf16[128,512]{1,0:T(8,128)(2,1)} %bitcast.20), channel_id=1, source_target_pairs={{0,8},{1,9},{2,10},{3,11},{4,12},{5,13},{6,14},{7,15},{8,0},{9,1},... | collective-permute-start | bytes 393224 | tf_op jit(solution)/shard_map/ppermute | solution.py:212
  6.3 6.4 %collective-permute-start.3 = (bf16[128,512]{1,0:T(8,128)(2,1)}, bf16[128,512]{1,0:T(8,128)(2,1)S(1)}, u32[]{:S(2)}, u32[]{:S(2)}) collective-permute-start(bf16[128,512]{1,0:T(8,128)(2,1)} %bitcast.21), channel_id=1, source_target_pairs={{0,2},{1,3},{2,0},{3,1},{4,6},{5,7},{6,4},{7,5},{8,10},{9,11},{10,... | collective-permute-start | bytes 393224 | tf_op jit(solution)/shard_map/ppermute | solution.py:212
  7.8 1.0 %copy-start.2 = (bf16[1,128,2048]{2,1,0:T(8,128)(2,1)S(1)}, bf16[1,128,2048]{2,1,0:T(8,128)(2,1)}, u32[]{:S(2)}) copy-start(bf16[1,128,2048]{2,1,0:T(8,128)(2,1)} %param.5) | copy-start | bytes 1572868
  8.9 0.9 %copy-start.4 = (bf16[1,128,512]{2,1,0:T(8,128)(2,1)S(1)}, bf16[1,128,512]{2,1,0:T(8,128)(2,1)}, u32[]{:S(2)}) copy-start(bf16[1,128,512]{2,1,0:T(8,128)(2,1)} %param.9) | copy-start | bytes 393220
  9.8 12.8 %copy-start.5 = (bf16[1,128,2048]{2,1,0:T(8,128)(2,1)S(1)}, bf16[1,128,2048]{2,1,0:T(8,128)(2,1)}, u32[]{:S(2)}) copy-start(bf16[1,128,2048]{2,1,0:T(8,128)(2,1)} %param.6) | copy-start | bytes 1572868
  10.2 11.6 %collective-permute-start.1 = (bf16[2,4,128,128]{3,2,1,0:T(8,128)(2,1)S(1)}, bf16[2,4,128,128]{3,2,1,0:T(8,128)(2,1)S(1)}, u32[]{:S(2)}, u32[]{:S(2)}) collective-permute-start(bf16[2,4,128,128]{3,2,1,0:T(8,128)(2,1)S(1)} %get-tuple-element.59), channel_id=1, source_target_pairs={{0,1},{1,0},{2,3},{3,2},{4,5},{5,4},{6,7},{7,6},{8,9},{9,8},{10,11... | collective-permute-start | bytes 786440 | tf_op jit(solution)/shard_map/ppermute | solution.py:212
  10.3 7.8 %collective-permute-start.4 = (bf16[128,512]{1,0:T(8,128)(2,1)S(1)}, bf16[128,512]{1,0:T(8,128)(2,1)S(1)}, u32[]{:S(2)}, u32[]{:S(2)}) collective-permute-start(bf16[128,512]{1,0:T(8,128)(2,1)S(1)} %collective-permute-done.refs_2_), channel_id=1, source_target_pairs={{0,2},{1,3},{2,0},{3,1},{4,6},{5,7},{6,4},{7,5},{8,10},{9,11},{10,... | collective-permute-start | bytes 393224 | tf_op jit(solution)/shard_map/ppermute | solution.py:212
  12.7 9.2 %collective-permute-start.5 = (bf16[128,512]{1,0:T(8,128)(2,1)S(1)}, bf16[128,512]{1,0:T(8,128)(2,1)S(1)}, u32[]{:S(2)}, u32[]{:S(2)}) collective-permute-start(bf16[128,512]{1,0:T(8,128)(2,1)S(1)} %collective-permute-done.2.refs_4_), channel_id=1, source_target_pairs={{0,2},{1,3},{2,0},{3,1},{4,6},{5,7},{6,4},{7,5},{8,10},{9,11},{10,... | collective-permute-start | bytes 393224 | tf_op jit(solution)/shard_map/ppermute | solution.py:212
  14.2 7.6 %collective-permute-start.7 = (bf16[128,512]{1,0:T(8,128)(2,1)S(1)}, bf16[128,512]{1,0:T(8,128)(2,1)S(1)}, u32[]{:S(2)}, u32[]{:S(2)}) collective-permute-start(bf16[128,512]{1,0:T(8,128)(2,1)S(1)} %collective-permute-done.2.refs_4_), channel_id=1, source_target_pairs={{0,6},{1,7},{2,4},{3,5},{4,2},{5,3},{6,0},{7,1},{8,14},{9,15},{10,... | collective-permute-start | bytes 393224 | tf_op jit(solution)/shard_map/ppermute | solution.py:212
  14.6 7.3 %collective-permute-start.6 = (bf16[128,512]{1,0:T(8,128)(2,1)S(1)}, bf16[128,512]{1,0:T(8,128)(2,1)S(1)}, u32[]{:S(2)}, u32[]{:S(2)}) collective-permute-start(bf16[128,512]{1,0:T(8,128)(2,1)S(1)} %collective-permute-done.2.refs_4_), channel_id=1, source_target_pairs={{0,4},{1,5},{2,6},{3,7},{4,0},{5,1},{6,2},{7,3},{8,12},{9,13},{10,... | collective-permute-start | bytes 393224 | tf_op jit(solution)/shard_map/ppermute | solution.py:212
  22.6 1.6 %collective-permute-start.8 = (f32[128,512]{1,0:T(8,128)S(1)}, f32[128,512]{1,0:T(8,128)S(1)}, u32[]{:S(2)}, u32[]{:S(2)}) collective-permute-start(f32[128,512]{1,0:T(8,128)S(1)} %get-tuple-element.67), channel_id=1, source_target_pairs={{0,1},{1,0},{2,3},{3,2},{4,5},{5,4},{6,7},{7,6},{8,9},{9,8},{10,11... | collective-permute-start | bytes 786440 | tf_op jit(solution)/shard_map/ppermute | solution.py:212
  22.6 16.4 %collective-permute-start.13 = (bf16[1,128,2048]{2,1,0:T(8,128)(2,1)S(1)}, bf16[1,128,2048]{2,1,0:T(8,128)(2,1)S(1)}, u32[]{:S(2)}, u32[]{:S(2)}) collective-permute-start(bf16[1,128,2048]{2,1,0:T(8,128)(2,1)S(1)} %copy-done.5), channel_id=1, source_target_pairs={{16,0},{0,16},{17,1},{1,17},{18,2},{2,18},{19,3},{3,19},{20,4},{4,... | collective-permute-start | bytes 1572872 | tf_op jit(solution)/shard_map/ppermute | solution.py:217
  24.2 3.6 %collective-permute-start.9 = (bf16[128,512]{1,0:T(8,128)(2,1)S(1)}, bf16[128,512]{1,0:T(8,128)(2,1)S(1)}, u32[]{:S(2)}, u32[]{:S(2)}) collective-permute-start(bf16[128,512]{1,0:T(8,128)(2,1)S(1)} %add_convert_fusion.1.own_ref), channel_id=1, source_target_pairs={{0,1},{1,0},{2,3},{3,2},{4,5},{5,4},{6,7},{7,6},{8,9},{9,8},{10,11... | collective-permute-start | bytes 393224 | tf_op jit(solution)/shard_map/ppermute | solution.py:212
  24.5 7.2 %collective-permute-start.10 = (bf16[128,512]{1,0:T(8,128)(2,1)S(1)}, bf16[128,512]{1,0:T(8,128)(2,1)S(1)}, u32[]{:S(2)}, u32[]{:S(2)}) collective-permute-start(bf16[128,512]{1,0:T(8,128)(2,1)S(1)} %add_convert_fusion.1.own_ref), channel_id=1, source_target_pairs={{0,15},{1,2},{2,1},{3,4},{4,3},{5,6},{6,5},{7,8},{8,7},{9,10},{10,... | collective-permute-start | bytes 393224 | tf_op jit(solution)/shard_map/ppermute | solution.py:223
  28.9 10.2 %collective-permute-start.11 = (bf16[4,128,128]{2,1,0:T(8,128)(2,1)S(1)}, bf16[4,128,128]{2,1,0:T(8,128)(2,1)S(1)}, u32[]{:S(2)}, u32[]{:S(2)}) collective-permute-start(bf16[4,128,128]{2,1,0:T(8,128)(2,1)S(1)} %get-tuple-element.79), channel_id=1, source_target_pairs={{0,2},{1,3},{2,0},{3,1},{4,6},{5,7},{6,4},{7,5},{8,10},{9,11},{10,... | collective-permute-start | bytes 393224 | tf_op jit(solution)/shard_map/ppermute | solution.py:212
  28.9 10.1 %collective-permute-start.12 = (bf16[4,128,128]{2,1,0:T(8,128)(2,1)S(1)}, bf16[4,128,128]{2,1,0:T(8,128)(2,1)S(1)}, u32[]{:S(2)}, u32[]{:S(2)}) collective-permute-start(bf16[4,128,128]{2,1,0:T(8,128)(2,1)S(1)} %get-tuple-element.80), channel_id=1, source_target_pairs={{0,3},{1,2},{2,1},{3,0},{4,7},{5,6},{6,5},{7,4},{8,11},{9,10},{10,... | collective-permute-start | bytes 393224 | tf_op jit(solution)/shard_map/ppermute | solution.py:212
  33.6 7.2 %collective-permute-start.15 = (bf16[128,512]{1,0:T(8,128)(2,1)S(1)}, bf16[128,512]{1,0:T(8,128)(2,1)S(1)}, u32[]{:S(2)}, u32[]{:S(2)}) collective-permute-start(bf16[128,512]{1,0:T(8,128)(2,1)S(1)} %get-tuple-element.87), channel_id=1, source_target_pairs={{0,15},{1,2},{2,1},{3,4},{4,3},{5,6},{6,5},{7,8},{8,7},{9,10},{10,... | collective-permute-start | bytes 393224 | tf_op jit(solution)/shard_map/ppermute | solution.py:223
  39.0 13.4 %copy-start.3 = (bf16[1,128,2048]{2,1,0:T(8,128)(2,1)S(1)}, bf16[1,128,2048]{2,1,0:T(8,128)(2,1)}, u32[]{:S(2)}) copy-start(bf16[1,128,2048]{2,1,0:T(8,128)(2,1)} %param.5) | copy-start | bytes 1572868
  39.1 1.7 %collective-permute-start.14 = (bf16[128,512]{1,0:T(8,128)(2,1)S(1)}, bf16[128,512]{1,0:T(8,128)(2,1)S(1)}, u32[]{:S(2)}, u32[]{:S(2)}) collective-permute-start(bf16[128,512]{1,0:T(8,128)(2,1)S(1)} %get-tuple-element.86), channel_id=1, source_target_pairs={{0,1},{1,0},{2,3},{3,2},{4,5},{5,4},{6,7},{7,6},{8,9},{9,8},{10,11... | collective-permute-start | bytes 393224 | tf_op jit(solution)/shard_map/ppermute | solution.py:212
  40.8 5.3 %collective-permute-start.17 = (bf16[128,512]{1,0:T(8,128)(2,1)S(1)}, bf16[128,512]{1,0:T(8,128)(2,1)S(1)}, u32[]{:S(2)}, u32[]{:S(2)}) collective-permute-start(bf16[128,512]{1,0:T(8,128)(2,1)S(1)} %add_convert_fusion.refs_3_.own_ref), channel_id=1, source_target_pairs={{0,2},{1,3},{2,0},{3,1},{4,6},{5,7},{6,4},{7,5},{8,10},{9,11},{10,... | collective-permute-start | bytes 393224 | tf_op jit(solution)/shard_map/ppermute | solution.py:212
  40.9 5.2 %collective-permute-start.16 = (bf16[128,512]{1,0:T(8,128)(2,1)S(1)}, bf16[128,512]{1,0:T(8,128)(2,1)S(1)}, u32[]{:S(2)}, u32[]{:S(2)}) collective-permute-start(bf16[128,512]{1,0:T(8,128)(2,1)S(1)} %add_convert_fusion.refs_3_.own_ref), channel_id=1, source_target_pairs={{0,1},{1,0},{2,3},{3,2},{4,5},{5,4},{6,7},{7,6},{8,9},{9,8},{10,11... | collective-permute-start | bytes 393224 | tf_op jit(solution)/shard_map/ppermute | solution.py:212
  46.1 1.3 %collective-permute-start.18 = (bf16[128,512]{1,0:T(8,128)(2,1)S(1)}, bf16[128,512]{1,0:T(8,128)(2,1)S(1)}, u32[]{:S(2)}, u32[]{:S(2)}) collective-permute-start(bf16[128,512]{1,0:T(8,128)(2,1)S(1)} %collective-permute-done.17.refs_5_), channel_id=1, source_target_pairs={{0,1},{1,0},{2,3},{3,2},{4,5},{5,4},{6,7},{7,6},{8,9},{9,8},{10,11... | collective-permute-start | bytes 393224 | tf_op jit(solution)/shard_map/ppermute | solution.py:212
  46.9 5.6 %collective-permute-start.22 = (bf16[8,128,128]{2,1,0:T(8,128)(2,1)S(1)}, bf16[8,128,128]{2,1,0:T(8,128)(2,1)S(1)}, u32[]{:S(2)}, u32[]{:S(2)}) collective-permute-start(bf16[8,128,128]{2,1,0:T(8,128)(2,1)S(1)} %get-tuple-element.94), channel_id=1, source_target_pairs={{0,1},{1,0},{2,3},{3,2},{4,5},{5,4},{6,7},{7,6},{8,9},{9,8},{10,11... | collective-permute-start | bytes 786440 | tf_op jit(solution)/shard_map/ppermute | solution.py:212
  48.0 10.8 %collective-permute-start.19 = (bf16[128,512]{1,0:T(8,128)(2,1)S(1)}, bf16[128,512]{1,0:T(8,128)(2,1)S(1)}, u32[]{:S(2)}, u32[]{:S(2)}) collective-permute-start(bf16[128,512]{1,0:T(8,128)(2,1)S(1)} %get-tuple-element.88), channel_id=1, source_target_pairs={{0,8},{1,9},{2,10},{3,11},{4,12},{5,13},{6,14},{7,15},{8,0},{9,1},... | collective-permute-start | bytes 393224 | tf_op jit(solution)/shard_map/ppermute | solution.py:212
  48.0 11.2 %collective-permute-start.20 = (bf16[128,512]{1,0:T(8,128)(2,1)S(1)}, bf16[128,512]{1,0:T(8,128)(2,1)S(1)}, u32[]{:S(2)}, u32[]{:S(2)}) collective-permute-start(bf16[128,512]{1,0:T(8,128)(2,1)S(1)} %get-tuple-element.89), channel_id=1, source_target_pairs={{0,4},{1,5},{2,6},{3,7},{4,0},{5,1},{6,2},{7,3},{8,12},{9,13},{10,... | collective-permute-start | bytes 393224 | tf_op jit(solution)/shard_map/ppermute | solution.py:212
  49.5 9.8 %collective-permute-start.21 = (bf16[128,512]{1,0:T(8,128)(2,1)S(1)}, bf16[128,512]{1,0:T(8,128)(2,1)S(1)}, u32[]{:S(2)}, u32[]{:S(2)}) collective-permute-start(bf16[128,512]{1,0:T(8,128)(2,1)S(1)} %get-tuple-element.90), channel_id=1, source_target_pairs={{0,12},{1,13},{2,14},{3,15},{4,8},{5,9},{6,10},{7,11},{8,4},{9,5},... | collective-permute-start | bytes 393224 | tf_op jit(solution)/shard_map/ppermute | solution.py:212

commit v5 on v4

--- a/solution.py
+++ b/solution.py
@@ -9,6 +9,7 @@
 from jax.sharding import PartitionSpec as P
 
 HEAD_DIM = 128
+BATCH = 8
 KV_HEADS = 2
 EPSILON = 1e-06
 NT = (((1,), (1,)), ((), ()))
@@ -67,17 +68,16 @@
     beside_ref[...] = total[rows:]
 
 
-def head_pair(ref, pair):
-    at = 2 * pair * HEAD_DIM
-    first, second = ref[:, at : at + HEAD_DIM], ref[:, at + HEAD_DIM : at + 2 * HEAD_DIM]
-    return jnp.concatenate([first, second], axis=0)
+def head_rows(ref, block, size):
+    at = block * size * HEAD_DIM
+    return jnp.concatenate([ref[:, at + h * HEAD_DIM : at + (h + 1) * HEAD_DIM] for h in range(size)], axis=0)
 
 
 def reach(me_ref, rows, near):
     key_pos = lax.broadcasted_iota(jnp.int32, (rows, rows), 0)
     query_pos = lax.broadcasted_iota(jnp.int32, (rows, rows), 1)
     offset = (key_pos - query_pos) * (1 - 2 * (me_ref[0] % 2))
-    return jnp.concatenate([offset <= 0 if near else offset >= 0] * 2, axis=1)
+    return jnp.concatenate([offset <= 0 if near else offset >= 0] * BATCH, axis=1)
 
 
 def columns(group):
@@ -95,11 +95,11 @@
         keys = jnp.concatenate([beside_ref[:, key_at], own_ref[:, key_at]], axis=0)
         values = jnp.concatenate([beside_ref[:, value_at], own_ref[:, value_at]], axis=0)
         for pair in range(group * pairs // KV_HEADS, (group + 1) * pairs // KV_HEADS):
-            scores = f32dot(keys, head_pair(q_ref, pair), NT) * scale
+            scores = f32dot(keys, head_rows(q_ref, pair, BATCH), NT) * scale
             scores = jnp.concatenate([jnp.where(mask, scores[:rows], -1e30), scores[rows:]], axis=0)
             peak = jnp.max(scores, axis=0, keepdims=True)
             lifted = jnp.exp2(scores - peak)
-            weighted = lifted * f32dot(values, head_pair(g_ref, pair), NT)
+            weighted = lifted * f32dot(values, head_rows(g_ref, pair, BATCH), NT)
             lifted_ref[pair] = lifted
             weighted_ref[pair] = weighted
             stats_ref[pair, 0:1] = peak
@@ -117,7 +117,7 @@
         keys, values = across_ref[:, key_at], across_ref[:, value_at]
         d_keys = d_values = None
         for pair in range(group * pairs // KV_HEADS, (group + 1) * pairs // KV_HEADS):
-            q, g = head_pair(q_ref, pair), head_pair(g_ref, pair)
+            q, g = head_rows(q_ref, pair, BATCH), head_rows(g_ref, pair, BATCH)
             scores = f32dot(keys, q, NT) * (scale * math.log2(math.e))
             scores = jnp.where(mask, scores, -1e30)
             near_peak = stats_ref[pair, 0:1]
@@ -155,14 +155,14 @@
             d_scores = (weighted_ref[pair] - lifted * rest_ref[pair, 1:2]) * (part * scale)
             d_scores = d_scores.astype(jnp.bfloat16)
             probs = (lifted * part).astype(jnp.bfloat16)
-            dk = f32dot(d_scores, head_pair(q_ref, pair))
-            dv = f32dot(probs, head_pair(g_ref, pair))
+            dk = f32dot(d_scores, head_rows(q_ref, pair, BATCH))
+            dv = f32dot(probs, head_rows(g_ref, pair, BATCH))
             d_keys = dk if d_keys is None else d_keys + dk
             d_values = dv if d_values is None else d_values + dv
             dq = f32dot(keys, jnp.concatenate([d_scores, far_ref[pair]], axis=0)).astype(jnp.bfloat16)
-            at = 2 * pair * HEAD_DIM
-            dq_ref[:, at : at + HEAD_DIM] = dq[:, :rows].T
-            dq_ref[:, at + HEAD_DIM : at + 2 * HEAD_DIM] = dq[:, rows:].T
+            for h in range(BATCH):
+                at = (BATCH * pair + h) * HEAD_DIM
+                dq_ref[:, at : at + HEAD_DIM] = dq[:, h * rows : (h + 1) * rows].T
         for at, grad in ((key_at, d_keys), (value_at, d_values)):
             db_ref[:, at] = grad[:rows].astype(jnp.bfloat16)
             do_ref[:, at] = grad[rows:]
@@ -268,18 +268,18 @@
     kv = (kv + swap(kv_lent, 1)).astype(bf16)
     across = crossed(kv)
     beside = swap(kv, 1)
-    pairs = model // (2 * HEAD_DIM)
-    block = ((pairs, 2 * rows, 2 * rows), f32)
+    pairs = model // (BATCH * HEAD_DIM)
+    block = ((pairs, 2 * rows, BATCH * rows), f32)
     lifted, weighted, stats = call(
         near_kernel,
-        [block, block, ((pairs, 3, 2 * rows), f32)],
+        [block, block, ((pairs, 3, BATCH * rows), f32)],
         [me, queries[0], d_heads[0], beside, kv],
     )
     stats, turned = lax.optimization_barrier((stats, turned))
     turned = [turned[0], swap(turned[1], 2), swap(turned[2], 3)]
     d_across, far, kept = call(
         far_kernel,
-        [half, ((pairs, rows, 2 * rows), bf16), ((pairs, 2, 2 * rows), f32)],
+        [half, ((pairs, rows, BATCH * rows), bf16), ((pairs, 2, BATCH * rows), f32)],
         [me, queries[0], d_heads[0], across, stats],
     )
     from_across = crossed(d_across)

time: 60.2 us -> 60.1 us (level)
  Pallas kernels: 8.59 us -> 7.74 us
    pallas_call x8, Pallas kernels: 8.59 us -> 7.74 us  [call(): pl.pallas_call(kernel, out_shape=[jax.ShapeDtypeStruct(s, d) for s, d in...]
  transfers between devices with their start and end apart: 23 -> 23, of which waited for: 9 -> 9; matrix products, arithmetic and copies ran while one was open for 0% -> 0% of each run, Pallas kernels for 13% -> 12%
where the time goes in v5:
time: 60.1 us; the launch traced here: 59.6 us
  starting transfers between devices  25.6 us (43%)
  waiting for transfers between devices  22.6 us (38%)
  Pallas kernels  7.74 us (13%)
  local copies, waits for them, and re-layouts  1.96 us (3%)
  other arithmetic  0.85 us (1%)
  between operations  0.81 us (1%)
    ppermute x20, waiting for transfers between devices, swap(): return lax.ppermute(block, 'ctx', [(i, i ^ distance) for i in range(count)])  18.3 us
    ppermute x20, starting transfers between devices, swap(): return lax.ppermute(block, 'ctx', [(i, i ^ distance) for i in range(count)])  17.2 us
    pallas_call x8, Pallas kernels, call(): pl.pallas_call(kernel, out_shape=[jax.ShapeDtypeStruct(s, d) for s, d in...  7.74 us
    ppermute x2, starting transfers between devices, crossed(): return lax.ppermute(block, 'ctx', route)  6.82 us
    ppermute x2, waiting for transfers between devices, crossed(): return lax.ppermute(block, 'ctx', route)  4.35 us
    unnamed x12, local copies, waits for them, and re-layouts  1.96 us
    ppermute x1, starting transfers between devices, shifted(): lax.ppermute(block, axis, [((i - distance) % count, i) for i in range(cou...  1.55 us
  transfers between devices with their start and end apart: 23, of which 9 were waited for; matrix products, arithmetic and copies ran while one was open for 0% of the time, Pallas kernels for 12%

profile of v5, /device:TPU:0, one launch (start us, length us, event | category | flops | bytes accessed | tf_op | source)
XLA Modules:
  0.0 59.6 jit_solution(17367148935335566554)
XLA Ops:
  0.7 3.1 %collective-permute-start = (bf16[128,512]{1,0:T(8,128)(2,1)}, bf16[128,512]{1,0:T(8,128)(2,1)S(1)}, u32[]{:S(2)}, u32[]{:S(2)}) collective-permute-start(bf16[128,512]{1,0:T(8,128)(2,1)} %bitcast.19), channel_id=1, source_target_pairs={{0,4},{1,5},{2,6},{3,7},{4,0},{5,1},{6,2},{7,3},{8,12},{9,13},{10,... | collective-permute-start | bytes 393224 | tf_op jit(solution)/shard_map/ppermute | solution.py:212
  3.7 2.6 %collective-permute-start.2 = (bf16[128,512]{1,0:T(8,128)(2,1)}, bf16[128,512]{1,0:T(8,128)(2,1)S(1)}, u32[]{:S(2)}, u32[]{:S(2)}) collective-permute-start(bf16[128,512]{1,0:T(8,128)(2,1)} %bitcast.20), channel_id=1, source_target_pairs={{0,8},{1,9},{2,10},{3,11},{4,12},{5,13},{6,14},{7,15},{8,0},{9,1},... | collective-permute-start | bytes 393224 | tf_op jit(solution)/shard_map/ppermute | solution.py:212
  6.3 1.5 %collective-permute-start.3 = (bf16[128,512]{1,0:T(8,128)(2,1)}, bf16[128,512]{1,0:T(8,128)(2,1)S(1)}, u32[]{:S(2)}, u32[]{:S(2)}) collective-permute-start(bf16[128,512]{1,0:T(8,128)(2,1)} %bitcast.21), channel_id=1, source_target_pairs={{0,2},{1,3},{2,0},{3,1},{4,6},{5,7},{6,4},{7,5},{8,10},{9,11},{10,... | collective-permute-start | bytes 393224 | tf_op jit(solution)/shard_map/ppermute | solution.py:212
  7.9 1.0 %copy-done.2 = bf16[1,128,2048]{2,1,0:T(8,128)(2,1)S(1)} copy-done((bf16[1,128,2048]{2,1,0:T(8,128)(2,1)S(1)}, bf16[1,128,2048]{2,1,0:T(8,128)(2,1)}, u32[]{:S(2)}) %copy-start.2) | copy-done | bytes 524312
  8.9 0.9 %copy-done.4 = bf16[1,128,512]{2,1,0:T(8,128)(2,1)S(1)} copy-done((bf16[1,128,512]{2,1,0:T(8,128)(2,1)S(1)}, bf16[1,128,512]{2,1,0:T(8,128)(2,1)}, u32[]{:S(2)}) %copy-start.4) | copy-done | bytes 131096
  9.8 0.4 shard_map.76
  10.3 0.8 %collective-permute-start.4 = (bf16[128,512]{1,0:T(8,128)(2,1)S(1)}, bf16[128,512]{1,0:T(8,128)(2,1)S(1)}, u32[]{:S(2)}, u32[]{:S(2)}) collective-permute-start(bf16[128,512]{1,0:T(8,128)(2,1)S(1)} %collective-permute-done.refs_2_), channel_id=1, source_target_pairs={{0,2},{1,3},{2,0},{3,1},{4,6},{5,7},{6,4},{7,5},{8,10},{9,11},{10,... | collective-permute-start | bytes 393224 | tf_op jit(solution)/shard_map/ppermute | solution.py:212
  11.1 1.6 %collective-permute-done.2.refs_4_ = bf16[128,512]{1,0:T(8,128)(2,1)S(1)} collective-permute-done((bf16[128,512]{1,0:T(8,128)(2,1)}, bf16[128,512]{1,0:T(8,128)(2,1)S(1)}, u32[]{:S(2)}, u32[]{:S(2)}) %collective-permute-start.2) | collective-permute-done | bytes 131104 | tf_op jit(solution)/shard_map/ppermute | solution.py:212
  12.7 1.5 %collective-permute-start.5 = (bf16[128,512]{1,0:T(8,128)(2,1)S(1)}, bf16[128,512]{1,0:T(8,128)(2,1)S(1)}, u32[]{:S(2)}, u32[]{:S(2)}) collective-permute-start(bf16[128,512]{1,0:T(8,128)(2,1)S(1)} %collective-permute-done.2.refs_4_), channel_id=1, source_target_pairs={{0,2},{1,3},{2,0},{3,1},{4,6},{5,7},{6,4},{7,5},{8,10},{9,11},{10,... | collective-permute-start | bytes 393224 | tf_op jit(solution)/shard_map/ppermute | solution.py:212
  14.2 0.4 collective-permute-start.7
  14.6 1.6 %collective-permute-start.6 = (bf16[128,512]{1,0:T(8,128)(2,1)S(1)}, bf16[128,512]{1,0:T(8,128)(2,1)S(1)}, u32[]{:S(2)}, u32[]{:S(2)}) collective-permute-start(bf16[128,512]{1,0:T(8,128)(2,1)S(1)} %collective-permute-done.2.refs_4_), channel_id=1, source_target_pairs={{0,4},{1,5},{2,6},{3,7},{4,0},{5,1},{6,2},{7,3},{8,12},{9,13},{10,... | collective-permute-start | bytes 393224 | tf_op jit(solution)/shard_map/ppermute | solution.py:212
  16.2 1.9 %collective-permute-done.4.refs_3_ = bf16[128,512]{1,0:T(8,128)(2,1)S(1)} collective-permute-done((bf16[128,512]{1,0:T(8,128)(2,1)S(1)}, bf16[128,512]{1,0:T(8,128)(2,1)S(1)}, u32[]{:S(2)}, u32[]{:S(2)}) %collective-permute-start.4) | collective-permute-done | bytes 131104 | tf_op jit(solution)/shard_map/ppermute | solution.py:212
  18.1 3.8 %collective-permute-done.5.refs_5_ = bf16[128,512]{1,0:T(8,128)(2,1)S(1)} collective-permute-done((bf16[128,512]{1,0:T(8,128)(2,1)S(1)}, bf16[128,512]{1,0:T(8,128)(2,1)S(1)}, u32[]{:S(2)}, u32[]{:S(2)}) %collective-permute-start.5) | collective-permute-done | bytes 131104 | tf_op jit(solution)/shard_map/ppermute | solution.py:212
  21.9 0.7 %shard_map.77 = (f32[128,512]{1,0:T(8,128)S(1)}, f32[128,512]{1,0:T(8,128)S(1)}) custom-call(s32[1]{0:T(128)} %bitcast.me_ref, bf16[2,4,128,128]{3,2,1,0:T(8,128)(2,1)S(1)} %get-tuple-element.60.near_ref, bf16[2,4,128,128]{3,2,1,0:T(8,128)(2,1)S(1)} %collective-permute-done.1.lent_ref, bf16[128,512]{1,0:T(8,128)(2,1)S(1)} %get-tuple-element.61.refs_0_, ...), custom_call_target="tpu_custom_call" | custom-call | tf_op jit(solution)/shard_map/pallas_call | solution.py:27
  22.6 1.6 %collective-permute-start.13 = (bf16[1,128,2048]{2,1,0:T(8,128)(2,1)S(1)}, bf16[1,128,2048]{2,1,0:T(8,128)(2,1)S(1)}, u32[]{:S(2)}, u32[]{:S(2)}) collective-permute-start(bf16[1,128,2048]{2,1,0:T(8,128)(2,1)S(1)} %copy-done.5), channel_id=1, source_target_pairs={{16,0},{0,16},{17,1},{1,17},{18,2},{2,18},{19,3},{3,19},{20,4},{4,... | collective-permute-start | bytes 1572872 | tf_op jit(solution)/shard_map/ppermute | solution.py:217
  24.5 3.4 %collective-permute-start.10 = (bf16[128,512]{1,0:T(8,128)(2,1)S(1)}, bf16[128,512]{1,0:T(8,128)(2,1)S(1)}, u32[]{:S(2)}, u32[]{:S(2)}) collective-permute-start(bf16[128,512]{1,0:T(8,128)(2,1)S(1)} %add_convert_fusion.1.own_ref), channel_id=1, source_target_pairs={{0,15},{1,2},{2,1},{3,4},{4,3},{5,6},{6,5},{7,8},{8,7},{9,10},{10,... | collective-permute-start | bytes 393224 | tf_op jit(solution)/shard_map/ppermute | solution.py:223
  27.9 1.0 %shard_map.78 = (f32[2,256,1024]{2,1,0:T(8,128)S(1)}, f32[2,256,1024]{2,1,0:T(8,128)S(1)}, f32[2,3,1024]{2,1,0:T(4,128)S(1)}) custom-call(s32[1]{0:T(128)} %bitcast.me_ref, bf16[128,2048]{1,0:T(8,128)(2,1)S(1)} %bitcast.10, bf16[128,2048]{1,0:T(8,128)(2,1)S(1)} %bitcast.13, bf16[128,512]{1,0:T(8,128)(2,1)S(1)} %collective-permute-done.9.beside_ref, ...), custom_call_target="tpu_custom_call" | custom-call | tf_op jit(solution)/shard_map/pallas_call | solution.py:27
  29.0 2.7 %collective-permute-done.10.across_ref = bf16[128,512]{1,0:T(8,128)(2,1)S(1)} collective-permute-done((bf16[128,512]{1,0:T(8,128)(2,1)S(1)}, bf16[128,512]{1,0:T(8,128)(2,1)S(1)}, u32[]{:S(2)}, u32[]{:S(2)}) %collective-permute-start.10) | collective-permute-done | bytes 131104 | tf_op jit(solution)/shard_map/ppermute | solution.py:223
  31.7 1.2 %shard_map.79 = (bf16[128,512]{1,0:T(8,128)(2,1)S(1)}, bf16[2,128,1024]{2,1,0:T(8,128)(2,1)S(1)}, f32[2,2,1024]{2,1,0:T(2,128)S(1)}) custom-call(s32[1]{0:T(128)} %bitcast.me_ref, bf16[128,2048]{1,0:T(8,128)(2,1)S(1)} %bitcast.11, bf16[128,2048]{1,0:T(8,128)(2,1)S(1)} %bitcast.14, bf16[128,512]{1,0:T(8,128)(2,1)S(1)} %collective-permute-done.10.across_ref, ...), custom_call_target="tpu_custom_call" | custom-call | tf_op jit(solution)/shard_map/pallas_call | solution.py:27
  32.8 3.4 %collective-permute-start.15 = (bf16[128,512]{1,0:T(8,128)(2,1)S(1)}, bf16[128,512]{1,0:T(8,128)(2,1)S(1)}, u32[]{:S(2)}, u32[]{:S(2)}) collective-permute-start(bf16[128,512]{1,0:T(8,128)(2,1)S(1)} %get-tuple-element.87), channel_id=1, source_target_pairs={{0,15},{1,2},{2,1},{3,4},{4,3},{5,6},{6,5},{7,8},{8,7},{9,10},{10,... | collective-permute-start | bytes 393224 | tf_op jit(solution)/shard_map/ppermute | solution.py:223
  36.3 1.9 %shard_map.80 = (bf16[128,2048]{1,0:T(8,128)(2,1)}, bf16[128,512]{1,0:T(8,128)(2,1)S(1)}, f32[128,512]{1,0:T(8,128)S(1)}) custom-call(bf16[128,2048]{1,0:T(8,128)(2,1)S(1)} %bitcast.12, bf16[128,2048]{1,0:T(8,128)(2,1)S(1)} %bitcast.15, bf16[128,512]{1,0:T(8,128)(2,1)S(1)} %collective-permute-done.9.beside_ref, ...), custom_call_target="tpu_custom_call" | custom-call | tf_op jit(solution)/shard_map/pallas_call | solution.py:27
  38.3 1.7 %collective-permute-done.15 = bf16[128,512]{1,0:T(8,128)(2,1)S(1)} collective-permute-done((bf16[128,512]{1,0:T(8,128)(2,1)S(1)}, bf16[128,512]{1,0:T(8,128)(2,1)S(1)}, u32[]{:S(2)}, u32[]{:S(2)}) %collective-permute-start.15) | collective-permute-done | bytes 131104 | tf_op jit(solution)/shard_map/ppermute | solution.py:223
  40.2 5.1 %collective-permute-done.17.refs_5_ = bf16[128,512]{1,0:T(8,128)(2,1)S(1)} collective-permute-done((bf16[128,512]{1,0:T(8,128)(2,1)S(1)}, bf16[128,512]{1,0:T(8,128)(2,1)S(1)}, u32[]{:S(2)}, u32[]{:S(2)}) %collective-permute-start.17) | collective-permute-done | bytes 131104 | tf_op jit(solution)/shard_map/ppermute | solution.py:212
  45.3 0.7 %shard_map.82 = (f32[8,128,128]{2,1,0:T(8,128)S(1)}, bf16[8,128,128]{2,1,0:T(8,128)(2,1)S(1)}) custom-call(bf16[128,512]{1,0:T(8,128)(2,1)S(1)} %add_convert_fusion.refs_3_.own_ref, bf16[128,512]{1,0:T(8,128)(2,1)S(1)} %collective-permute-done.16.refs_4_.beside_ref, bf16[128,512]{1,0:T(8,128)(2,1)S(1)} %get-tuple-element.61.refs_0_, ...), custom_call_target="tpu_custom_call" | custom-call | tf_op jit(solution)/shard_map/pallas_call | solution.py:27
  46.1 0.6 collective-permute-start.22
  46.7 0.5 shard_map.81
  47.2 0.3 collective-permute-start.19
  47.5 2.1 %collective-permute-start.20 = (bf16[128,512]{1,0:T(8,128)(2,1)S(1)}, bf16[128,512]{1,0:T(8,128)(2,1)S(1)}, u32[]{:S(2)}, u32[]{:S(2)}) collective-permute-start(bf16[128,512]{1,0:T(8,128)(2,1)S(1)} %get-tuple-element.89), channel_id=1, source_target_pairs={{0,4},{1,5},{2,6},{3,7},{4,0},{5,1},{6,2},{7,3},{8,12},{9,13},{10,... | collective-permute-start | bytes 393224 | tf_op jit(solution)/shard_map/ppermute | solution.py:212
  49.6 2.1 %collective-permute-start.21 = (bf16[128,512]{1,0:T(8,128)(2,1)S(1)}, bf16[128,512]{1,0:T(8,128)(2,1)S(1)}, u32[]{:S(2)}, u32[]{:S(2)}) collective-permute-start(bf16[128,512]{1,0:T(8,128)(2,1)S(1)} %get-tuple-element.90), channel_id=1, source_target_pairs={{0,12},{1,13},{2,14},{3,15},{4,8},{5,9},{6,10},{7,11},{8,4},{9,5},... | collective-permute-start | bytes 393224 | tf_op jit(solution)/shard_map/ppermute | solution.py:212
  51.6 1.4 %shard_map.83 = bf16[128,2048]{1,0:T(8,128)(2,1)} custom-call(s32[1]{0:T(128)} %bitcast.me_ref, bf16[128,2048]{1,0:T(8,128)(2,1)S(1)} %bitcast.17, f32[128,1]{1,0:T(8,128)S(1)} %get-tuple-element.91.factor_ref, bf16[128,2048]{1,0:T(8,128)(2,1)S(1)} %bitcast.18, f32[8,128,128]{2,1,0:T(8,128)S(1)} %get-tuple-element.93.near_ref, ...), custom_call_target="tpu_custom_call" | custom-call | tf_op jit(solution)/shard_map/pallas_call | solution.py:27
  53.0 5.7 %collective-permute-done.19 = bf16[128,512]{1,0:T(8,128)(2,1)S(1)} collective-permute-done((bf16[128,512]{1,0:T(8,128)(2,1)S(1)}, bf16[128,512]{1,0:T(8,128)(2,1)S(1)}, u32[]{:S(2)}, u32[]{:S(2)}) %collective-permute-start.19) | collective-permute-done | bytes 131104 | tf_op jit(solution)/shard_map/ppermute | solution.py:212
  58.9 0.8 %multiply_bitcast_fusion = f32[1,128,512]{2,1,0:T(8,128)} fusion(bf16[128,512]{1,0:T(8,128)(2,1)S(1)} %collective-permute-done.21, bf16[128,512]{1,0:T(8,128)(2,1)S(1)} %collective-permute-done.20, f32[128,512]{1,0:T(8,128)S(1)} %get-tuple-element.97, bf16[128,512]{1,0:T(8,128)(2,1)S(1)} %collective-permute-done.19), kind=kLoop, calls=%fused_computation | loop fusion | flops 458752 | bytes 917504 | tf_op jit(solution)/shard_map/broadcast_in_dim | solution.py:320
  (37 shorter events, 1.0 us)
Async XLA Ops:
  0.6 27.2 %copy-start = (bf16[1,128,2048]{2,1,0:T(8,128)(2,1)S(1)}, bf16[1,128,2048]{2,1,0:T(8,128)(2,1)}, u32[]{:S(2)}) copy-start(bf16[1,128,2048]{2,1,0:T(8,128)(2,1)} %param.7) | copy-start | bytes 1572868
  0.6 27.2 %copy-start.1 = (bf16[1,128,2048]{2,1,0:T(8,128)(2,1)S(1)}, bf16[1,128,2048]{2,1,0:T(8,128)(2,1)}, u32[]{:S(2)}) copy-start(bf16[1,128,2048]{2,1,0:T(8,128)(2,1)} %param.8) | copy-start | bytes 1572868
  0.7 9.6 %collective-permute-start = (bf16[128,512]{1,0:T(8,128)(2,1)}, bf16[128,512]{1,0:T(8,128)(2,1)S(1)}, u32[]{:S(2)}, u32[]{:S(2)}) collective-permute-start(bf16[128,512]{1,0:T(8,128)(2,1)} %bitcast.19), channel_id=1, source_target_pairs={{0,4},{1,5},{2,6},{3,7},{4,0},{5,1},{6,2},{7,3},{8,12},{9,13},{10,... | collective-permute-start | bytes 393224 | tf_op jit(solution)/shard_map/ppermute | solution.py:212
  3.7 8.9 %collective-permute-start.2 = (bf16[128,512]{1,0:T(8,128)(2,1)}, bf16[128,512]{1,0:T(8,128)(2,1)S(1)}, u32[]{:S(2)}, u32[]{:S(2)}) collective-permute-start(bf16[128,512]{1,0:T(8,128)(2,1)} %bitcast.20), channel_id=1, source_target_pairs={{0,8},{1,9},{2,10},{3,11},{4,12},{5,13},{6,14},{7,15},{8,0},{9,1},... | collective-permute-start | bytes 393224 | tf_op jit(solution)/shard_map/ppermute | solution.py:212
  6.3 6.4 %collective-permute-start.3 = (bf16[128,512]{1,0:T(8,128)(2,1)}, bf16[128,512]{1,0:T(8,128)(2,1)S(1)}, u32[]{:S(2)}, u32[]{:S(2)}) collective-permute-start(bf16[128,512]{1,0:T(8,128)(2,1)} %bitcast.21), channel_id=1, source_target_pairs={{0,2},{1,3},{2,0},{3,1},{4,6},{5,7},{6,4},{7,5},{8,10},{9,11},{10,... | collective-permute-start | bytes 393224 | tf_op jit(solution)/shard_map/ppermute | solution.py:212
  7.8 1.0 %copy-start.2 = (bf16[1,128,2048]{2,1,0:T(8,128)(2,1)S(1)}, bf16[1,128,2048]{2,1,0:T(8,128)(2,1)}, u32[]{:S(2)}) copy-start(bf16[1,128,2048]{2,1,0:T(8,128)(2,1)} %param.5) | copy-start | bytes 1572868
  8.9 0.9 %copy-start.4 = (bf16[1,128,512]{2,1,0:T(8,128)(2,1)S(1)}, bf16[1,128,512]{2,1,0:T(8,128)(2,1)}, u32[]{:S(2)}) copy-start(bf16[1,128,512]{2,1,0:T(8,128)(2,1)} %param.9) | copy-start | bytes 393220
  9.8 12.8 %copy-start.5 = (bf16[1,128,2048]{2,1,0:T(8,128)(2,1)S(1)}, bf16[1,128,2048]{2,1,0:T(8,128)(2,1)}, u32[]{:S(2)}) copy-start(bf16[1,128,2048]{2,1,0:T(8,128)(2,1)} %param.6) | copy-start | bytes 1572868
  10.2 11.6 %collective-permute-start.1 = (bf16[2,4,128,128]{3,2,1,0:T(8,128)(2,1)S(1)}, bf16[2,4,128,128]{3,2,1,0:T(8,128)(2,1)S(1)}, u32[]{:S(2)}, u32[]{:S(2)}) collective-permute-start(bf16[2,4,128,128]{3,2,1,0:T(8,128)(2,1)S(1)} %get-tuple-element.59), channel_id=1, source_target_pairs={{0,1},{1,0},{2,3},{3,2},{4,5},{5,4},{6,7},{7,6},{8,9},{9,8},{10,11... | collective-permute-start | bytes 786440 | tf_op jit(solution)/shard_map/ppermute | solution.py:212
  10.3 7.8 %collective-permute-start.4 = (bf16[128,512]{1,0:T(8,128)(2,1)S(1)}, bf16[128,512]{1,0:T(8,128)(2,1)S(1)}, u32[]{:S(2)}, u32[]{:S(2)}) collective-permute-start(bf16[128,512]{1,0:T(8,128)(2,1)S(1)} %collective-permute-done.refs_2_), channel_id=1, source_target_pairs={{0,2},{1,3},{2,0},{3,1},{4,6},{5,7},{6,4},{7,5},{8,10},{9,11},{10,... | collective-permute-start | bytes 393224 | tf_op jit(solution)/shard_map/ppermute | solution.py:212
  12.7 9.2 %collective-permute-start.5 = (bf16[128,512]{1,0:T(8,128)(2,1)S(1)}, bf16[128,512]{1,0:T(8,128)(2,1)S(1)}, u32[]{:S(2)}, u32[]{:S(2)}) collective-permute-start(bf16[128,512]{1,0:T(8,128)(2,1)S(1)} %collective-permute-done.2.refs_4_), channel_id=1, source_target_pairs={{0,2},{1,3},{2,0},{3,1},{4,6},{5,7},{6,4},{7,5},{8,10},{9,11},{10,... | collective-permute-start | bytes 393224 | tf_op jit(solution)/shard_map/ppermute | solution.py:212
  14.2 7.6 %collective-permute-start.7 = (bf16[128,512]{1,0:T(8,128)(2,1)S(1)}, bf16[128,512]{1,0:T(8,128)(2,1)S(1)}, u32[]{:S(2)}, u32[]{:S(2)}) collective-permute-start(bf16[128,512]{1,0:T(8,128)(2,1)S(1)} %collective-permute-done.2.refs_4_), channel_id=1, source_target_pairs={{0,6},{1,7},{2,4},{3,5},{4,2},{5,3},{6,0},{7,1},{8,14},{9,15},{10,... | collective-permute-start | bytes 393224 | tf_op jit(solution)/shard_map/ppermute | solution.py:212
  14.6 7.3 %collective-permute-start.6 = (bf16[128,512]{1,0:T(8,128)(2,1)S(1)}, bf16[128,512]{1,0:T(8,128)(2,1)S(1)}, u32[]{:S(2)}, u32[]{:S(2)}) collective-permute-start(bf16[128,512]{1,0:T(8,128)(2,1)S(1)} %collective-permute-done.2.refs_4_), channel_id=1, source_target_pairs={{0,4},{1,5},{2,6},{3,7},{4,0},{5,1},{6,2},{7,3},{8,12},{9,13},{10,... | collective-permute-start | bytes 393224 | tf_op jit(solution)/shard_map/ppermute | solution.py:212
  22.6 1.6 %collective-permute-start.8 = (f32[128,512]{1,0:T(8,128)S(1)}, f32[128,512]{1,0:T(8,128)S(1)}, u32[]{:S(2)}, u32[]{:S(2)}) collective-permute-start(f32[128,512]{1,0:T(8,128)S(1)} %get-tuple-element.67), channel_id=1, source_target_pairs={{0,1},{1,0},{2,3},{3,2},{4,5},{5,4},{6,7},{7,6},{8,9},{9,8},{10,11... | collective-permute-start | bytes 786440 | tf_op jit(solution)/shard_map/ppermute | solution.py:212
  22.6 15.6 %collective-permute-start.13 = (bf16[1,128,2048]{2,1,0:T(8,128)(2,1)S(1)}, bf16[1,128,2048]{2,1,0:T(8,128)(2,1)S(1)}, u32[]{:S(2)}, u32[]{:S(2)}) collective-permute-start(bf16[1,128,2048]{2,1,0:T(8,128)(2,1)S(1)} %copy-done.5), channel_id=1, source_target_pairs={{16,0},{0,16},{17,1},{1,17},{18,2},{2,18},{19,3},{3,19},{20,4},{4,... | collective-permute-start | bytes 1572872 | tf_op jit(solution)/shard_map/ppermute | solution.py:217
  24.2 3.6 %collective-permute-start.9 = (bf16[128,512]{1,0:T(8,128)(2,1)S(1)}, bf16[128,512]{1,0:T(8,128)(2,1)S(1)}, u32[]{:S(2)}, u32[]{:S(2)}) collective-permute-start(bf16[128,512]{1,0:T(8,128)(2,1)S(1)} %add_convert_fusion.1.own_ref), channel_id=1, source_target_pairs={{0,1},{1,0},{2,3},{3,2},{4,5},{5,4},{6,7},{7,6},{8,9},{9,8},{10,11... | collective-permute-start | bytes 393224 | tf_op jit(solution)/shard_map/ppermute | solution.py:212
  24.5 7.2 %collective-permute-start.10 = (bf16[128,512]{1,0:T(8,128)(2,1)S(1)}, bf16[128,512]{1,0:T(8,128)(2,1)S(1)}, u32[]{:S(2)}, u32[]{:S(2)}) collective-permute-start(bf16[128,512]{1,0:T(8,128)(2,1)S(1)} %add_convert_fusion.1.own_ref), channel_id=1, source_target_pairs={{0,15},{1,2},{2,1},{3,4},{4,3},{5,6},{6,5},{7,8},{8,7},{9,10},{10,... | collective-permute-start | bytes 393224 | tf_op jit(solution)/shard_map/ppermute | solution.py:223
  28.8 9.4 %collective-permute-start.11 = (bf16[4,128,128]{2,1,0:T(8,128)(2,1)S(1)}, bf16[4,128,128]{2,1,0:T(8,128)(2,1)S(1)}, u32[]{:S(2)}, u32[]{:S(2)}) collective-permute-start(bf16[4,128,128]{2,1,0:T(8,128)(2,1)S(1)} %get-tuple-element.79), channel_id=1, source_target_pairs={{0,2},{1,3},{2,0},{3,1},{4,6},{5,7},{6,4},{7,5},{8,10},{9,11},{10,... | collective-permute-start | bytes 393224 | tf_op jit(solution)/shard_map/ppermute | solution.py:212
  28.9 9.4 %collective-permute-start.12 = (bf16[4,128,128]{2,1,0:T(8,128)(2,1)S(1)}, bf16[4,128,128]{2,1,0:T(8,128)(2,1)S(1)}, u32[]{:S(2)}, u32[]{:S(2)}) collective-permute-start(bf16[4,128,128]{2,1,0:T(8,128)(2,1)S(1)} %get-tuple-element.80), channel_id=1, source_target_pairs={{0,3},{1,2},{2,1},{3,0},{4,7},{5,6},{6,5},{7,4},{8,11},{9,10},{10,... | collective-permute-start | bytes 393224 | tf_op jit(solution)/shard_map/ppermute | solution.py:212
  32.8 7.2 %collective-permute-start.15 = (bf16[128,512]{1,0:T(8,128)(2,1)S(1)}, bf16[128,512]{1,0:T(8,128)(2,1)S(1)}, u32[]{:S(2)}, u32[]{:S(2)}) collective-permute-start(bf16[128,512]{1,0:T(8,128)(2,1)S(1)} %get-tuple-element.87), channel_id=1, source_target_pairs={{0,15},{1,2},{2,1},{3,4},{4,3},{5,6},{6,5},{7,8},{8,7},{9,10},{10,... | collective-permute-start | bytes 393224 | tf_op jit(solution)/shard_map/ppermute | solution.py:223
  38.2 13.4 %copy-start.3 = (bf16[1,128,2048]{2,1,0:T(8,128)(2,1)S(1)}, bf16[1,128,2048]{2,1,0:T(8,128)(2,1)}, u32[]{:S(2)}) copy-start(bf16[1,128,2048]{2,1,0:T(8,128)(2,1)} %param.5) | copy-start | bytes 1572868
  38.3 1.7 %collective-permute-start.14 = (bf16[128,512]{1,0:T(8,128)(2,1)S(1)}, bf16[128,512]{1,0:T(8,128)(2,1)S(1)}, u32[]{:S(2)}, u32[]{:S(2)}) collective-permute-start(bf16[128,512]{1,0:T(8,128)(2,1)S(1)} %get-tuple-element.86), channel_id=1, source_target_pairs={{0,1},{1,0},{2,3},{3,2},{4,5},{5,4},{6,7},{7,6},{8,9},{9,8},{10,11... | collective-permute-start | bytes 393224 | tf_op jit(solution)/shard_map/ppermute | solution.py:212
  40.1 5.3 %collective-permute-start.17 = (bf16[128,512]{1,0:T(8,128)(2,1)S(1)}, bf16[128,512]{1,0:T(8,128)(2,1)S(1)}, u32[]{:S(2)}, u32[]{:S(2)}) collective-permute-start(bf16[128,512]{1,0:T(8,128)(2,1)S(1)} %add_convert_fusion.refs_3_.own_ref), channel_id=1, source_target_pairs={{0,2},{1,3},{2,0},{3,1},{4,6},{5,7},{6,4},{7,5},{8,10},{9,11},{10,... | collective-permute-start | bytes 393224 | tf_op jit(solution)/shard_map/ppermute | solution.py:212
  40.1 5.2 %collective-permute-start.16 = (bf16[128,512]{1,0:T(8,128)(2,1)S(1)}, bf16[128,512]{1,0:T(8,128)(2,1)S(1)}, u32[]{:S(2)}, u32[]{:S(2)}) collective-permute-start(bf16[128,512]{1,0:T(8,128)(2,1)S(1)} %add_convert_fusion.refs_3_.own_ref), channel_id=1, source_target_pairs={{0,1},{1,0},{2,3},{3,2},{4,5},{5,4},{6,7},{7,6},{8,9},{9,8},{10,11... | collective-permute-start | bytes 393224 | tf_op jit(solution)/shard_map/ppermute | solution.py:212
  45.3 1.3 %collective-permute-start.18 = (bf16[128,512]{1,0:T(8,128)(2,1)S(1)}, bf16[128,512]{1,0:T(8,128)(2,1)S(1)}, u32[]{:S(2)}, u32[]{:S(2)}) collective-permute-start(bf16[128,512]{1,0:T(8,128)(2,1)S(1)} %collective-permute-done.17.refs_5_), channel_id=1, source_target_pairs={{0,1},{1,0},{2,3},{3,2},{4,5},{5,4},{6,7},{7,6},{8,9},{9,8},{10,11... | collective-permute-start | bytes 393224 | tf_op jit(solution)/shard_map/ppermute | solution.py:212
  46.1 5.6 %collective-permute-start.22 = (bf16[8,128,128]{2,1,0:T(8,128)(2,1)S(1)}, bf16[8,128,128]{2,1,0:T(8,128)(2,1)S(1)}, u32[]{:S(2)}, u32[]{:S(2)}) collective-permute-start(bf16[8,128,128]{2,1,0:T(8,128)(2,1)S(1)} %get-tuple-element.94), channel_id=1, source_target_pairs={{0,1},{1,0},{2,3},{3,2},{4,5},{5,4},{6,7},{7,6},{8,9},{9,8},{10,11... | collective-permute-start | bytes 786440 | tf_op jit(solution)/shard_map/ppermute | solution.py:212
  47.2 11.6 %collective-permute-start.19 = (bf16[128,512]{1,0:T(8,128)(2,1)S(1)}, bf16[128,512]{1,0:T(8,128)(2,1)S(1)}, u32[]{:S(2)}, u32[]{:S(2)}) collective-permute-start(bf16[128,512]{1,0:T(8,128)(2,1)S(1)} %get-tuple-element.88), channel_id=1, source_target_pairs={{0,8},{1,9},{2,10},{3,11},{4,12},{5,13},{6,14},{7,15},{8,0},{9,1},... | collective-permute-start | bytes 393224 | tf_op jit(solution)/shard_map/ppermute | solution.py:212
  47.5 11.3 %collective-permute-start.20 = (bf16[128,512]{1,0:T(8,128)(2,1)S(1)}, bf16[128,512]{1,0:T(8,128)(2,1)S(1)}, u32[]{:S(2)}, u32[]{:S(2)}) collective-permute-start(bf16[128,512]{1,0:T(8,128)(2,1)S(1)} %get-tuple-element.89), channel_id=1, source_target_pairs={{0,4},{1,5},{2,6},{3,7},{4,0},{5,1},{6,2},{7,3},{8,12},{9,13},{10,... | collective-permute-start | bytes 393224 | tf_op jit(solution)/shard_map/ppermute | solution.py:212
  49.6 9.3 %collective-permute-start.21 = (bf16[128,512]{1,0:T(8,128)(2,1)S(1)}, bf16[128,512]{1,0:T(8,128)(2,1)S(1)}, u32[]{:S(2)}, u32[]{:S(2)}) collective-permute-start(bf16[128,512]{1,0:T(8,128)(2,1)S(1)} %get-tuple-element.90), channel_id=1, source_target_pairs={{0,12},{1,13},{2,14},{3,15},{4,8},{5,9},{6,10},{7,11},{8,4},{9,5},... | collective-permute-start | bytes 393224 | tf_op jit(solution)/shard_map/ppermute | solution.py:212

commit v6 on v5

--- a/solution.py
+++ b/solution.py
@@ -59,10 +59,11 @@
     own = me_ref[0] // 4
     rows = own_ref.shape[0]
     total = None
-    for half, weight in enumerate(weights):
-        at = own ^ (half // 2)
-        lhs = jnp.concatenate([near_ref[half % 2, at], lent_ref[half % 2, at]], axis=0)
-        part = f32dot(lhs, weight[...])
+    for zz in range(len(weights) // 2):
+        at = own ^ zz
+        lhs = [jnp.concatenate([near_ref[k, at], lent_ref[k, at]], axis=0) for k in range(2)]
+        rhs = jnp.concatenate([weights[2 * zz][...], weights[2 * zz + 1][...]], axis=0)
+        part = f32dot(jnp.concatenate(lhs, axis=1), rhs)
         total = part if total is None else total + part
     own_ref[...] = total[:rows]
     beside_ref[...] = total[rows:]

time: 60.1 us -> 59.9 us (level)
  no operation moved by 1% of the time
where the time goes in v6:
time: 59.9 us; the launch traced here: 59.4 us
  starting transfers between devices  25.6 us (43%)
  waiting for transfers between devices  22.7 us (38%)
  Pallas kernels  7.5 us (13%)
  local copies, waits for them, and re-layouts  1.96 us (3%)
  other arithmetic  0.85 us (1%)
  between operations  0.81 us (1%)
    ppermute x20, waiting for transfers between devices, swap(): return lax.ppermute(block, 'ctx', [(i, i ^ distance) for i in range(count)])  18.3 us
    ppermute x20, starting transfers between devices, swap(): return lax.ppermute(block, 'ctx', [(i, i ^ distance) for i in range(count)])  17.2 us
    pallas_call x8, Pallas kernels, call(): pl.pallas_call(kernel, out_shape=[jax.ShapeDtypeStruct(s, d) for s, d in...  7.5 us
    ppermute x2, starting transfers between devices, crossed(): return lax.ppermute(block, 'ctx', route)  6.81 us
    ppermute x2, waiting for transfers between devices, crossed(): return lax.ppermute(block, 'ctx', route)  4.36 us
    unnamed x12, local copies, waits for them, and re-layouts  1.96 us
    ppermute x1, starting transfers between devices, shifted(): lax.ppermute(block, axis, [((i - distance) % count, i) for i in range(cou...  1.56 us
  transfers between devices with their start and end apart: 23, of which 9 were waited for; matrix products, arithmetic and copies ran while one was open for 0% of the time, Pallas kernels for 12%

profile of v6, /device:TPU:0, one launch (start us, length us, event | category | flops | bytes accessed | tf_op | source)
XLA Modules:
  0.0 59.4 jit_solution(5924406094370470104)
XLA Ops:
  0.7 3.1 %collective-permute-start = (bf16[128,512]{1,0:T(8,128)(2,1)}, bf16[128,512]{1,0:T(8,128)(2,1)S(1)}, u32[]{:S(2)}, u32[]{:S(2)}) collective-permute-start(bf16[128,512]{1,0:T(8,128)(2,1)} %bitcast.19), channel_id=1, source_target_pairs={{0,4},{1,5},{2,6},{3,7},{4,0},{5,1},{6,2},{7,3},{8,12},{9,13},{10,... | collective-permute-start | bytes 393224 | tf_op jit(solution)/shard_map/ppermute | solution.py:213
  3.7 2.6 %collective-permute-start.2 = (bf16[128,512]{1,0:T(8,128)(2,1)}, bf16[128,512]{1,0:T(8,128)(2,1)S(1)}, u32[]{:S(2)}, u32[]{:S(2)}) collective-permute-start(bf16[128,512]{1,0:T(8,128)(2,1)} %bitcast.20), channel_id=1, source_target_pairs={{0,8},{1,9},{2,10},{3,11},{4,12},{5,13},{6,14},{7,15},{8,0},{9,1},... | collective-permute-start | bytes 393224 | tf_op jit(solution)/shard_map/ppermute | solution.py:213
  6.3 1.5 %collective-permute-start.3 = (bf16[128,512]{1,0:T(8,128)(2,1)}, bf16[128,512]{1,0:T(8,128)(2,1)S(1)}, u32[]{:S(2)}, u32[]{:S(2)}) collective-permute-start(bf16[128,512]{1,0:T(8,128)(2,1)} %bitcast.21), channel_id=1, source_target_pairs={{0,2},{1,3},{2,0},{3,1},{4,6},{5,7},{6,4},{7,5},{8,10},{9,11},{10,... | collective-permute-start | bytes 393224 | tf_op jit(solution)/shard_map/ppermute | solution.py:213
  7.9 1.0 %copy-done.2 = bf16[1,128,2048]{2,1,0:T(8,128)(2,1)S(1)} copy-done((bf16[1,128,2048]{2,1,0:T(8,128)(2,1)S(1)}, bf16[1,128,2048]{2,1,0:T(8,128)(2,1)}, u32[]{:S(2)}) %copy-start.2) | copy-done | bytes 524312
  8.9 0.9 %copy-done.4 = bf16[1,128,512]{2,1,0:T(8,128)(2,1)S(1)} copy-done((bf16[1,128,512]{2,1,0:T(8,128)(2,1)S(1)}, bf16[1,128,512]{2,1,0:T(8,128)(2,1)}, u32[]{:S(2)}) %copy-start.4) | copy-done | bytes 131096
  9.8 0.4 shard_map.76
  10.3 0.8 %collective-permute-start.4 = (bf16[128,512]{1,0:T(8,128)(2,1)S(1)}, bf16[128,512]{1,0:T(8,128)(2,1)S(1)}, u32[]{:S(2)}, u32[]{:S(2)}) collective-permute-start(bf16[128,512]{1,0:T(8,128)(2,1)S(1)} %collective-permute-done.refs_2_), channel_id=1, source_target_pairs={{0,2},{1,3},{2,0},{3,1},{4,6},{5,7},{6,4},{7,5},{8,10},{9,11},{10,... | collective-permute-start | bytes 393224 | tf_op jit(solution)/shard_map/ppermute | solution.py:213
  11.1 1.6 %collective-permute-done.2.refs_4_ = bf16[128,512]{1,0:T(8,128)(2,1)S(1)} collective-permute-done((bf16[128,512]{1,0:T(8,128)(2,1)}, bf16[128,512]{1,0:T(8,128)(2,1)S(1)}, u32[]{:S(2)}, u32[]{:S(2)}) %collective-permute-start.2) | collective-permute-done | bytes 131104 | tf_op jit(solution)/shard_map/ppermute | solution.py:213
  12.7 1.5 %collective-permute-start.5 = (bf16[128,512]{1,0:T(8,128)(2,1)S(1)}, bf16[128,512]{1,0:T(8,128)(2,1)S(1)}, u32[]{:S(2)}, u32[]{:S(2)}) collective-permute-start(bf16[128,512]{1,0:T(8,128)(2,1)S(1)} %collective-permute-done.2.refs_4_), channel_id=1, source_target_pairs={{0,2},{1,3},{2,0},{3,1},{4,6},{5,7},{6,4},{7,5},{8,10},{9,11},{10,... | collective-permute-start | bytes 393224 | tf_op jit(solution)/shard_map/ppermute | solution.py:213
  14.2 0.4 collective-permute-start.7
  14.6 1.6 %collective-permute-start.6 = (bf16[128,512]{1,0:T(8,128)(2,1)S(1)}, bf16[128,512]{1,0:T(8,128)(2,1)S(1)}, u32[]{:S(2)}, u32[]{:S(2)}) collective-permute-start(bf16[128,512]{1,0:T(8,128)(2,1)S(1)} %collective-permute-done.2.refs_4_), channel_id=1, source_target_pairs={{0,4},{1,5},{2,6},{3,7},{4,0},{5,1},{6,2},{7,3},{8,12},{9,13},{10,... | collective-permute-start | bytes 393224 | tf_op jit(solution)/shard_map/ppermute | solution.py:213
  16.2 1.9 %collective-permute-done.4.refs_3_ = bf16[128,512]{1,0:T(8,128)(2,1)S(1)} collective-permute-done((bf16[128,512]{1,0:T(8,128)(2,1)S(1)}, bf16[128,512]{1,0:T(8,128)(2,1)S(1)}, u32[]{:S(2)}, u32[]{:S(2)}) %collective-permute-start.4) | collective-permute-done | bytes 131104 | tf_op jit(solution)/shard_map/ppermute | solution.py:213
  18.1 3.8 %collective-permute-done.5.refs_5_ = bf16[128,512]{1,0:T(8,128)(2,1)S(1)} collective-permute-done((bf16[128,512]{1,0:T(8,128)(2,1)S(1)}, bf16[128,512]{1,0:T(8,128)(2,1)S(1)}, u32[]{:S(2)}, u32[]{:S(2)}) %collective-permute-start.5) | collective-permute-done | bytes 131104 | tf_op jit(solution)/shard_map/ppermute | solution.py:213
  21.9 0.4 shard_map.77
  22.4 1.6 %collective-permute-start.13 = (bf16[1,128,2048]{2,1,0:T(8,128)(2,1)S(1)}, bf16[1,128,2048]{2,1,0:T(8,128)(2,1)S(1)}, u32[]{:S(2)}, u32[]{:S(2)}) collective-permute-start(bf16[1,128,2048]{2,1,0:T(8,128)(2,1)S(1)} %copy-done.5), channel_id=1, source_target_pairs={{16,0},{0,16},{17,1},{1,17},{18,2},{2,18},{19,3},{3,19},{20,4},{4,... | collective-permute-start | bytes 1572872 | tf_op jit(solution)/shard_map/ppermute | solution.py:218
  24.2 3.4 %collective-permute-start.10 = (bf16[128,512]{1,0:T(8,128)(2,1)S(1)}, bf16[128,512]{1,0:T(8,128)(2,1)S(1)}, u32[]{:S(2)}, u32[]{:S(2)}) collective-permute-start(bf16[128,512]{1,0:T(8,128)(2,1)S(1)} %add_convert_fusion.1.own_ref), channel_id=1, source_target_pairs={{0,15},{1,2},{2,1},{3,4},{4,3},{5,6},{6,5},{7,8},{8,7},{9,10},{10,... | collective-permute-start | bytes 393224 | tf_op jit(solution)/shard_map/ppermute | solution.py:224
  27.6 1.0 %shard_map.78 = (f32[2,256,1024]{2,1,0:T(8,128)S(1)}, f32[2,256,1024]{2,1,0:T(8,128)S(1)}, f32[2,3,1024]{2,1,0:T(4,128)S(1)}) custom-call(s32[1]{0:T(128)} %bitcast.me_ref, bf16[128,2048]{1,0:T(8,128)(2,1)S(1)} %bitcast.10, bf16[128,2048]{1,0:T(8,128)(2,1)S(1)} %bitcast.13, bf16[128,512]{1,0:T(8,128)(2,1)S(1)} %collective-permute-done.9.beside_ref, ...), custom_call_target="tpu_custom_call" | custom-call | tf_op jit(solution)/shard_map/pallas_call | solution.py:27
  28.7 2.7 %collective-permute-done.10.across_ref = bf16[128,512]{1,0:T(8,128)(2,1)S(1)} collective-permute-done((bf16[128,512]{1,0:T(8,128)(2,1)S(1)}, bf16[128,512]{1,0:T(8,128)(2,1)S(1)}, u32[]{:S(2)}, u32[]{:S(2)}) %collective-permute-start.10) | collective-permute-done | bytes 131104 | tf_op jit(solution)/shard_map/ppermute | solution.py:224
  31.4 1.2 %shard_map.79 = (bf16[128,512]{1,0:T(8,128)(2,1)S(1)}, bf16[2,128,1024]{2,1,0:T(8,128)(2,1)S(1)}, f32[2,2,1024]{2,1,0:T(2,128)S(1)}) custom-call(s32[1]{0:T(128)} %bitcast.me_ref, bf16[128,2048]{1,0:T(8,128)(2,1)S(1)} %bitcast.11, bf16[128,2048]{1,0:T(8,128)(2,1)S(1)} %bitcast.14, bf16[128,512]{1,0:T(8,128)(2,1)S(1)} %collective-permute-done.10.across_ref, ...), custom_call_target="tpu_custom_call" | custom-call | tf_op jit(solution)/shard_map/pallas_call | solution.py:27
  32.6 3.4 %collective-permute-start.15 = (bf16[128,512]{1,0:T(8,128)(2,1)S(1)}, bf16[128,512]{1,0:T(8,128)(2,1)S(1)}, u32[]{:S(2)}, u32[]{:S(2)}) collective-permute-start(bf16[128,512]{1,0:T(8,128)(2,1)S(1)} %get-tuple-element.87), channel_id=1, source_target_pairs={{0,15},{1,2},{2,1},{3,4},{4,3},{5,6},{6,5},{7,8},{8,7},{9,10},{10,... | collective-permute-start | bytes 393224 | tf_op jit(solution)/shard_map/ppermute | solution.py:224
  36.0 1.9 %shard_map.80 = (bf16[128,2048]{1,0:T(8,128)(2,1)}, bf16[128,512]{1,0:T(8,128)(2,1)S(1)}, f32[128,512]{1,0:T(8,128)S(1)}) custom-call(bf16[128,2048]{1,0:T(8,128)(2,1)S(1)} %bitcast.12, bf16[128,2048]{1,0:T(8,128)(2,1)S(1)} %bitcast.15, bf16[128,512]{1,0:T(8,128)(2,1)S(1)} %collective-permute-done.9.beside_ref, ...), custom_call_target="tpu_custom_call" | custom-call | tf_op jit(solution)/shard_map/pallas_call | solution.py:27
  38.1 1.7 %collective-permute-done.15 = bf16[128,512]{1,0:T(8,128)(2,1)S(1)} collective-permute-done((bf16[128,512]{1,0:T(8,128)(2,1)S(1)}, bf16[128,512]{1,0:T(8,128)(2,1)S(1)}, u32[]{:S(2)}, u32[]{:S(2)}) %collective-permute-start.15) | collective-permute-done | bytes 131104 | tf_op jit(solution)/shard_map/ppermute | solution.py:224
  40.0 5.1 %collective-permute-done.17.refs_5_ = bf16[128,512]{1,0:T(8,128)(2,1)S(1)} collective-permute-done((bf16[128,512]{1,0:T(8,128)(2,1)S(1)}, bf16[128,512]{1,0:T(8,128)(2,1)S(1)}, u32[]{:S(2)}, u32[]{:S(2)}) %collective-permute-start.17) | collective-permute-done | bytes 131104 | tf_op jit(solution)/shard_map/ppermute | solution.py:213
  45.1 0.7 %shard_map.82 = (f32[8,128,128]{2,1,0:T(8,128)S(1)}, bf16[8,128,128]{2,1,0:T(8,128)(2,1)S(1)}) custom-call(bf16[128,512]{1,0:T(8,128)(2,1)S(1)} %add_convert_fusion.refs_3_.own_ref, bf16[128,512]{1,0:T(8,128)(2,1)S(1)} %collective-permute-done.16.refs_4_.beside_ref, bf16[128,512]{1,0:T(8,128)(2,1)S(1)} %get-tuple-element.61.refs_0_, ...), custom_call_target="tpu_custom_call" | custom-call | tf_op jit(solution)/shard_map/pallas_call | solution.py:27
  45.8 0.6 collective-permute-start.22
  46.4 0.5 shard_map.81
  46.9 0.3 collective-permute-start.19
  47.3 2.1 %collective-permute-start.20 = (bf16[128,512]{1,0:T(8,128)(2,1)S(1)}, bf16[128,512]{1,0:T(8,128)(2,1)S(1)}, u32[]{:S(2)}, u32[]{:S(2)}) collective-permute-start(bf16[128,512]{1,0:T(8,128)(2,1)S(1)} %get-tuple-element.89), channel_id=1, source_target_pairs={{0,4},{1,5},{2,6},{3,7},{4,0},{5,1},{6,2},{7,3},{8,12},{9,13},{10,... | collective-permute-start | bytes 393224 | tf_op jit(solution)/shard_map/ppermute | solution.py:213
  49.3 2.0 %collective-permute-start.21 = (bf16[128,512]{1,0:T(8,128)(2,1)S(1)}, bf16[128,512]{1,0:T(8,128)(2,1)S(1)}, u32[]{:S(2)}, u32[]{:S(2)}) collective-permute-start(bf16[128,512]{1,0:T(8,128)(2,1)S(1)} %get-tuple-element.90), channel_id=1, source_target_pairs={{0,12},{1,13},{2,14},{3,15},{4,8},{5,9},{6,10},{7,11},{8,4},{9,5},... | collective-permute-start | bytes 393224 | tf_op jit(solution)/shard_map/ppermute | solution.py:213
  51.4 1.4 %shard_map.83 = bf16[128,2048]{1,0:T(8,128)(2,1)} custom-call(s32[1]{0:T(128)} %bitcast.me_ref, bf16[128,2048]{1,0:T(8,128)(2,1)S(1)} %bitcast.17, f32[128,1]{1,0:T(8,128)S(1)} %get-tuple-element.91.factor_ref, bf16[128,2048]{1,0:T(8,128)(2,1)S(1)} %bitcast.18, f32[8,128,128]{2,1,0:T(8,128)S(1)} %get-tuple-element.93.near_ref, ...), custom_call_target="tpu_custom_call" | custom-call | tf_op jit(solution)/shard_map/pallas_call | solution.py:27
  52.8 5.7 %collective-permute-done.19 = bf16[128,512]{1,0:T(8,128)(2,1)S(1)} collective-permute-done((bf16[128,512]{1,0:T(8,128)(2,1)S(1)}, bf16[128,512]{1,0:T(8,128)(2,1)S(1)}, u32[]{:S(2)}, u32[]{:S(2)}) %collective-permute-start.19) | collective-permute-done | bytes 131104 | tf_op jit(solution)/shard_map/ppermute | solution.py:213
  58.6 0.8 %multiply_bitcast_fusion = f32[1,128,512]{2,1,0:T(8,128)} fusion(bf16[128,512]{1,0:T(8,128)(2,1)S(1)} %collective-permute-done.21, bf16[128,512]{1,0:T(8,128)(2,1)S(1)} %collective-permute-done.20, f32[128,512]{1,0:T(8,128)S(1)} %get-tuple-element.97, bf16[128,512]{1,0:T(8,128)(2,1)S(1)} %collective-permute-done.19), kind=kLoop, calls=%fused_computation | loop fusion | flops 458752 | bytes 917504 | tf_op jit(solution)/shard_map/broadcast_in_dim | solution.py:321
  (37 shorter events, 1.0 us)
Async XLA Ops:
  0.6 27.0 %copy-start = (bf16[1,128,2048]{2,1,0:T(8,128)(2,1)S(1)}, bf16[1,128,2048]{2,1,0:T(8,128)(2,1)}, u32[]{:S(2)}) copy-start(bf16[1,128,2048]{2,1,0:T(8,128)(2,1)} %param.7) | copy-start | bytes 1572868
  0.6 27.0 %copy-start.1 = (bf16[1,128,2048]{2,1,0:T(8,128)(2,1)S(1)}, bf16[1,128,2048]{2,1,0:T(8,128)(2,1)}, u32[]{:S(2)}) copy-start(bf16[1,128,2048]{2,1,0:T(8,128)(2,1)} %param.8) | copy-start | bytes 1572868
  0.7 9.6 %collective-permute-start = (bf16[128,512]{1,0:T(8,128)(2,1)}, bf16[128,512]{1,0:T(8,128)(2,1)S(1)}, u32[]{:S(2)}, u32[]{:S(2)}) collective-permute-start(bf16[128,512]{1,0:T(8,128)(2,1)} %bitcast.19), channel_id=1, source_target_pairs={{0,4},{1,5},{2,6},{3,7},{4,0},{5,1},{6,2},{7,3},{8,12},{9,13},{10,... | collective-permute-start | bytes 393224 | tf_op jit(solution)/shard_map/ppermute | solution.py:213
  3.7 8.9 %collective-permute-start.2 = (bf16[128,512]{1,0:T(8,128)(2,1)}, bf16[128,512]{1,0:T(8,128)(2,1)S(1)}, u32[]{:S(2)}, u32[]{:S(2)}) collective-permute-start(bf16[128,512]{1,0:T(8,128)(2,1)} %bitcast.20), channel_id=1, source_target_pairs={{0,8},{1,9},{2,10},{3,11},{4,12},{5,13},{6,14},{7,15},{8,0},{9,1},... | collective-permute-start | bytes 393224 | tf_op jit(solution)/shard_map/ppermute | solution.py:213
  6.3 6.4 %collective-permute-start.3 = (bf16[128,512]{1,0:T(8,128)(2,1)}, bf16[128,512]{1,0:T(8,128)(2,1)S(1)}, u32[]{:S(2)}, u32[]{:S(2)}) collective-permute-start(bf16[128,512]{1,0:T(8,128)(2,1)} %bitcast.21), channel_id=1, source_target_pairs={{0,2},{1,3},{2,0},{3,1},{4,6},{5,7},{6,4},{7,5},{8,10},{9,11},{10,... | collective-permute-start | bytes 393224 | tf_op jit(solution)/shard_map/ppermute | solution.py:213
  7.8 1.0 %copy-start.2 = (bf16[1,128,2048]{2,1,0:T(8,128)(2,1)S(1)}, bf16[1,128,2048]{2,1,0:T(8,128)(2,1)}, u32[]{:S(2)}) copy-start(bf16[1,128,2048]{2,1,0:T(8,128)(2,1)} %param.5) | copy-start | bytes 1572868
  8.9 0.9 %copy-start.4 = (bf16[1,128,512]{2,1,0:T(8,128)(2,1)S(1)}, bf16[1,128,512]{2,1,0:T(8,128)(2,1)}, u32[]{:S(2)}) copy-start(bf16[1,128,512]{2,1,0:T(8,128)(2,1)} %param.9) | copy-start | bytes 393220
  9.8 12.6 %copy-start.5 = (bf16[1,128,2048]{2,1,0:T(8,128)(2,1)S(1)}, bf16[1,128,2048]{2,1,0:T(8,128)(2,1)}, u32[]{:S(2)}) copy-start(bf16[1,128,2048]{2,1,0:T(8,128)(2,1)} %param.6) | copy-start | bytes 1572868
  10.2 11.6 %collective-permute-start.1 = (bf16[2,4,128,128]{3,2,1,0:T(8,128)(2,1)S(1)}, bf16[2,4,128,128]{3,2,1,0:T(8,128)(2,1)S(1)}, u32[]{:S(2)}, u32[]{:S(2)}) collective-permute-start(bf16[2,4,128,128]{3,2,1,0:T(8,128)(2,1)S(1)} %get-tuple-element.59), channel_id=1, source_target_pairs={{0,1},{1,0},{2,3},{3,2},{4,5},{5,4},{6,7},{7,6},{8,9},{9,8},{10,11... | collective-permute-start | bytes 786440 | tf_op jit(solution)/shard_map/ppermute | solution.py:213
  10.3 7.8 %collective-permute-start.4 = (bf16[128,512]{1,0:T(8,128)(2,1)S(1)}, bf16[128,512]{1,0:T(8,128)(2,1)S(1)}, u32[]{:S(2)}, u32[]{:S(2)}) collective-permute-start(bf16[128,512]{1,0:T(8,128)(2,1)S(1)} %collective-permute-done.refs_2_), channel_id=1, source_target_pairs={{0,2},{1,3},{2,0},{3,1},{4,6},{5,7},{6,4},{7,5},{8,10},{9,11},{10,... | collective-permute-start | bytes 393224 | tf_op jit(solution)/shard_map/ppermute | solution.py:213
  12.7 9.2 %collective-permute-start.5 = (bf16[128,512]{1,0:T(8,128)(2,1)S(1)}, bf16[128,512]{1,0:T(8,128)(2,1)S(1)}, u32[]{:S(2)}, u32[]{:S(2)}) collective-permute-start(bf16[128,512]{1,0:T(8,128)(2,1)S(1)} %collective-permute-done.2.refs_4_), channel_id=1, source_target_pairs={{0,2},{1,3},{2,0},{3,1},{4,6},{5,7},{6,4},{7,5},{8,10},{9,11},{10,... | collective-permute-start | bytes 393224 | tf_op jit(solution)/shard_map/ppermute | solution.py:213
  14.2 7.6 %collective-permute-start.7 = (bf16[128,512]{1,0:T(8,128)(2,1)S(1)}, bf16[128,512]{1,0:T(8,128)(2,1)S(1)}, u32[]{:S(2)}, u32[]{:S(2)}) collective-permute-start(bf16[128,512]{1,0:T(8,128)(2,1)S(1)} %collective-permute-done.2.refs_4_), channel_id=1, source_target_pairs={{0,6},{1,7},{2,4},{3,5},{4,2},{5,3},{6,0},{7,1},{8,14},{9,15},{10,... | collective-permute-start | bytes 393224 | tf_op jit(solution)/shard_map/ppermute | solution.py:213
  14.6 7.3 %collective-permute-start.6 = (bf16[128,512]{1,0:T(8,128)(2,1)S(1)}, bf16[128,512]{1,0:T(8,128)(2,1)S(1)}, u32[]{:S(2)}, u32[]{:S(2)}) collective-permute-start(bf16[128,512]{1,0:T(8,128)(2,1)S(1)} %collective-permute-done.2.refs_4_), channel_id=1, source_target_pairs={{0,4},{1,5},{2,6},{3,7},{4,0},{5,1},{6,2},{7,3},{8,12},{9,13},{10,... | collective-permute-start | bytes 393224 | tf_op jit(solution)/shard_map/ppermute | solution.py:213
  22.3 1.6 %collective-permute-start.8 = (f32[128,512]{1,0:T(8,128)S(1)}, f32[128,512]{1,0:T(8,128)S(1)}, u32[]{:S(2)}, u32[]{:S(2)}) collective-permute-start(f32[128,512]{1,0:T(8,128)S(1)} %get-tuple-element.67), channel_id=1, source_target_pairs={{0,1},{1,0},{2,3},{3,2},{4,5},{5,4},{6,7},{7,6},{8,9},{9,8},{10,11... | collective-permute-start | bytes 786440 | tf_op jit(solution)/shard_map/ppermute | solution.py:213
  22.4 15.6 %collective-permute-start.13 = (bf16[1,128,2048]{2,1,0:T(8,128)(2,1)S(1)}, bf16[1,128,2048]{2,1,0:T(8,128)(2,1)S(1)}, u32[]{:S(2)}, u32[]{:S(2)}) collective-permute-start(bf16[1,128,2048]{2,1,0:T(8,128)(2,1)S(1)} %copy-done.5), channel_id=1, source_target_pairs={{16,0},{0,16},{17,1},{1,17},{18,2},{2,18},{19,3},{3,19},{20,4},{4,... | collective-permute-start | bytes 1572872 | tf_op jit(solution)/shard_map/ppermute | solution.py:218
  24.0 3.6 %collective-permute-start.9 = (bf16[128,512]{1,0:T(8,128)(2,1)S(1)}, bf16[128,512]{1,0:T(8,128)(2,1)S(1)}, u32[]{:S(2)}, u32[]{:S(2)}) collective-permute-start(bf16[128,512]{1,0:T(8,128)(2,1)S(1)} %add_convert_fusion.1.own_ref), channel_id=1, source_target_pairs={{0,1},{1,0},{2,3},{3,2},{4,5},{5,4},{6,7},{7,6},{8,9},{9,8},{10,11... | collective-permute-start | bytes 393224 | tf_op jit(solution)/shard_map/ppermute | solution.py:213
  24.2 7.2 %collective-permute-start.10 = (bf16[128,512]{1,0:T(8,128)(2,1)S(1)}, bf16[128,512]{1,0:T(8,128)(2,1)S(1)}, u32[]{:S(2)}, u32[]{:S(2)}) collective-permute-start(bf16[128,512]{1,0:T(8,128)(2,1)S(1)} %add_convert_fusion.1.own_ref), channel_id=1, source_target_pairs={{0,15},{1,2},{2,1},{3,4},{4,3},{5,6},{6,5},{7,8},{8,7},{9,10},{10,... | collective-permute-start | bytes 393224 | tf_op jit(solution)/shard_map/ppermute | solution.py:224
  28.6 9.4 %collective-permute-start.11 = (bf16[4,128,128]{2,1,0:T(8,128)(2,1)S(1)}, bf16[4,128,128]{2,1,0:T(8,128)(2,1)S(1)}, u32[]{:S(2)}, u32[]{:S(2)}) collective-permute-start(bf16[4,128,128]{2,1,0:T(8,128)(2,1)S(1)} %get-tuple-element.79), channel_id=1, source_target_pairs={{0,2},{1,3},{2,0},{3,1},{4,6},{5,7},{6,4},{7,5},{8,10},{9,11},{10,... | collective-permute-start | bytes 393224 | tf_op jit(solution)/shard_map/ppermute | solution.py:213
  28.6 9.3 %collective-permute-start.12 = (bf16[4,128,128]{2,1,0:T(8,128)(2,1)S(1)}, bf16[4,128,128]{2,1,0:T(8,128)(2,1)S(1)}, u32[]{:S(2)}, u32[]{:S(2)}) collective-permute-start(bf16[4,128,128]{2,1,0:T(8,128)(2,1)S(1)} %get-tuple-element.80), channel_id=1, source_target_pairs={{0,3},{1,2},{2,1},{3,0},{4,7},{5,6},{6,5},{7,4},{8,11},{9,10},{10,... | collective-permute-start | bytes 393224 | tf_op jit(solution)/shard_map/ppermute | solution.py:213
  32.6 7.2 %collective-permute-start.15 = (bf16[128,512]{1,0:T(8,128)(2,1)S(1)}, bf16[128,512]{1,0:T(8,128)(2,1)S(1)}, u32[]{:S(2)}, u32[]{:S(2)}) collective-permute-start(bf16[128,512]{1,0:T(8,128)(2,1)S(1)} %get-tuple-element.87), channel_id=1, source_target_pairs={{0,15},{1,2},{2,1},{3,4},{4,3},{5,6},{6,5},{7,8},{8,7},{9,10},{10,... | collective-permute-start | bytes 393224 | tf_op jit(solution)/shard_map/ppermute | solution.py:224
  38.0 13.4 %copy-start.3 = (bf16[1,128,2048]{2,1,0:T(8,128)(2,1)S(1)}, bf16[1,128,2048]{2,1,0:T(8,128)(2,1)}, u32[]{:S(2)}) copy-start(bf16[1,128,2048]{2,1,0:T(8,128)(2,1)} %param.5) | copy-start | bytes 1572868
  38.0 1.8 %collective-permute-start.14 = (bf16[128,512]{1,0:T(8,128)(2,1)S(1)}, bf16[128,512]{1,0:T(8,128)(2,1)S(1)}, u32[]{:S(2)}, u32[]{:S(2)}) collective-permute-start(bf16[128,512]{1,0:T(8,128)(2,1)S(1)} %get-tuple-element.86), channel_id=1, source_target_pairs={{0,1},{1,0},{2,3},{3,2},{4,5},{5,4},{6,7},{7,6},{8,9},{9,8},{10,11... | collective-permute-start | bytes 393224 | tf_op jit(solution)/shard_map/ppermute | solution.py:213
  39.8 5.3 %collective-permute-start.17 = (bf16[128,512]{1,0:T(8,128)(2,1)S(1)}, bf16[128,512]{1,0:T(8,128)(2,1)S(1)}, u32[]{:S(2)}, u32[]{:S(2)}) collective-permute-start(bf16[128,512]{1,0:T(8,128)(2,1)S(1)} %add_convert_fusion.refs_3_.own_ref), channel_id=1, source_target_pairs={{0,2},{1,3},{2,0},{3,1},{4,6},{5,7},{6,4},{7,5},{8,10},{9,11},{10,... | collective-permute-start | bytes 393224 | tf_op jit(solution)/shard_map/ppermute | solution.py:213
  39.9 5.2 %collective-permute-start.16 = (bf16[128,512]{1,0:T(8,128)(2,1)S(1)}, bf16[128,512]{1,0:T(8,128)(2,1)S(1)}, u32[]{:S(2)}, u32[]{:S(2)}) collective-permute-start(bf16[128,512]{1,0:T(8,128)(2,1)S(1)} %add_convert_fusion.refs_3_.own_ref), channel_id=1, source_target_pairs={{0,1},{1,0},{2,3},{3,2},{4,5},{5,4},{6,7},{7,6},{8,9},{9,8},{10,11... | collective-permute-start | bytes 393224 | tf_op jit(solution)/shard_map/ppermute | solution.py:213
  45.1 1.3 %collective-permute-start.18 = (bf16[128,512]{1,0:T(8,128)(2,1)S(1)}, bf16[128,512]{1,0:T(8,128)(2,1)S(1)}, u32[]{:S(2)}, u32[]{:S(2)}) collective-permute-start(bf16[128,512]{1,0:T(8,128)(2,1)S(1)} %collective-permute-done.17.refs_5_), channel_id=1, source_target_pairs={{0,1},{1,0},{2,3},{3,2},{4,5},{5,4},{6,7},{7,6},{8,9},{9,8},{10,11... | collective-permute-start | bytes 393224 | tf_op jit(solution)/shard_map/ppermute | solution.py:213
  45.8 5.6 %collective-permute-start.22 = (bf16[8,128,128]{2,1,0:T(8,128)(2,1)S(1)}, bf16[8,128,128]{2,1,0:T(8,128)(2,1)S(1)}, u32[]{:S(2)}, u32[]{:S(2)}) collective-permute-start(bf16[8,128,128]{2,1,0:T(8,128)(2,1)S(1)} %get-tuple-element.94), channel_id=1, source_target_pairs={{0,1},{1,0},{2,3},{3,2},{4,5},{5,4},{6,7},{7,6},{8,9},{9,8},{10,11... | collective-permute-start | bytes 786440 | tf_op jit(solution)/shard_map/ppermute | solution.py:213
  46.9 11.6 %collective-permute-start.19 = (bf16[128,512]{1,0:T(8,128)(2,1)S(1)}, bf16[128,512]{1,0:T(8,128)(2,1)S(1)}, u32[]{:S(2)}, u32[]{:S(2)}) collective-permute-start(bf16[128,512]{1,0:T(8,128)(2,1)S(1)} %get-tuple-element.88), channel_id=1, source_target_pairs={{0,8},{1,9},{2,10},{3,11},{4,12},{5,13},{6,14},{7,15},{8,0},{9,1},... | collective-permute-start | bytes 393224 | tf_op jit(solution)/shard_map/ppermute | solution.py:213
  47.3 11.4 %collective-permute-start.20 = (bf16[128,512]{1,0:T(8,128)(2,1)S(1)}, bf16[128,512]{1,0:T(8,128)(2,1)S(1)}, u32[]{:S(2)}, u32[]{:S(2)}) collective-permute-start(bf16[128,512]{1,0:T(8,128)(2,1)S(1)} %get-tuple-element.89), channel_id=1, source_target_pairs={{0,4},{1,5},{2,6},{3,7},{4,0},{5,1},{6,2},{7,3},{8,12},{9,13},{10,... | collective-permute-start | bytes 393224 | tf_op jit(solution)/shard_map/ppermute | solution.py:213
  49.3 9.3 %collective-permute-start.21 = (bf16[128,512]{1,0:T(8,128)(2,1)S(1)}, bf16[128,512]{1,0:T(8,128)(2,1)S(1)}, u32[]{:S(2)}, u32[]{:S(2)}) collective-permute-start(bf16[128,512]{1,0:T(8,128)(2,1)S(1)} %get-tuple-element.90), channel_id=1, source_target_pairs={{0,12},{1,13},{2,14},{3,15},{4,8},{5,9},{6,10},{7,11},{8,4},{9,5},... | collective-permute-start | bytes 393224 | tf_op jit(solution)/shard_map/ppermute | solution.py:213

commit v7 on v6

--- a/solution.py
+++ b/solution.py
@@ -55,9 +55,8 @@
 
 
 def kv_kernel(me_ref, near_ref, lent_ref, *refs):
-    weights, own_ref, beside_ref = refs[:-2], refs[-2], refs[-1]
+    weights, out_ref = refs[:-1], refs[-1]
     own = me_ref[0] // 4
-    rows = own_ref.shape[0]
     total = None
     for zz in range(len(weights) // 2):
         at = own ^ zz
@@ -65,8 +64,7 @@
         rhs = jnp.concatenate([weights[2 * zz][...], weights[2 * zz + 1][...]], axis=0)
         part = f32dot(jnp.concatenate(lhs, axis=1), rhs)
         total = part if total is None else total + part
-    own_ref[...] = total[:rows]
-    beside_ref[...] = total[rows:]
+    out_ref[...] = total
 
 
 def head_rows(ref, block, size):
@@ -224,6 +222,12 @@
     return lax.ppermute(block, "ctx", route)
 
 
+def passed(block):
+    count = lax.axis_size("ctx")
+    route = [(i, (i - 2) % count if i % 2 else (i + 2) % count) for i in range(count)]
+    return lax.ppermute(block, "ctx", route)
+
+
 def gathered(block, pieces):
     count = lax.axis_size("ctx")
     first = count // 2
@@ -265,10 +269,11 @@
     upstream = shifted(grad_in, "pipe", -1)[0]
     partial = ((rows, kv2), f32)
     half = ((rows, kv2), bf16)
-    kv, kv_lent = call(kv_kernel, [partial, partial], [me, near, lent, *weights])
-    kv = (kv + swap(kv_lent, 1)).astype(bf16)
-    across = crossed(kv)
-    beside = swap(kv, 1)
+    (both,) = call(kv_kernel, [((2 * rows, kv2), f32)], [me, near, lent, *weights])
+    other = swap(both, 1)
+    kv = (both[:rows] + other[rows:]).astype(bf16)
+    beside = (both[rows:] + other[:rows]).astype(bf16)
+    across = passed(beside)
     pairs = model // (BATCH * HEAD_DIM)
     block = ((pairs, 2 * rows, BATCH * rows), f32)
     lifted, weighted, stats = call(
@@ -289,7 +294,8 @@
         [((rows, model), bf16), half, partial],
         [queries[0], d_heads[0], beside, kv, across, lifted, weighted, kept, far],
     )
-    d_beside, turned, upstream = lax.optimization_barrier((d_beside, turned, upstream))
+    d_beside, turned = lax.optimization_barrier((d_beside, turned))
+    from_across, upstream = lax.optimization_barrier((from_across, upstream))
     from_beside = swap(d_beside, 1)
     d_kv = (d_own + from_beside.astype(f32) + from_across.astype(f32)).astype(bf16)
     above = swap(d_kv, 2)

time: 59.9 us -> 60.1 us (level)
  waiting for transfers between devices: 22.7 us -> 23.6 us
    ppermute x2 -> x1, starting transfers between devices: 6.81 us -> 2.08 us  [crossed(): return lax.ppermute(block, 'ctx', route)]
    ppermute x20 -> x19, starting transfers between devices: 17.2 us -> 20.7 us  [swap(): return lax.ppermute(block, 'ctx', [(i, i ^ distance) for i in range(count)])]
    ppermute x0 -> x1, waiting for transfers between devices: none -> 2.11 us  [passed(): return lax.ppermute(block, 'ctx', route)]
    ppermute x2 -> x1, waiting for transfers between devices: 4.36 us -> 2.65 us  [crossed(): return lax.ppermute(block, 'ctx', route)]
    ppermute x0 -> x1, starting transfers between devices: none -> 0.84 us  [passed(): return lax.ppermute(block, 'ctx', route)]
    ppermute x20 -> x19, waiting for transfers between devices: 18.3 us -> 18.9 us  [swap(): return lax.ppermute(block, 'ctx', [(i, i ^ distance) for i in range(count)])]
  transfers between devices with their start and end apart: 23 -> 22, of which waited for: 9 -> 11; matrix products, arithmetic and copies ran while one was open for 0% -> 0% of each run, Pallas kernels for 12% -> 12%
where the time goes in v7:
time: 60.1 us; the launch traced here: 59.9 us
  starting transfers between devices  25.2 us (42%)
  waiting for transfers between devices  23.6 us (39%)
  Pallas kernels  7.49 us (12%)
  local copies, waits for them, and re-layouts  1.96 us (3%)
  other arithmetic  0.91 us (2%)
  between operations  0.78 us (1%)
    ppermute x19, starting transfers between devices, swap(): return lax.ppermute(block, 'ctx', [(i, i ^ distance) for i in range(count)])  20.7 us
    ppermute x19, waiting for transfers between devices, swap(): return lax.ppermute(block, 'ctx', [(i, i ^ distance) for i in range(count)])  18.9 us
    pallas_call x8, Pallas kernels, call(): pl.pallas_call(kernel, out_shape=[jax.ShapeDtypeStruct(s, d) for s, d in...  7.49 us
    ppermute x1, waiting for transfers between devices, crossed(): return lax.ppermute(block, 'ctx', route)  2.65 us
    ppermute x1, waiting for transfers between devices, passed(): return lax.ppermute(block, 'ctx', route)  2.11 us
    ppermute x1, starting transfers between devices, crossed(): return lax.ppermute(block, 'ctx', route)  2.08 us
    unnamed x12, local copies, waits for them, and re-layouts  1.96 us
    ppermute x1, starting transfers between devices, shifted(): lax.ppermute(block, axis, [((i - distance) % count, i) for i in range(cou...  1.56 us
  transfers between devices with their start and end apart: 22, of which 11 were waited for; matrix products, arithmetic and copies ran while one was open for 0% of the time, Pallas kernels for 12%

profile of v7, /device:TPU:0, one launch (start us, length us, event | category | flops | bytes accessed | tf_op | source)
XLA Modules:
  0.0 59.9 jit_solution(8349962123917562974)
XLA Ops:
  0.7 3.1 %collective-permute-start = (bf16[128,512]{1,0:T(8,128)(2,1)}, bf16[128,512]{1,0:T(8,128)(2,1)S(1)}, u32[]{:S(2)}, u32[]{:S(2)}) collective-permute-start(bf16[128,512]{1,0:T(8,128)(2,1)} %bitcast.19), channel_id=1, source_target_pairs={{0,4},{1,5},{2,6},{3,7},{4,0},{5,1},{6,2},{7,3},{8,12},{9,13},{10,... | collective-permute-start | bytes 393224 | tf_op jit(solution)/shard_map/ppermute | solution.py:211
  3.7 2.6 %collective-permute-start.2 = (bf16[128,512]{1,0:T(8,128)(2,1)}, bf16[128,512]{1,0:T(8,128)(2,1)S(1)}, u32[]{:S(2)}, u32[]{:S(2)}) collective-permute-start(bf16[128,512]{1,0:T(8,128)(2,1)} %bitcast.20), channel_id=1, source_target_pairs={{0,8},{1,9},{2,10},{3,11},{4,12},{5,13},{6,14},{7,15},{8,0},{9,1},... | collective-permute-start | bytes 393224 | tf_op jit(solution)/shard_map/ppermute | solution.py:211
  6.3 1.5 %collective-permute-start.3 = (bf16[128,512]{1,0:T(8,128)(2,1)}, bf16[128,512]{1,0:T(8,128)(2,1)S(1)}, u32[]{:S(2)}, u32[]{:S(2)}) collective-permute-start(bf16[128,512]{1,0:T(8,128)(2,1)} %bitcast.21), channel_id=1, source_target_pairs={{0,2},{1,3},{2,0},{3,1},{4,6},{5,7},{6,4},{7,5},{8,10},{9,11},{10,... | collective-permute-start | bytes 393224 | tf_op jit(solution)/shard_map/ppermute | solution.py:211
  7.9 1.0 %copy-done.2 = bf16[1,128,2048]{2,1,0:T(8,128)(2,1)S(1)} copy-done((bf16[1,128,2048]{2,1,0:T(8,128)(2,1)S(1)}, bf16[1,128,2048]{2,1,0:T(8,128)(2,1)}, u32[]{:S(2)}) %copy-start.2) | copy-done | bytes 524312
  8.9 0.9 %copy-done.4 = bf16[1,128,512]{2,1,0:T(8,128)(2,1)S(1)} copy-done((bf16[1,128,512]{2,1,0:T(8,128)(2,1)S(1)}, bf16[1,128,512]{2,1,0:T(8,128)(2,1)}, u32[]{:S(2)}) %copy-start.4) | copy-done | bytes 131096
  10.3 0.8 %collective-permute-start.4 = (bf16[128,512]{1,0:T(8,128)(2,1)S(1)}, bf16[128,512]{1,0:T(8,128)(2,1)S(1)}, u32[]{:S(2)}, u32[]{:S(2)}) collective-permute-start(bf16[128,512]{1,0:T(8,128)(2,1)S(1)} %collective-permute-done.refs_2_), channel_id=1, source_target_pairs={{0,2},{1,3},{2,0},{3,1},{4,6},{5,7},{6,4},{7,5},{8,10},{9,11},{10,... | collective-permute-start | bytes 393224 | tf_op jit(solution)/shard_map/ppermute | solution.py:211
  11.1 1.6 %collective-permute-done.2.refs_4_ = bf16[128,512]{1,0:T(8,128)(2,1)S(1)} collective-permute-done((bf16[128,512]{1,0:T(8,128)(2,1)}, bf16[128,512]{1,0:T(8,128)(2,1)S(1)}, u32[]{:S(2)}, u32[]{:S(2)}) %collective-permute-start.2) | collective-permute-done | bytes 131104 | tf_op jit(solution)/shard_map/ppermute | solution.py:211
  12.7 1.5 %collective-permute-start.5 = (bf16[128,512]{1,0:T(8,128)(2,1)S(1)}, bf16[128,512]{1,0:T(8,128)(2,1)S(1)}, u32[]{:S(2)}, u32[]{:S(2)}) collective-permute-start(bf16[128,512]{1,0:T(8,128)(2,1)S(1)} %collective-permute-done.2.refs_4_), channel_id=1, source_target_pairs={{0,2},{1,3},{2,0},{3,1},{4,6},{5,7},{6,4},{7,5},{8,10},{9,11},{10,... | collective-permute-start | bytes 393224 | tf_op jit(solution)/shard_map/ppermute | solution.py:211
  14.6 1.5 %collective-permute-start.7 = (bf16[128,512]{1,0:T(8,128)(2,1)S(1)}, bf16[128,512]{1,0:T(8,128)(2,1)S(1)}, u32[]{:S(2)}, u32[]{:S(2)}) collective-permute-start(bf16[128,512]{1,0:T(8,128)(2,1)S(1)} %collective-permute-done.2.refs_4_), channel_id=1, source_target_pairs={{0,6},{1,7},{2,4},{3,5},{4,2},{5,3},{6,0},{7,1},{8,14},{9,15},{10,... | collective-permute-start | bytes 393224 | tf_op jit(solution)/shard_map/ppermute | solution.py:211
  16.2 1.8 %collective-permute-done.4.refs_3_ = bf16[128,512]{1,0:T(8,128)(2,1)S(1)} collective-permute-done((bf16[128,512]{1,0:T(8,128)(2,1)S(1)}, bf16[128,512]{1,0:T(8,128)(2,1)S(1)}, u32[]{:S(2)}, u32[]{:S(2)}) %collective-permute-start.4) | collective-permute-done | bytes 131104 | tf_op jit(solution)/shard_map/ppermute | solution.py:211
  18.0 3.9 %collective-permute-done.5.refs_5_ = bf16[128,512]{1,0:T(8,128)(2,1)S(1)} collective-permute-done((bf16[128,512]{1,0:T(8,128)(2,1)S(1)}, bf16[128,512]{1,0:T(8,128)(2,1)S(1)}, u32[]{:S(2)}, u32[]{:S(2)}) %collective-permute-start.5) | collective-permute-done | bytes 131104 | tf_op jit(solution)/shard_map/ppermute | solution.py:211
  22.4 1.6 %collective-permute-start.14 = (bf16[1,128,2048]{2,1,0:T(8,128)(2,1)S(1)}, bf16[1,128,2048]{2,1,0:T(8,128)(2,1)S(1)}, u32[]{:S(2)}, u32[]{:S(2)}) collective-permute-start(bf16[1,128,2048]{2,1,0:T(8,128)(2,1)S(1)} %copy-done.5), channel_id=1, source_target_pairs={{16,0},{0,16},{17,1},{1,17},{18,2},{2,18},{19,3},{3,19},{20,4},{4,... | collective-permute-start | bytes 1572872 | tf_op jit(solution)/shard_map/ppermute | solution.py:216
  24.4 0.8 %collective-permute-start.9 = (bf16[128,512]{1,0:T(8,128)(2,1)S(1)}, bf16[128,512]{1,0:T(8,128)(2,1)S(1)}, u32[]{:S(2)}, u32[]{:S(2)}) collective-permute-start(bf16[128,512]{1,0:T(8,128)(2,1)S(1)} %get-tuple-element.100.beside_ref), channel_id=1, source_target_pairs={{0,2},{1,15},{2,4},{3,1},{4,6},{5,3},{6,8},{7,5},{8,10},{9,7},{10,... | collective-permute-start | bytes 393224 | tf_op jit(solution)/shard_map/ppermute | solution.py:228
  25.2 1.0 %shard_map.78 = (f32[2,256,1024]{2,1,0:T(8,128)S(1)}, f32[2,256,1024]{2,1,0:T(8,128)S(1)}, f32[2,3,1024]{2,1,0:T(4,128)S(1)}) custom-call(s32[1]{0:T(128)} %bitcast.me_ref, bf16[128,2048]{1,0:T(8,128)(2,1)S(1)} %bitcast.10, bf16[128,2048]{1,0:T(8,128)(2,1)S(1)} %bitcast.13, bf16[128,512]{1,0:T(8,128)(2,1)S(1)} %get-tuple-element.100.beside_ref, ...), custom_call_target="tpu_custom_call" | custom-call | tf_op jit(solution)/shard_map/pallas_call | solution.py:27
  26.2 1.2 %collective-permute-start.10 = (bf16[4,128,128]{2,1,0:T(8,128)(2,1)S(1)}, bf16[4,128,128]{2,1,0:T(8,128)(2,1)S(1)}, u32[]{:S(2)}, u32[]{:S(2)}) collective-permute-start(bf16[4,128,128]{2,1,0:T(8,128)(2,1)S(1)} %get-tuple-element.76), channel_id=1, source_target_pairs={{0,2},{1,3},{2,0},{3,1},{4,6},{5,7},{6,4},{7,5},{8,10},{9,11},{10,... | collective-permute-start | bytes 393224 | tf_op jit(solution)/shard_map/ppermute | solution.py:211
  27.4 2.7 %collective-permute-start.11 = (bf16[4,128,128]{2,1,0:T(8,128)(2,1)S(1)}, bf16[4,128,128]{2,1,0:T(8,128)(2,1)S(1)}, u32[]{:S(2)}, u32[]{:S(2)}) collective-permute-start(bf16[4,128,128]{2,1,0:T(8,128)(2,1)S(1)} %get-tuple-element.77), channel_id=1, source_target_pairs={{0,3},{1,2},{2,1},{3,0},{4,7},{5,6},{6,5},{7,4},{8,11},{9,10},{10,... | collective-permute-start | bytes 393224 | tf_op jit(solution)/shard_map/ppermute | solution.py:211
  30.1 2.1 %collective-permute-done.9.across_ref = bf16[128,512]{1,0:T(8,128)(2,1)S(1)} collective-permute-done((bf16[128,512]{1,0:T(8,128)(2,1)S(1)}, bf16[128,512]{1,0:T(8,128)(2,1)S(1)}, u32[]{:S(2)}, u32[]{:S(2)}) %collective-permute-start.9) | collective-permute-done | bytes 131104 | tf_op jit(solution)/shard_map/ppermute | solution.py:228
  32.2 1.2 %shard_map.79 = (bf16[128,512]{1,0:T(8,128)(2,1)S(1)}, bf16[2,128,1024]{2,1,0:T(8,128)(2,1)S(1)}, f32[2,2,1024]{2,1,0:T(2,128)S(1)}) custom-call(s32[1]{0:T(128)} %bitcast.me_ref, bf16[128,2048]{1,0:T(8,128)(2,1)S(1)} %bitcast.11, bf16[128,2048]{1,0:T(8,128)(2,1)S(1)} %bitcast.14, bf16[128,512]{1,0:T(8,128)(2,1)S(1)} %collective-permute-done.9.across_ref, ...), custom_call_target="tpu_custom_call" | custom-call | tf_op jit(solution)/shard_map/pallas_call | solution.py:27
  33.4 2.1 %collective-permute-start.13 = (bf16[128,512]{1,0:T(8,128)(2,1)S(1)}, bf16[128,512]{1,0:T(8,128)(2,1)S(1)}, u32[]{:S(2)}, u32[]{:S(2)}) collective-permute-start(bf16[128,512]{1,0:T(8,128)(2,1)S(1)} %get-tuple-element.83), channel_id=1, source_target_pairs={{0,15},{1,2},{2,1},{3,4},{4,3},{5,6},{6,5},{7,8},{8,7},{9,10},{10,... | collective-permute-start | bytes 393224 | tf_op jit(solution)/shard_map/ppermute | solution.py:222
  35.5 1.9 %shard_map.80 = (bf16[128,2048]{1,0:T(8,128)(2,1)}, bf16[128,512]{1,0:T(8,128)(2,1)S(1)}, f32[128,512]{1,0:T(8,128)S(1)}) custom-call(bf16[128,2048]{1,0:T(8,128)(2,1)S(1)} %bitcast.12, bf16[128,2048]{1,0:T(8,128)(2,1)S(1)} %bitcast.15, bf16[128,512]{1,0:T(8,128)(2,1)S(1)} %get-tuple-element.100.beside_ref, bf16[128,512]{1,0:T(8,128)(2,1)S(1)} %get-tuple-element.99.own_ref, ...), custom_call_target="tpu_custom_call" | custom-call | tf_op jit(solution)/shard_map/pallas_call | solution.py:27
  37.4 0.5 collective-permute-done.11.refs_2_
  37.9 2.6 %collective-permute-done.13 = bf16[128,512]{1,0:T(8,128)(2,1)S(1)} collective-permute-done((bf16[128,512]{1,0:T(8,128)(2,1)S(1)}, bf16[128,512]{1,0:T(8,128)(2,1)S(1)}, u32[]{:S(2)}, u32[]{:S(2)}) %collective-permute-start.13) | collective-permute-done | bytes 131104 | tf_op jit(solution)/shard_map/ppermute | solution.py:222
  40.7 4.9 %collective-permute-done.16.refs_5_ = bf16[128,512]{1,0:T(8,128)(2,1)S(1)} collective-permute-done((bf16[128,512]{1,0:T(8,128)(2,1)S(1)}, bf16[128,512]{1,0:T(8,128)(2,1)S(1)}, u32[]{:S(2)}, u32[]{:S(2)}) %collective-permute-start.16) | collective-permute-done | bytes 131104 | tf_op jit(solution)/shard_map/ppermute | solution.py:211
  45.6 0.7 %shard_map.82 = (f32[8,128,128]{2,1,0:T(8,128)S(1)}, bf16[8,128,128]{2,1,0:T(8,128)(2,1)S(1)}) custom-call(bf16[128,512]{1,0:T(8,128)(2,1)S(1)} %add_convert_fusion.refs_3_.own_ref, bf16[128,512]{1,0:T(8,128)(2,1)S(1)} %collective-permute-done.15.refs_4_.beside_ref, bf16[128,512]{1,0:T(8,128)(2,1)S(1)} %get-tuple-element.60.refs_0_, ...), custom_call_target="tpu_custom_call" | custom-call | tf_op jit(solution)/shard_map/pallas_call | solution.py:27
  46.3 0.6 collective-permute-start.21
  47.0 0.5 shard_map.81
  47.4 0.8 %collective-permute-start.18 = (bf16[128,512]{1,0:T(8,128)(2,1)S(1)}, bf16[128,512]{1,0:T(8,128)(2,1)S(1)}, u32[]{:S(2)}, u32[]{:S(2)}) collective-permute-start(bf16[128,512]{1,0:T(8,128)(2,1)S(1)} %get-tuple-element.86), channel_id=1, source_target_pairs={{0,8},{1,9},{2,10},{3,11},{4,12},{5,13},{6,14},{7,15},{8,0},{9,1},... | collective-permute-start | bytes 393224 | tf_op jit(solution)/shard_map/ppermute | solution.py:211
  48.6 3.3 %collective-permute-start.20 = (bf16[128,512]{1,0:T(8,128)(2,1)S(1)}, bf16[128,512]{1,0:T(8,128)(2,1)S(1)}, u32[]{:S(2)}, u32[]{:S(2)}) collective-permute-start(bf16[128,512]{1,0:T(8,128)(2,1)S(1)} %get-tuple-element.88), channel_id=1, source_target_pairs={{0,12},{1,13},{2,14},{3,15},{4,8},{5,9},{6,10},{7,11},{8,4},{9,5},... | collective-permute-start | bytes 393224 | tf_op jit(solution)/shard_map/ppermute | solution.py:211
  51.9 1.4 %shard_map.83 = bf16[128,2048]{1,0:T(8,128)(2,1)} custom-call(s32[1]{0:T(128)} %bitcast.me_ref, bf16[128,2048]{1,0:T(8,128)(2,1)S(1)} %bitcast.17, f32[128,1]{1,0:T(8,128)S(1)} %get-tuple-element.89.factor_ref, bf16[128,2048]{1,0:T(8,128)(2,1)S(1)} %bitcast.18, f32[8,128,128]{2,1,0:T(8,128)S(1)} %get-tuple-element.91.near_ref, ...), custom_call_target="tpu_custom_call" | custom-call | tf_op jit(solution)/shard_map/pallas_call | solution.py:27
  53.3 5.0 %collective-permute-done.18 = bf16[128,512]{1,0:T(8,128)(2,1)S(1)} collective-permute-done((bf16[128,512]{1,0:T(8,128)(2,1)S(1)}, bf16[128,512]{1,0:T(8,128)(2,1)S(1)}, u32[]{:S(2)}, u32[]{:S(2)}) %collective-permute-start.18) | collective-permute-done | bytes 131104 | tf_op jit(solution)/shard_map/ppermute | solution.py:211
  58.3 0.8 %collective-permute-done.19 = bf16[128,512]{1,0:T(8,128)(2,1)S(1)} collective-permute-done((bf16[128,512]{1,0:T(8,128)(2,1)S(1)}, bf16[128,512]{1,0:T(8,128)(2,1)S(1)}, u32[]{:S(2)}, u32[]{:S(2)}) %collective-permute-start.19) | collective-permute-done | bytes 131104 | tf_op jit(solution)/shard_map/ppermute | solution.py:211
  59.2 0.8 %multiply_bitcast_fusion = f32[1,128,512]{2,1,0:T(8,128)} fusion(bf16[128,512]{1,0:T(8,128)(2,1)S(1)} %collective-permute-done.20, bf16[128,512]{1,0:T(8,128)(2,1)S(1)} %collective-permute-done.19, f32[128,512]{1,0:T(8,128)S(1)} %get-tuple-element.95, bf16[128,512]{1,0:T(8,128)(2,1)S(1)} %collective-permute-done.18), kind=kLoop, calls=%fused_computation.4 | loop fusion | flops 458752 | bytes 917504 | tf_op jit(solution)/shard_map/broadcast_in_dim | solution.py:327
  (35 shorter events, 2.5 us)
Async XLA Ops:
  0.6 24.6 %copy-start = (bf16[1,128,2048]{2,1,0:T(8,128)(2,1)S(1)}, bf16[1,128,2048]{2,1,0:T(8,128)(2,1)}, u32[]{:S(2)}) copy-start(bf16[1,128,2048]{2,1,0:T(8,128)(2,1)} %param.7) | copy-start | bytes 1572868
  0.6 24.6 %copy-start.1 = (bf16[1,128,2048]{2,1,0:T(8,128)(2,1)S(1)}, bf16[1,128,2048]{2,1,0:T(8,128)(2,1)}, u32[]{:S(2)}) copy-start(bf16[1,128,2048]{2,1,0:T(8,128)(2,1)} %param.8) | copy-start | bytes 1572868
  0.7 9.6 %collective-permute-start = (bf16[128,512]{1,0:T(8,128)(2,1)}, bf16[128,512]{1,0:T(8,128)(2,1)S(1)}, u32[]{:S(2)}, u32[]{:S(2)}) collective-permute-start(bf16[128,512]{1,0:T(8,128)(2,1)} %bitcast.19), channel_id=1, source_target_pairs={{0,4},{1,5},{2,6},{3,7},{4,0},{5,1},{6,2},{7,3},{8,12},{9,13},{10,... | collective-permute-start | bytes 393224 | tf_op jit(solution)/shard_map/ppermute | solution.py:211
  3.7 8.9 %collective-permute-start.2 = (bf16[128,512]{1,0:T(8,128)(2,1)}, bf16[128,512]{1,0:T(8,128)(2,1)S(1)}, u32[]{:S(2)}, u32[]{:S(2)}) collective-permute-start(bf16[128,512]{1,0:T(8,128)(2,1)} %bitcast.20), channel_id=1, source_target_pairs={{0,8},{1,9},{2,10},{3,11},{4,12},{5,13},{6,14},{7,15},{8,0},{9,1},... | collective-permute-start | bytes 393224 | tf_op jit(solution)/shard_map/ppermute | solution.py:211
  6.3 6.4 %collective-permute-start.3 = (bf16[128,512]{1,0:T(8,128)(2,1)}, bf16[128,512]{1,0:T(8,128)(2,1)S(1)}, u32[]{:S(2)}, u32[]{:S(2)}) collective-permute-start(bf16[128,512]{1,0:T(8,128)(2,1)} %bitcast.21), channel_id=1, source_target_pairs={{0,2},{1,3},{2,0},{3,1},{4,6},{5,7},{6,4},{7,5},{8,10},{9,11},{10,... | collective-permute-start | bytes 393224 | tf_op jit(solution)/shard_map/ppermute | solution.py:211
  7.8 1.0 %copy-start.2 = (bf16[1,128,2048]{2,1,0:T(8,128)(2,1)S(1)}, bf16[1,128,2048]{2,1,0:T(8,128)(2,1)}, u32[]{:S(2)}) copy-start(bf16[1,128,2048]{2,1,0:T(8,128)(2,1)} %param.5) | copy-start | bytes 1572868
  8.9 0.9 %copy-start.4 = (bf16[1,128,512]{2,1,0:T(8,128)(2,1)S(1)}, bf16[1,128,512]{2,1,0:T(8,128)(2,1)}, u32[]{:S(2)}) copy-start(bf16[1,128,512]{2,1,0:T(8,128)(2,1)} %param.9) | copy-start | bytes 393220
  9.8 12.6 %copy-start.5 = (bf16[1,128,2048]{2,1,0:T(8,128)(2,1)S(1)}, bf16[1,128,2048]{2,1,0:T(8,128)(2,1)}, u32[]{:S(2)}) copy-start(bf16[1,128,2048]{2,1,0:T(8,128)(2,1)} %param.6) | copy-start | bytes 1572868
  10.2 11.6 %collective-permute-start.1 = (bf16[2,4,128,128]{3,2,1,0:T(8,128)(2,1)S(1)}, bf16[2,4,128,128]{3,2,1,0:T(8,128)(2,1)S(1)}, u32[]{:S(2)}, u32[]{:S(2)}) collective-permute-start(bf16[2,4,128,128]{3,2,1,0:T(8,128)(2,1)S(1)} %get-tuple-element.58), channel_id=1, source_target_pairs={{0,1},{1,0},{2,3},{3,2},{4,5},{5,4},{6,7},{7,6},{8,9},{9,8},{10,11... | collective-permute-start | bytes 786440 | tf_op jit(solution)/shard_map/ppermute | solution.py:211
  10.3 7.7 %collective-permute-start.4 = (bf16[128,512]{1,0:T(8,128)(2,1)S(1)}, bf16[128,512]{1,0:T(8,128)(2,1)S(1)}, u32[]{:S(2)}, u32[]{:S(2)}) collective-permute-start(bf16[128,512]{1,0:T(8,128)(2,1)S(1)} %collective-permute-done.refs_2_), channel_id=1, source_target_pairs={{0,2},{1,3},{2,0},{3,1},{4,6},{5,7},{6,4},{7,5},{8,10},{9,11},{10,... | collective-permute-start | bytes 393224 | tf_op jit(solution)/shard_map/ppermute | solution.py:211
  12.7 9.2 %collective-permute-start.5 = (bf16[128,512]{1,0:T(8,128)(2,1)S(1)}, bf16[128,512]{1,0:T(8,128)(2,1)S(1)}, u32[]{:S(2)}, u32[]{:S(2)}) collective-permute-start(bf16[128,512]{1,0:T(8,128)(2,1)S(1)} %collective-permute-done.2.refs_4_), channel_id=1, source_target_pairs={{0,2},{1,3},{2,0},{3,1},{4,6},{5,7},{6,4},{7,5},{8,10},{9,11},{10,... | collective-permute-start | bytes 393224 | tf_op jit(solution)/shard_map/ppermute | solution.py:211
  14.2 7.6 %collective-permute-start.6 = (bf16[128,512]{1,0:T(8,128)(2,1)S(1)}, bf16[128,512]{1,0:T(8,128)(2,1)S(1)}, u32[]{:S(2)}, u32[]{:S(2)}) collective-permute-start(bf16[128,512]{1,0:T(8,128)(2,1)S(1)} %collective-permute-done.2.refs_4_), channel_id=1, source_target_pairs={{0,4},{1,5},{2,6},{3,7},{4,0},{5,1},{6,2},{7,3},{8,12},{9,13},{10,... | collective-permute-start | bytes 393224 | tf_op jit(solution)/shard_map/ppermute | solution.py:211
  14.6 7.2 %collective-permute-start.7 = (bf16[128,512]{1,0:T(8,128)(2,1)S(1)}, bf16[128,512]{1,0:T(8,128)(2,1)S(1)}, u32[]{:S(2)}, u32[]{:S(2)}) collective-permute-start(bf16[128,512]{1,0:T(8,128)(2,1)S(1)} %collective-permute-done.2.refs_4_), channel_id=1, source_target_pairs={{0,6},{1,7},{2,4},{3,5},{4,2},{5,3},{6,0},{7,1},{8,14},{9,15},{10,... | collective-permute-start | bytes 393224 | tf_op jit(solution)/shard_map/ppermute | solution.py:211
  22.3 2.0 %collective-permute-start.8 = (f32[256,512]{1,0:T(8,128)S(1)}, f32[256,512]{1,0:T(8,128)S(1)}, u32[]{:S(2)}, u32[]{:S(2)}) collective-permute-start(f32[256,512]{1,0:T(8,128)S(1)} %shard_map.77), channel_id=1, source_target_pairs={{0,1},{1,0},{2,3},{3,2},{4,5},{5,4},{6,7},{7,6},{8,9},{9,8},{10,11... | collective-permute-start | bytes 1572872 | tf_op jit(solution)/shard_map/ppermute | solution.py:211
  22.4 15.5 %collective-permute-start.14 = (bf16[1,128,2048]{2,1,0:T(8,128)(2,1)S(1)}, bf16[1,128,2048]{2,1,0:T(8,128)(2,1)S(1)}, u32[]{:S(2)}, u32[]{:S(2)}) collective-permute-start(bf16[1,128,2048]{2,1,0:T(8,128)(2,1)S(1)} %copy-done.5), channel_id=1, source_target_pairs={{16,0},{0,16},{17,1},{1,17},{18,2},{2,18},{19,3},{3,19},{20,4},{4,... | collective-permute-start | bytes 1572872 | tf_op jit(solution)/shard_map/ppermute | solution.py:216
  24.4 7.8 %collective-permute-start.9 = (bf16[128,512]{1,0:T(8,128)(2,1)S(1)}, bf16[128,512]{1,0:T(8,128)(2,1)S(1)}, u32[]{:S(2)}, u32[]{:S(2)}) collective-permute-start(bf16[128,512]{1,0:T(8,128)(2,1)S(1)} %get-tuple-element.100.beside_ref), channel_id=1, source_target_pairs={{0,2},{1,15},{2,4},{3,1},{4,6},{5,3},{6,8},{7,5},{8,10},{9,7},{10,... | collective-permute-start | bytes 393224 | tf_op jit(solution)/shard_map/ppermute | solution.py:228
  26.2 11.2 %collective-permute-start.10 = (bf16[4,128,128]{2,1,0:T(8,128)(2,1)S(1)}, bf16[4,128,128]{2,1,0:T(8,128)(2,1)S(1)}, u32[]{:S(2)}, u32[]{:S(2)}) collective-permute-start(bf16[4,128,128]{2,1,0:T(8,128)(2,1)S(1)} %get-tuple-element.76), channel_id=1, source_target_pairs={{0,2},{1,3},{2,0},{3,1},{4,6},{5,7},{6,4},{7,5},{8,10},{9,11},{10,... | collective-permute-start | bytes 393224 | tf_op jit(solution)/shard_map/ppermute | solution.py:211
  27.4 10.5 %collective-permute-start.11 = (bf16[4,128,128]{2,1,0:T(8,128)(2,1)S(1)}, bf16[4,128,128]{2,1,0:T(8,128)(2,1)S(1)}, u32[]{:S(2)}, u32[]{:S(2)}) collective-permute-start(bf16[4,128,128]{2,1,0:T(8,128)(2,1)S(1)} %get-tuple-element.77), channel_id=1, source_target_pairs={{0,3},{1,2},{2,1},{3,0},{4,7},{5,6},{6,5},{7,4},{8,11},{9,10},{10,... | collective-permute-start | bytes 393224 | tf_op jit(solution)/shard_map/ppermute | solution.py:211
  33.4 7.2 %collective-permute-start.13 = (bf16[128,512]{1,0:T(8,128)(2,1)S(1)}, bf16[128,512]{1,0:T(8,128)(2,1)S(1)}, u32[]{:S(2)}, u32[]{:S(2)}) collective-permute-start(bf16[128,512]{1,0:T(8,128)(2,1)S(1)} %get-tuple-element.83), channel_id=1, source_target_pairs={{0,15},{1,2},{2,1},{3,4},{4,3},{5,6},{6,5},{7,8},{8,7},{9,10},{10,... | collective-permute-start | bytes 393224 | tf_op jit(solution)/shard_map/ppermute | solution.py:222
  37.4 14.5 %copy-start.3 = (bf16[1,128,2048]{2,1,0:T(8,128)(2,1)S(1)}, bf16[1,128,2048]{2,1,0:T(8,128)(2,1)}, u32[]{:S(2)}) copy-start(bf16[1,128,2048]{2,1,0:T(8,128)(2,1)} %param.5) | copy-start | bytes 1572868
  37.9 2.7 %collective-permute-start.12 = (bf16[128,512]{1,0:T(8,128)(2,1)S(1)}, bf16[128,512]{1,0:T(8,128)(2,1)S(1)}, u32[]{:S(2)}, u32[]{:S(2)}) collective-permute-start(bf16[128,512]{1,0:T(8,128)(2,1)S(1)} %get-tuple-element.82), channel_id=1, source_target_pairs={{0,1},{1,0},{2,3},{3,2},{4,5},{5,4},{6,7},{7,6},{8,9},{9,8},{10,11... | collective-permute-start | bytes 393224 | tf_op jit(solution)/shard_map/ppermute | solution.py:211
  40.6 5.0 %collective-permute-start.16 = (bf16[128,512]{1,0:T(8,128)(2,1)S(1)}, bf16[128,512]{1,0:T(8,128)(2,1)S(1)}, u32[]{:S(2)}, u32[]{:S(2)}) collective-permute-start(bf16[128,512]{1,0:T(8,128)(2,1)S(1)} %add_convert_fusion.refs_3_.own_ref), channel_id=1, source_target_pairs={{0,2},{1,3},{2,0},{3,1},{4,6},{5,7},{6,4},{7,5},{8,10},{9,11},{10,... | collective-permute-start | bytes 393224 | tf_op jit(solution)/shard_map/ppermute | solution.py:211
  40.7 5.0 %collective-permute-start.15 = (bf16[128,512]{1,0:T(8,128)(2,1)S(1)}, bf16[128,512]{1,0:T(8,128)(2,1)S(1)}, u32[]{:S(2)}, u32[]{:S(2)}) collective-permute-start(bf16[128,512]{1,0:T(8,128)(2,1)S(1)} %add_convert_fusion.refs_3_.own_ref), channel_id=1, source_target_pairs={{0,1},{1,0},{2,3},{3,2},{4,5},{5,4},{6,7},{7,6},{8,9},{9,8},{10,11... | collective-permute-start | bytes 393224 | tf_op jit(solution)/shard_map/ppermute | solution.py:211
  45.6 1.3 %collective-permute-start.17 = (bf16[128,512]{1,0:T(8,128)(2,1)S(1)}, bf16[128,512]{1,0:T(8,128)(2,1)S(1)}, u32[]{:S(2)}, u32[]{:S(2)}) collective-permute-start(bf16[128,512]{1,0:T(8,128)(2,1)S(1)} %collective-permute-done.16.refs_5_), channel_id=1, source_target_pairs={{0,1},{1,0},{2,3},{3,2},{4,5},{5,4},{6,7},{7,6},{8,9},{9,8},{10,11... | collective-permute-start | bytes 393224 | tf_op jit(solution)/shard_map/ppermute | solution.py:211
  46.3 5.6 %collective-permute-start.21 = (bf16[8,128,128]{2,1,0:T(8,128)(2,1)S(1)}, bf16[8,128,128]{2,1,0:T(8,128)(2,1)S(1)}, u32[]{:S(2)}, u32[]{:S(2)}) collective-permute-start(bf16[8,128,128]{2,1,0:T(8,128)(2,1)S(1)} %get-tuple-element.92), channel_id=1, source_target_pairs={{0,1},{1,0},{2,3},{3,2},{4,5},{5,4},{6,7},{7,6},{8,9},{9,8},{10,11... | collective-permute-start | bytes 786440 | tf_op jit(solution)/shard_map/ppermute | solution.py:211
  47.4 10.9 %collective-permute-start.18 = (bf16[128,512]{1,0:T(8,128)(2,1)S(1)}, bf16[128,512]{1,0:T(8,128)(2,1)S(1)}, u32[]{:S(2)}, u32[]{:S(2)}) collective-permute-start(bf16[128,512]{1,0:T(8,128)(2,1)S(1)} %get-tuple-element.86), channel_id=1, source_target_pairs={{0,8},{1,9},{2,10},{3,11},{4,12},{5,13},{6,14},{7,15},{8,0},{9,1},... | collective-permute-start | bytes 393224 | tf_op jit(solution)/shard_map/ppermute | solution.py:211
  48.3 10.9 %collective-permute-start.19 = (bf16[128,512]{1,0:T(8,128)(2,1)S(1)}, bf16[128,512]{1,0:T(8,128)(2,1)S(1)}, u32[]{:S(2)}, u32[]{:S(2)}) collective-permute-start(bf16[128,512]{1,0:T(8,128)(2,1)S(1)} %get-tuple-element.87), channel_id=1, source_target_pairs={{0,4},{1,5},{2,6},{3,7},{4,0},{5,1},{6,2},{7,3},{8,12},{9,13},{10,... | collective-permute-start | bytes 393224 | tf_op jit(solution)/shard_map/ppermute | solution.py:211
  48.6 10.5 %collective-permute-start.20 = (bf16[128,512]{1,0:T(8,128)(2,1)S(1)}, bf16[128,512]{1,0:T(8,128)(2,1)S(1)}, u32[]{:S(2)}, u32[]{:S(2)}) collective-permute-start(bf16[128,512]{1,0:T(8,128)(2,1)S(1)} %get-tuple-element.88), channel_id=1, source_target_pairs={{0,12},{1,13},{2,14},{3,15},{4,8},{5,9},{6,10},{7,11},{8,4},{9,5},... | collective-permute-start | bytes 393224 | tf_op jit(solution)/shard_map/ppermute | solution.py:211

commit v8 on v7

--- a/solution.py
+++ b/solution.py
@@ -282,7 +282,8 @@
         [me, queries[0], d_heads[0], beside, kv],
     )
     stats, turned = lax.optimization_barrier((stats, turned))
-    turned = [turned[0], swap(turned[1], 2), swap(turned[2], 3)]
+    diagonal = swap(turned[2], 3)
+    turned = [turned[0], swap(turned[1], 2), diagonal]
     d_across, far, kept = call(
         far_kernel,
         [half, ((pairs, rows, BATCH * rows), bf16), ((pairs, 2, BATCH * rows), f32)],

time: 60.1 us -> 60.1 us (level)
  no operation moved by 1% of the time
where the time goes in v8:
time: 60.1 us; the launch traced here: 59.9 us
  starting transfers between devices  25.2 us (42%)
  waiting for transfers between devices  23.6 us (39%)
  Pallas kernels  7.49 us (12%)
  local copies, waits for them, and re-layouts  1.96 us (3%)
  other arithmetic  0.91 us (2%)
  between operations  0.78 us (1%)
    ppermute x19, starting transfers between devices, swap(): return lax.ppermute(block, 'ctx', [(i, i ^ distance) for i in range(count)])  20.7 us
    ppermute x19, waiting for transfers between devices, swap(): return lax.ppermute(block, 'ctx', [(i, i ^ distance) for i in range(count)])  18.9 us
    pallas_call x8, Pallas kernels, call(): pl.pallas_call(kernel, out_shape=[jax.ShapeDtypeStruct(s, d) for s, d in...  7.49 us
    ppermute x1, waiting for transfers between devices, crossed(): return lax.ppermute(block, 'ctx', route)  2.65 us
    ppermute x1, waiting for transfers between devices, passed(): return lax.ppermute(block, 'ctx', route)  2.11 us
    ppermute x1, starting transfers between devices, crossed(): return lax.ppermute(block, 'ctx', route)  2.08 us
    unnamed x12, local copies, waits for them, and re-layouts  1.96 us
    ppermute x1, starting transfers between devices, shifted(): lax.ppermute(block, axis, [((i - distance) % count, i) for i in range(cou...  1.56 us
  transfers between devices with their start and end apart: 22, of which 11 were waited for; matrix products, arithmetic and copies ran while one was open for 0% of the time, Pallas kernels for 12%

profile of v8, /device:TPU:0, one launch (start us, length us, event | category | flops | bytes accessed | tf_op | source)
XLA Modules:
  0.0 59.9 jit_solution(8349962123917562974)
XLA Ops:
  0.7 3.1 %collective-permute-start = (bf16[128,512]{1,0:T(8,128)(2,1)}, bf16[128,512]{1,0:T(8,128)(2,1)S(1)}, u32[]{:S(2)}, u32[]{:S(2)}) collective-permute-start(bf16[128,512]{1,0:T(8,128)(2,1)} %bitcast.19), channel_id=1, source_target_pairs={{0,4},{1,5},{2,6},{3,7},{4,0},{5,1},{6,2},{7,3},{8,12},{9,13},{10,... | collective-permute-start | bytes 393224 | tf_op jit(solution)/shard_map/ppermute | solution.py:211
  3.7 2.6 %collective-permute-start.2 = (bf16[128,512]{1,0:T(8,128)(2,1)}, bf16[128,512]{1,0:T(8,128)(2,1)S(1)}, u32[]{:S(2)}, u32[]{:S(2)}) collective-permute-start(bf16[128,512]{1,0:T(8,128)(2,1)} %bitcast.20), channel_id=1, source_target_pairs={{0,8},{1,9},{2,10},{3,11},{4,12},{5,13},{6,14},{7,15},{8,0},{9,1},... | collective-permute-start | bytes 393224 | tf_op jit(solution)/shard_map/ppermute | solution.py:211
  6.3 1.5 %collective-permute-start.3 = (bf16[128,512]{1,0:T(8,128)(2,1)}, bf16[128,512]{1,0:T(8,128)(2,1)S(1)}, u32[]{:S(2)}, u32[]{:S(2)}) collective-permute-start(bf16[128,512]{1,0:T(8,128)(2,1)} %bitcast.21), channel_id=1, source_target_pairs={{0,2},{1,3},{2,0},{3,1},{4,6},{5,7},{6,4},{7,5},{8,10},{9,11},{10,... | collective-permute-start | bytes 393224 | tf_op jit(solution)/shard_map/ppermute | solution.py:211
  7.9 1.0 %copy-done.2 = bf16[1,128,2048]{2,1,0:T(8,128)(2,1)S(1)} copy-done((bf16[1,128,2048]{2,1,0:T(8,128)(2,1)S(1)}, bf16[1,128,2048]{2,1,0:T(8,128)(2,1)}, u32[]{:S(2)}) %copy-start.2) | copy-done | bytes 524312
  8.9 0.9 %copy-done.4 = bf16[1,128,512]{2,1,0:T(8,128)(2,1)S(1)} copy-done((bf16[1,128,512]{2,1,0:T(8,128)(2,1)S(1)}, bf16[1,128,512]{2,1,0:T(8,128)(2,1)}, u32[]{:S(2)}) %copy-start.4) | copy-done | bytes 131096
  10.3 0.8 %collective-permute-start.4 = (bf16[128,512]{1,0:T(8,128)(2,1)S(1)}, bf16[128,512]{1,0:T(8,128)(2,1)S(1)}, u32[]{:S(2)}, u32[]{:S(2)}) collective-permute-start(bf16[128,512]{1,0:T(8,128)(2,1)S(1)} %collective-permute-done.refs_2_), channel_id=1, source_target_pairs={{0,2},{1,3},{2,0},{3,1},{4,6},{5,7},{6,4},{7,5},{8,10},{9,11},{10,... | collective-permute-start | bytes 393224 | tf_op jit(solution)/shard_map/ppermute | solution.py:211
  11.1 1.6 %collective-permute-done.2.refs_4_ = bf16[128,512]{1,0:T(8,128)(2,1)S(1)} collective-permute-done((bf16[128,512]{1,0:T(8,128)(2,1)}, bf16[128,512]{1,0:T(8,128)(2,1)S(1)}, u32[]{:S(2)}, u32[]{:S(2)}) %collective-permute-start.2) | collective-permute-done | bytes 131104 | tf_op jit(solution)/shard_map/ppermute | solution.py:211
  12.7 1.5 %collective-permute-start.5 = (bf16[128,512]{1,0:T(8,128)(2,1)S(1)}, bf16[128,512]{1,0:T(8,128)(2,1)S(1)}, u32[]{:S(2)}, u32[]{:S(2)}) collective-permute-start(bf16[128,512]{1,0:T(8,128)(2,1)S(1)} %collective-permute-done.2.refs_4_), channel_id=1, source_target_pairs={{0,2},{1,3},{2,0},{3,1},{4,6},{5,7},{6,4},{7,5},{8,10},{9,11},{10,... | collective-permute-start | bytes 393224 | tf_op jit(solution)/shard_map/ppermute | solution.py:211
  14.6 1.5 %collective-permute-start.7 = (bf16[128,512]{1,0:T(8,128)(2,1)S(1)}, bf16[128,512]{1,0:T(8,128)(2,1)S(1)}, u32[]{:S(2)}, u32[]{:S(2)}) collective-permute-start(bf16[128,512]{1,0:T(8,128)(2,1)S(1)} %collective-permute-done.2.refs_4_), channel_id=1, source_target_pairs={{0,6},{1,7},{2,4},{3,5},{4,2},{5,3},{6,0},{7,1},{8,14},{9,15},{10,... | collective-permute-start | bytes 393224 | tf_op jit(solution)/shard_map/ppermute | solution.py:211
  16.2 1.8 %collective-permute-done.4.refs_3_ = bf16[128,512]{1,0:T(8,128)(2,1)S(1)} collective-permute-done((bf16[128,512]{1,0:T(8,128)(2,1)S(1)}, bf16[128,512]{1,0:T(8,128)(2,1)S(1)}, u32[]{:S(2)}, u32[]{:S(2)}) %collective-permute-start.4) | collective-permute-done | bytes 131104 | tf_op jit(solution)/shard_map/ppermute | solution.py:211
  18.0 3.9 %collective-permute-done.5.refs_5_ = bf16[128,512]{1,0:T(8,128)(2,1)S(1)} collective-permute-done((bf16[128,512]{1,0:T(8,128)(2,1)S(1)}, bf16[128,512]{1,0:T(8,128)(2,1)S(1)}, u32[]{:S(2)}, u32[]{:S(2)}) %collective-permute-start.5) | collective-permute-done | bytes 131104 | tf_op jit(solution)/shard_map/ppermute | solution.py:211
  22.4 1.6 %collective-permute-start.14 = (bf16[1,128,2048]{2,1,0:T(8,128)(2,1)S(1)}, bf16[1,128,2048]{2,1,0:T(8,128)(2,1)S(1)}, u32[]{:S(2)}, u32[]{:S(2)}) collective-permute-start(bf16[1,128,2048]{2,1,0:T(8,128)(2,1)S(1)} %copy-done.5), channel_id=1, source_target_pairs={{16,0},{0,16},{17,1},{1,17},{18,2},{2,18},{19,3},{3,19},{20,4},{4,... | collective-permute-start | bytes 1572872 | tf_op jit(solution)/shard_map/ppermute | solution.py:216
  24.4 0.8 %collective-permute-start.9 = (bf16[128,512]{1,0:T(8,128)(2,1)S(1)}, bf16[128,512]{1,0:T(8,128)(2,1)S(1)}, u32[]{:S(2)}, u32[]{:S(2)}) collective-permute-start(bf16[128,512]{1,0:T(8,128)(2,1)S(1)} %get-tuple-element.100.beside_ref), channel_id=1, source_target_pairs={{0,2},{1,15},{2,4},{3,1},{4,6},{5,3},{6,8},{7,5},{8,10},{9,7},{10,... | collective-permute-start | bytes 393224 | tf_op jit(solution)/shard_map/ppermute | solution.py:228
  25.2 1.0 %shard_map.78 = (f32[2,256,1024]{2,1,0:T(8,128)S(1)}, f32[2,256,1024]{2,1,0:T(8,128)S(1)}, f32[2,3,1024]{2,1,0:T(4,128)S(1)}) custom-call(s32[1]{0:T(128)} %bitcast.me_ref, bf16[128,2048]{1,0:T(8,128)(2,1)S(1)} %bitcast.10, bf16[128,2048]{1,0:T(8,128)(2,1)S(1)} %bitcast.13, bf16[128,512]{1,0:T(8,128)(2,1)S(1)} %get-tuple-element.100.beside_ref, ...), custom_call_target="tpu_custom_call" | custom-call | tf_op jit(solution)/shard_map/pallas_call | solution.py:27
  26.2 1.2 %collective-permute-start.10 = (bf16[4,128,128]{2,1,0:T(8,128)(2,1)S(1)}, bf16[4,128,128]{2,1,0:T(8,128)(2,1)S(1)}, u32[]{:S(2)}, u32[]{:S(2)}) collective-permute-start(bf16[4,128,128]{2,1,0:T(8,128)(2,1)S(1)} %get-tuple-element.76), channel_id=1, source_target_pairs={{0,2},{1,3},{2,0},{3,1},{4,6},{5,7},{6,4},{7,5},{8,10},{9,11},{10,... | collective-permute-start | bytes 393224 | tf_op jit(solution)/shard_map/ppermute | solution.py:211
  27.4 2.7 %collective-permute-start.11 = (bf16[4,128,128]{2,1,0:T(8,128)(2,1)S(1)}, bf16[4,128,128]{2,1,0:T(8,128)(2,1)S(1)}, u32[]{:S(2)}, u32[]{:S(2)}) collective-permute-start(bf16[4,128,128]{2,1,0:T(8,128)(2,1)S(1)} %get-tuple-element.77), channel_id=1, source_target_pairs={{0,3},{1,2},{2,1},{3,0},{4,7},{5,6},{6,5},{7,4},{8,11},{9,10},{10,... | collective-permute-start | bytes 393224 | tf_op jit(solution)/shard_map/ppermute | solution.py:211
  30.1 2.1 %collective-permute-done.9.across_ref = bf16[128,512]{1,0:T(8,128)(2,1)S(1)} collective-permute-done((bf16[128,512]{1,0:T(8,128)(2,1)S(1)}, bf16[128,512]{1,0:T(8,128)(2,1)S(1)}, u32[]{:S(2)}, u32[]{:S(2)}) %collective-permute-start.9) | collective-permute-done | bytes 131104 | tf_op jit(solution)/shard_map/ppermute | solution.py:228
  32.2 1.2 %shard_map.79 = (bf16[128,512]{1,0:T(8,128)(2,1)S(1)}, bf16[2,128,1024]{2,1,0:T(8,128)(2,1)S(1)}, f32[2,2,1024]{2,1,0:T(2,128)S(1)}) custom-call(s32[1]{0:T(128)} %bitcast.me_ref, bf16[128,2048]{1,0:T(8,128)(2,1)S(1)} %bitcast.11, bf16[128,2048]{1,0:T(8,128)(2,1)S(1)} %bitcast.14, bf16[128,512]{1,0:T(8,128)(2,1)S(1)} %collective-permute-done.9.across_ref, ...), custom_call_target="tpu_custom_call" | custom-call | tf_op jit(solution)/shard_map/pallas_call | solution.py:27
  33.4 2.1 %collective-permute-start.13 = (bf16[128,512]{1,0:T(8,128)(2,1)S(1)}, bf16[128,512]{1,0:T(8,128)(2,1)S(1)}, u32[]{:S(2)}, u32[]{:S(2)}) collective-permute-start(bf16[128,512]{1,0:T(8,128)(2,1)S(1)} %get-tuple-element.83), channel_id=1, source_target_pairs={{0,15},{1,2},{2,1},{3,4},{4,3},{5,6},{6,5},{7,8},{8,7},{9,10},{10,... | collective-permute-start | bytes 393224 | tf_op jit(solution)/shard_map/ppermute | solution.py:222
  35.5 1.9 %shard_map.80 = (bf16[128,2048]{1,0:T(8,128)(2,1)}, bf16[128,512]{1,0:T(8,128)(2,1)S(1)}, f32[128,512]{1,0:T(8,128)S(1)}) custom-call(bf16[128,2048]{1,0:T(8,128)(2,1)S(1)} %bitcast.12, bf16[128,2048]{1,0:T(8,128)(2,1)S(1)} %bitcast.15, bf16[128,512]{1,0:T(8,128)(2,1)S(1)} %get-tuple-element.100.beside_ref, bf16[128,512]{1,0:T(8,128)(2,1)S(1)} %get-tuple-element.99.own_ref, ...), custom_call_target="tpu_custom_call" | custom-call | tf_op jit(solution)/shard_map/pallas_call | solution.py:27
  37.4 0.5 collective-permute-done.11.refs_2_
  37.9 2.6 %collective-permute-done.13 = bf16[128,512]{1,0:T(8,128)(2,1)S(1)} collective-permute-done((bf16[128,512]{1,0:T(8,128)(2,1)S(1)}, bf16[128,512]{1,0:T(8,128)(2,1)S(1)}, u32[]{:S(2)}, u32[]{:S(2)}) %collective-permute-start.13) | collective-permute-done | bytes 131104 | tf_op jit(solution)/shard_map/ppermute | solution.py:222
  40.7 4.9 %collective-permute-done.16.refs_5_ = bf16[128,512]{1,0:T(8,128)(2,1)S(1)} collective-permute-done((bf16[128,512]{1,0:T(8,128)(2,1)S(1)}, bf16[128,512]{1,0:T(8,128)(2,1)S(1)}, u32[]{:S(2)}, u32[]{:S(2)}) %collective-permute-start.16) | collective-permute-done | bytes 131104 | tf_op jit(solution)/shard_map/ppermute | solution.py:211
  45.6 0.7 %shard_map.82 = (f32[8,128,128]{2,1,0:T(8,128)S(1)}, bf16[8,128,128]{2,1,0:T(8,128)(2,1)S(1)}) custom-call(bf16[128,512]{1,0:T(8,128)(2,1)S(1)} %add_convert_fusion.refs_3_.own_ref, bf16[128,512]{1,0:T(8,128)(2,1)S(1)} %collective-permute-done.15.refs_4_.beside_ref, bf16[128,512]{1,0:T(8,128)(2,1)S(1)} %get-tuple-element.60.refs_0_, ...), custom_call_target="tpu_custom_call" | custom-call | tf_op jit(solution)/shard_map/pallas_call | solution.py:27
  46.3 0.6 collective-permute-start.21
  47.0 0.5 shard_map.81
  47.4 0.8 %collective-permute-start.18 = (bf16[128,512]{1,0:T(8,128)(2,1)S(1)}, bf16[128,512]{1,0:T(8,128)(2,1)S(1)}, u32[]{:S(2)}, u32[]{:S(2)}) collective-permute-start(bf16[128,512]{1,0:T(8,128)(2,1)S(1)} %get-tuple-element.86), channel_id=1, source_target_pairs={{0,8},{1,9},{2,10},{3,11},{4,12},{5,13},{6,14},{7,15},{8,0},{9,1},... | collective-permute-start | bytes 393224 | tf_op jit(solution)/shard_map/ppermute | solution.py:211
  48.6 3.3 %collective-permute-start.20 = (bf16[128,512]{1,0:T(8,128)(2,1)S(1)}, bf16[128,512]{1,0:T(8,128)(2,1)S(1)}, u32[]{:S(2)}, u32[]{:S(2)}) collective-permute-start(bf16[128,512]{1,0:T(8,128)(2,1)S(1)} %get-tuple-element.88), channel_id=1, source_target_pairs={{0,12},{1,13},{2,14},{3,15},{4,8},{5,9},{6,10},{7,11},{8,4},{9,5},... | collective-permute-start | bytes 393224 | tf_op jit(solution)/shard_map/ppermute | solution.py:211
  51.9 1.4 %shard_map.83 = bf16[128,2048]{1,0:T(8,128)(2,1)} custom-call(s32[1]{0:T(128)} %bitcast.me_ref, bf16[128,2048]{1,0:T(8,128)(2,1)S(1)} %bitcast.17, f32[128,1]{1,0:T(8,128)S(1)} %get-tuple-element.89.factor_ref, bf16[128,2048]{1,0:T(8,128)(2,1)S(1)} %bitcast.18, f32[8,128,128]{2,1,0:T(8,128)S(1)} %get-tuple-element.91.near_ref, ...), custom_call_target="tpu_custom_call" | custom-call | tf_op jit(solution)/shard_map/pallas_call | solution.py:27
  53.3 5.0 %collective-permute-done.18 = bf16[128,512]{1,0:T(8,128)(2,1)S(1)} collective-permute-done((bf16[128,512]{1,0:T(8,128)(2,1)S(1)}, bf16[128,512]{1,0:T(8,128)(2,1)S(1)}, u32[]{:S(2)}, u32[]{:S(2)}) %collective-permute-start.18) | collective-permute-done | bytes 131104 | tf_op jit(solution)/shard_map/ppermute | solution.py:211
  58.3 0.8 %collective-permute-done.19 = bf16[128,512]{1,0:T(8,128)(2,1)S(1)} collective-permute-done((bf16[128,512]{1,0:T(8,128)(2,1)S(1)}, bf16[128,512]{1,0:T(8,128)(2,1)S(1)}, u32[]{:S(2)}, u32[]{:S(2)}) %collective-permute-start.19) | collective-permute-done | bytes 131104 | tf_op jit(solution)/shard_map/ppermute | solution.py:211
  59.2 0.8 %multiply_bitcast_fusion = f32[1,128,512]{2,1,0:T(8,128)} fusion(bf16[128,512]{1,0:T(8,128)(2,1)S(1)} %collective-permute-done.20, bf16[128,512]{1,0:T(8,128)(2,1)S(1)} %collective-permute-done.19, f32[128,512]{1,0:T(8,128)S(1)} %get-tuple-element.95, bf16[128,512]{1,0:T(8,128)(2,1)S(1)} %collective-permute-done.18), kind=kLoop, calls=%fused_computation.4 | loop fusion | flops 458752 | bytes 917504 | tf_op jit(solution)/shard_map/broadcast_in_dim | solution.py:328
  (35 shorter events, 2.5 us)
Async XLA Ops:
  0.6 24.6 %copy-start = (bf16[1,128,2048]{2,1,0:T(8,128)(2,1)S(1)}, bf16[1,128,2048]{2,1,0:T(8,128)(2,1)}, u32[]{:S(2)}) copy-start(bf16[1,128,2048]{2,1,0:T(8,128)(2,1)} %param.7) | copy-start | bytes 1572868
  0.6 24.6 %copy-start.1 = (bf16[1,128,2048]{2,1,0:T(8,128)(2,1)S(1)}, bf16[1,128,2048]{2,1,0:T(8,128)(2,1)}, u32[]{:S(2)}) copy-start(bf16[1,128,2048]{2,1,0:T(8,128)(2,1)} %param.8) | copy-start | bytes 1572868
  0.7 9.6 %collective-permute-start = (bf16[128,512]{1,0:T(8,128)(2,1)}, bf16[128,512]{1,0:T(8,128)(2,1)S(1)}, u32[]{:S(2)}, u32[]{:S(2)}) collective-permute-start(bf16[128,512]{1,0:T(8,128)(2,1)} %bitcast.19), channel_id=1, source_target_pairs={{0,4},{1,5},{2,6},{3,7},{4,0},{5,1},{6,2},{7,3},{8,12},{9,13},{10,... | collective-permute-start | bytes 393224 | tf_op jit(solution)/shard_map/ppermute | solution.py:211
  3.7 8.9 %collective-permute-start.2 = (bf16[128,512]{1,0:T(8,128)(2,1)}, bf16[128,512]{1,0:T(8,128)(2,1)S(1)}, u32[]{:S(2)}, u32[]{:S(2)}) collective-permute-start(bf16[128,512]{1,0:T(8,128)(2,1)} %bitcast.20), channel_id=1, source_target_pairs={{0,8},{1,9},{2,10},{3,11},{4,12},{5,13},{6,14},{7,15},{8,0},{9,1},... | collective-permute-start | bytes 393224 | tf_op jit(solution)/shard_map/ppermute | solution.py:211
  6.3 6.4 %collective-permute-start.3 = (bf16[128,512]{1,0:T(8,128)(2,1)}, bf16[128,512]{1,0:T(8,128)(2,1)S(1)}, u32[]{:S(2)}, u32[]{:S(2)}) collective-permute-start(bf16[128,512]{1,0:T(8,128)(2,1)} %bitcast.21), channel_id=1, source_target_pairs={{0,2},{1,3},{2,0},{3,1},{4,6},{5,7},{6,4},{7,5},{8,10},{9,11},{10,... | collective-permute-start | bytes 393224 | tf_op jit(solution)/shard_map/ppermute | solution.py:211
  7.8 1.0 %copy-start.2 = (bf16[1,128,2048]{2,1,0:T(8,128)(2,1)S(1)}, bf16[1,128,2048]{2,1,0:T(8,128)(2,1)}, u32[]{:S(2)}) copy-start(bf16[1,128,2048]{2,1,0:T(8,128)(2,1)} %param.5) | copy-start | bytes 1572868
  8.9 0.9 %copy-start.4 = (bf16[1,128,512]{2,1,0:T(8,128)(2,1)S(1)}, bf16[1,128,512]{2,1,0:T(8,128)(2,1)}, u32[]{:S(2)}) copy-start(bf16[1,128,512]{2,1,0:T(8,128)(2,1)} %param.9) | copy-start | bytes 393220
  9.8 12.6 %copy-start.5 = (bf16[1,128,2048]{2,1,0:T(8,128)(2,1)S(1)}, bf16[1,128,2048]{2,1,0:T(8,128)(2,1)}, u32[]{:S(2)}) copy-start(bf16[1,128,2048]{2,1,0:T(8,128)(2,1)} %param.6) | copy-start | bytes 1572868
  10.2 11.6 %collective-permute-start.1 = (bf16[2,4,128,128]{3,2,1,0:T(8,128)(2,1)S(1)}, bf16[2,4,128,128]{3,2,1,0:T(8,128)(2,1)S(1)}, u32[]{:S(2)}, u32[]{:S(2)}) collective-permute-start(bf16[2,4,128,128]{3,2,1,0:T(8,128)(2,1)S(1)} %get-tuple-element.58), channel_id=1, source_target_pairs={{0,1},{1,0},{2,3},{3,2},{4,5},{5,4},{6,7},{7,6},{8,9},{9,8},{10,11... | collective-permute-start | bytes 786440 | tf_op jit(solution)/shard_map/ppermute | solution.py:211
  10.3 7.7 %collective-permute-start.4 = (bf16[128,512]{1,0:T(8,128)(2,1)S(1)}, bf16[128,512]{1,0:T(8,128)(2,1)S(1)}, u32[]{:S(2)}, u32[]{:S(2)}) collective-permute-start(bf16[128,512]{1,0:T(8,128)(2,1)S(1)} %collective-permute-done.refs_2_), channel_id=1, source_target_pairs={{0,2},{1,3},{2,0},{3,1},{4,6},{5,7},{6,4},{7,5},{8,10},{9,11},{10,... | collective-permute-start | bytes 393224 | tf_op jit(solution)/shard_map/ppermute | solution.py:211
  12.7 9.2 %collective-permute-start.5 = (bf16[128,512]{1,0:T(8,128)(2,1)S(1)}, bf16[128,512]{1,0:T(8,128)(2,1)S(1)}, u32[]{:S(2)}, u32[]{:S(2)}) collective-permute-start(bf16[128,512]{1,0:T(8,128)(2,1)S(1)} %collective-permute-done.2.refs_4_), channel_id=1, source_target_pairs={{0,2},{1,3},{2,0},{3,1},{4,6},{5,7},{6,4},{7,5},{8,10},{9,11},{10,... | collective-permute-start | bytes 393224 | tf_op jit(solution)/shard_map/ppermute | solution.py:211
  14.2 7.6 %collective-permute-start.6 = (bf16[128,512]{1,0:T(8,128)(2,1)S(1)}, bf16[128,512]{1,0:T(8,128)(2,1)S(1)}, u32[]{:S(2)}, u32[]{:S(2)}) collective-permute-start(bf16[128,512]{1,0:T(8,128)(2,1)S(1)} %collective-permute-done.2.refs_4_), channel_id=1, source_target_pairs={{0,4},{1,5},{2,6},{3,7},{4,0},{5,1},{6,2},{7,3},{8,12},{9,13},{10,... | collective-permute-start | bytes 393224 | tf_op jit(solution)/shard_map/ppermute | solution.py:211
  14.6 7.2 %collective-permute-start.7 = (bf16[128,512]{1,0:T(8,128)(2,1)S(1)}, bf16[128,512]{1,0:T(8,128)(2,1)S(1)}, u32[]{:S(2)}, u32[]{:S(2)}) collective-permute-start(bf16[128,512]{1,0:T(8,128)(2,1)S(1)} %collective-permute-done.2.refs_4_), channel_id=1, source_target_pairs={{0,6},{1,7},{2,4},{3,5},{4,2},{5,3},{6,0},{7,1},{8,14},{9,15},{10,... | collective-permute-start | bytes 393224 | tf_op jit(solution)/shard_map/ppermute | solution.py:211
  22.3 2.0 %collective-permute-start.8 = (f32[256,512]{1,0:T(8,128)S(1)}, f32[256,512]{1,0:T(8,128)S(1)}, u32[]{:S(2)}, u32[]{:S(2)}) collective-permute-start(f32[256,512]{1,0:T(8,128)S(1)} %shard_map.77), channel_id=1, source_target_pairs={{0,1},{1,0},{2,3},{3,2},{4,5},{5,4},{6,7},{7,6},{8,9},{9,8},{10,11... | collective-permute-start | bytes 1572872 | tf_op jit(solution)/shard_map/ppermute | solution.py:211
  22.4 15.5 %collective-permute-start.14 = (bf16[1,128,2048]{2,1,0:T(8,128)(2,1)S(1)}, bf16[1,128,2048]{2,1,0:T(8,128)(2,1)S(1)}, u32[]{:S(2)}, u32[]{:S(2)}) collective-permute-start(bf16[1,128,2048]{2,1,0:T(8,128)(2,1)S(1)} %copy-done.5), channel_id=1, source_target_pairs={{16,0},{0,16},{17,1},{1,17},{18,2},{2,18},{19,3},{3,19},{20,4},{4,... | collective-permute-start | bytes 1572872 | tf_op jit(solution)/shard_map/ppermute | solution.py:216
  24.4 7.8 %collective-permute-start.9 = (bf16[128,512]{1,0:T(8,128)(2,1)S(1)}, bf16[128,512]{1,0:T(8,128)(2,1)S(1)}, u32[]{:S(2)}, u32[]{:S(2)}) collective-permute-start(bf16[128,512]{1,0:T(8,128)(2,1)S(1)} %get-tuple-element.100.beside_ref), channel_id=1, source_target_pairs={{0,2},{1,15},{2,4},{3,1},{4,6},{5,3},{6,8},{7,5},{8,10},{9,7},{10,... | collective-permute-start | bytes 393224 | tf_op jit(solution)/shard_map/ppermute | solution.py:228
  26.2 11.2 %collective-permute-start.10 = (bf16[4,128,128]{2,1,0:T(8,128)(2,1)S(1)}, bf16[4,128,128]{2,1,0:T(8,128)(2,1)S(1)}, u32[]{:S(2)}, u32[]{:S(2)}) collective-permute-start(bf16[4,128,128]{2,1,0:T(8,128)(2,1)S(1)} %get-tuple-element.76), channel_id=1, source_target_pairs={{0,2},{1,3},{2,0},{3,1},{4,6},{5,7},{6,4},{7,5},{8,10},{9,11},{10,... | collective-permute-start | bytes 393224 | tf_op jit(solution)/shard_map/ppermute | solution.py:211
  27.4 10.5 %collective-permute-start.11 = (bf16[4,128,128]{2,1,0:T(8,128)(2,1)S(1)}, bf16[4,128,128]{2,1,0:T(8,128)(2,1)S(1)}, u32[]{:S(2)}, u32[]{:S(2)}) collective-permute-start(bf16[4,128,128]{2,1,0:T(8,128)(2,1)S(1)} %get-tuple-element.77), channel_id=1, source_target_pairs={{0,3},{1,2},{2,1},{3,0},{4,7},{5,6},{6,5},{7,4},{8,11},{9,10},{10,... | collective-permute-start | bytes 393224 | tf_op jit(solution)/shard_map/ppermute | solution.py:211
  33.4 7.2 %collective-permute-start.13 = (bf16[128,512]{1,0:T(8,128)(2,1)S(1)}, bf16[128,512]{1,0:T(8,128)(2,1)S(1)}, u32[]{:S(2)}, u32[]{:S(2)}) collective-permute-start(bf16[128,512]{1,0:T(8,128)(2,1)S(1)} %get-tuple-element.83), channel_id=1, source_target_pairs={{0,15},{1,2},{2,1},{3,4},{4,3},{5,6},{6,5},{7,8},{8,7},{9,10},{10,... | collective-permute-start | bytes 393224 | tf_op jit(solution)/shard_map/ppermute | solution.py:222
  37.4 14.5 %copy-start.3 = (bf16[1,128,2048]{2,1,0:T(8,128)(2,1)S(1)}, bf16[1,128,2048]{2,1,0:T(8,128)(2,1)}, u32[]{:S(2)}) copy-start(bf16[1,128,2048]{2,1,0:T(8,128)(2,1)} %param.5) | copy-start | bytes 1572868
  37.9 2.7 %collective-permute-start.12 = (bf16[128,512]{1,0:T(8,128)(2,1)S(1)}, bf16[128,512]{1,0:T(8,128)(2,1)S(1)}, u32[]{:S(2)}, u32[]{:S(2)}) collective-permute-start(bf16[128,512]{1,0:T(8,128)(2,1)S(1)} %get-tuple-element.82), channel_id=1, source_target_pairs={{0,1},{1,0},{2,3},{3,2},{4,5},{5,4},{6,7},{7,6},{8,9},{9,8},{10,11... | collective-permute-start | bytes 393224 | tf_op jit(solution)/shard_map/ppermute | solution.py:211
  40.6 5.0 %collective-permute-start.16 = (bf16[128,512]{1,0:T(8,128)(2,1)S(1)}, bf16[128,512]{1,0:T(8,128)(2,1)S(1)}, u32[]{:S(2)}, u32[]{:S(2)}) collective-permute-start(bf16[128,512]{1,0:T(8,128)(2,1)S(1)} %add_convert_fusion.refs_3_.own_ref), channel_id=1, source_target_pairs={{0,2},{1,3},{2,0},{3,1},{4,6},{5,7},{6,4},{7,5},{8,10},{9,11},{10,... | collective-permute-start | bytes 393224 | tf_op jit(solution)/shard_map/ppermute | solution.py:211
  40.7 5.0 %collective-permute-start.15 = (bf16[128,512]{1,0:T(8,128)(2,1)S(1)}, bf16[128,512]{1,0:T(8,128)(2,1)S(1)}, u32[]{:S(2)}, u32[]{:S(2)}) collective-permute-start(bf16[128,512]{1,0:T(8,128)(2,1)S(1)} %add_convert_fusion.refs_3_.own_ref), channel_id=1, source_target_pairs={{0,1},{1,0},{2,3},{3,2},{4,5},{5,4},{6,7},{7,6},{8,9},{9,8},{10,11... | collective-permute-start | bytes 393224 | tf_op jit(solution)/shard_map/ppermute | solution.py:211
  45.6 1.3 %collective-permute-start.17 = (bf16[128,512]{1,0:T(8,128)(2,1)S(1)}, bf16[128,512]{1,0:T(8,128)(2,1)S(1)}, u32[]{:S(2)}, u32[]{:S(2)}) collective-permute-start(bf16[128,512]{1,0:T(8,128)(2,1)S(1)} %collective-permute-done.16.refs_5_), channel_id=1, source_target_pairs={{0,1},{1,0},{2,3},{3,2},{4,5},{5,4},{6,7},{7,6},{8,9},{9,8},{10,11... | collective-permute-start | bytes 393224 | tf_op jit(solution)/shard_map/ppermute | solution.py:211
  46.3 5.6 %collective-permute-start.21 = (bf16[8,128,128]{2,1,0:T(8,128)(2,1)S(1)}, bf16[8,128,128]{2,1,0:T(8,128)(2,1)S(1)}, u32[]{:S(2)}, u32[]{:S(2)}) collective-permute-start(bf16[8,128,128]{2,1,0:T(8,128)(2,1)S(1)} %get-tuple-element.92), channel_id=1, source_target_pairs={{0,1},{1,0},{2,3},{3,2},{4,5},{5,4},{6,7},{7,6},{8,9},{9,8},{10,11... | collective-permute-start | bytes 786440 | tf_op jit(solution)/shard_map/ppermute | solution.py:211
  47.4 10.9 %collective-permute-start.18 = (bf16[128,512]{1,0:T(8,128)(2,1)S(1)}, bf16[128,512]{1,0:T(8,128)(2,1)S(1)}, u32[]{:S(2)}, u32[]{:S(2)}) collective-permute-start(bf16[128,512]{1,0:T(8,128)(2,1)S(1)} %get-tuple-element.86), channel_id=1, source_target_pairs={{0,8},{1,9},{2,10},{3,11},{4,12},{5,13},{6,14},{7,15},{8,0},{9,1},... | collective-permute-start | bytes 393224 | tf_op jit(solution)/shard_map/ppermute | solution.py:211
  48.3 10.9 %collective-permute-start.19 = (bf16[128,512]{1,0:T(8,128)(2,1)S(1)}, bf16[128,512]{1,0:T(8,128)(2,1)S(1)}, u32[]{:S(2)}, u32[]{:S(2)}) collective-permute-start(bf16[128,512]{1,0:T(8,128)(2,1)S(1)} %get-tuple-element.87), channel_id=1, source_target_pairs={{0,4},{1,5},{2,6},{3,7},{4,0},{5,1},{6,2},{7,3},{8,12},{9,13},{10,... | collective-permute-start | bytes 393224 | tf_op jit(solution)/shard_map/ppermute | solution.py:211
  48.6 10.5 %collective-permute-start.20 = (bf16[128,512]{1,0:T(8,128)(2,1)S(1)}, bf16[128,512]{1,0:T(8,128)(2,1)S(1)}, u32[]{:S(2)}, u32[]{:S(2)}) collective-permute-start(bf16[128,512]{1,0:T(8,128)(2,1)S(1)} %get-tuple-element.88), channel_id=1, source_target_pairs={{0,12},{1,13},{2,14},{3,15},{4,8},{5,9},{6,10},{7,11},{8,4},{9,5},... | collective-permute-start | bytes 393224 | tf_op jit(solution)/shard_map/ppermute | solution.py:211
